TPU v7x, 768 devices: a whole 4x8x12 slice. The times are simulated.
768 devices in a mesh: lon: 48 (over z_lo, x, core), lat: 16 (over z_hi, y).
Axes of the slice: x: 4, y: 8, z: 12 (z_hi: 2, z_lo: 6; z = z_hi * 6 + z_lo), core: 2. Of those that a mesh axis runs over, the one named last changes fastest.
Arguments:
- tokens: bfloat16 [768, 512, 128], P('lon', 'lat'), may hold values from -24 to 24
- grad_out: bfloat16 [768, 512, 128], P('lon', 'lat'), may hold values from -6 to 6
- window_ids: int32 [768, 512], P('lon', 'lat'), may hold values from 0 to 2
- qkv_weight: bfloat16 [128, 384], replicated, may hold values from -0.5 to 0.5
- proj_weight: bfloat16 [128, 128], replicated, may hold values from -0.5 to 0.5
- up_weight: bfloat16 [128, 512], replicated, may hold values from -0.5 to 0.5
- down_weight: bfloat16 [512, 128], replicated, may hold values from -0.25 to 0.25
- conv_weight: bfloat16 [9, 128, 128], replicated, may hold values from -0.1875 to 0.1875
- gain_one: float32 [128], replicated, may hold values from 0.1 to 1.9
- gain_two: float32 [128], replicated, may hold values from 0.1 to 1.9
- position_bias: float32 [4, 15, 15], replicated, may hold values from -6 to 330
Outputs:
- downscaled: bfloat16 [768, 512, 128], P('lon', 'lat')
- grad_tokens: bfloat16 [768, 512, 128], P('lon', 'lat')
- grad_qkv: float32 [128, 384], replicated
- grad_proj: float32 [128, 128], replicated
- grad_up: float32 [128, 512], replicated
- grad_down: float32 [512, 128], replicated
- grad_conv: float32 [9, 128, 128], replicated
- grad_gain_one: float32 [128], replicated
- grad_gain_two: float32 [128], replicated
- grad_bias: float32 [4, 15, 15], replicated
All inputs are finite; a program needn't handle non-finite values.
Results may differ from a plain program's by a relative error of at most 0.018.
Values may be sent and summed in bfloat16 or wider, within the bound.
No kernel may reach another device: no remote copies, remote signals or barrier semaphores. Data moves between devices by JAX's collectives and lax.ppermute only.
A program may use at most 32 MiB of HBM per device.

v0:
```python
import math

import jax
import jax.numpy as jnp
from jax import lax
from jax.sharding import PartitionSpec as P

HEADS = 4
WIN = 8
SHIFT = 4
SPAN = 15
HEAD_DIM = 32


epsilon = 1e-05


def passed_along(value, axis, steps):
    count = lax.axis_size(axis)
    pairs = [(source, (source + steps) % count) for source in range(count)]
    return lax.ppermute(value, axis, pairs)


def extended(block, sides, width):
    for axis, dim in sides:
        count = lax.axis_size(axis)
        forward = [(i, i + 1) for i in range(count - 1)]
        forward.append((count - 1, 0))
        backward = [(target, source) for source, target in forward]
        low = lax.ppermute(
            lax.slice_in_dim(block, block.shape[dim] - width, None, axis=dim), axis, forward
        )
        high = lax.ppermute(lax.slice_in_dim(block, 0, width, axis=dim), axis, backward)
        block = jnp.concatenate([low, block, high], axis=dim)
    return block


def layer_norm(values, gain_vec):
    average = jnp.mean(values, axis=-1, keepdims=True)
    centred = values - average
    variance = jnp.mean(centred * centred, axis=-1, keepdims=True)
    inverse = lax.rsqrt(variance + epsilon)
    normed = centred * inverse
    return ((normed * gain_vec).astype(jnp.bfloat16), normed, inverse)


def layer_norm_back(grad_in, normed, inverse, gain_vec):
    scaled = grad_in * gain_vec
    first_mean = jnp.mean(scaled, axis=-1, keepdims=True)
    second = jnp.mean(scaled * normed, axis=-1, keepdims=True)
    return inverse * (scaled - first_mean - normed * second)


def gelu_slope(pre_act):
    cumulative = 0.5 * (1.0 + jax.scipy.special.erf(pre_act * 0.7071067811865476))
    density = jnp.exp(-0.5 * pre_act * pre_act) * 0.3989422804014327
    return cumulative + pre_act * density


def offsets_onehot():
    places = jnp.arange(WIN, dtype=jnp.int32)
    distance = places[:, None] - places[None, :] + WIN - 1
    return (distance[:, :, None] == jnp.arange(SPAN, dtype=jnp.int32)[None, None, :]).astype(
        jnp.float32
    )


def bias_matrix(position_bias):
    onehot = offsets_onehot()
    spread = jnp.einsum(
        "hmn,acm,bdn->habcd", position_bias, onehot, onehot, precision=lax.Precision.HIGHEST
    )
    return spread.reshape(HEADS, WIN * WIN, WIN * WIN)


def to_windows(values_grid):
    row_count, col_count = (values_grid.shape[0], values_grid.shape[1])
    trailing = values_grid.shape[2:]
    reshaped = values_grid.reshape((row_count // WIN, WIN, col_count // WIN, WIN) + trailing)
    permute = (0, 2, 1, 3) + tuple(range(4, 4 + len(trailing)))
    return reshaped.transpose(permute).reshape(
        (row_count // WIN * (col_count // WIN), WIN * WIN) + trailing
    )


def from_windows(blocks, row_count, col_count):
    trailing = blocks.shape[2:]
    reshaped = blocks.reshape((row_count // WIN, col_count // WIN, WIN, WIN) + trailing)
    permute = (0, 2, 1, 3) + tuple(range(4, 4 + len(trailing)))
    return reshaped.transpose(permute).reshape((row_count, col_count) + trailing)


def attend(windows, labels_win, qkv_weight, biases):
    window_count, length, width = windows.shape
    qkv_all = jnp.dot(windows, qkv_weight, preferred_element_type=jnp.float32).astype(jnp.bfloat16)
    split_heads = qkv_all.reshape(window_count, length, 3, HEADS, HEAD_DIM)
    query_heads, key_heads, value_heads = (
        split_heads[:, :, 0],
        split_heads[:, :, 1],
        split_heads[:, :, 2],
    )
    score_scale = HEAD_DIM ** (-0.5)
    scores = (
        jnp.einsum("nihe,njhe->nhij", query_heads, key_heads, preferred_element_type=jnp.float32)
        * score_scale
        + biases[None]
    )
    allowed = labels_win[:, None, :, None] == labels_win[:, None, None, :]
    scores = jnp.where(allowed, scores, -jnp.inf)
    probabilities = jax.nn.softmax(scores, axis=-1)
    weights = probabilities.astype(jnp.bfloat16)
    mixed_win = jnp.einsum(
        "nhij,njhe->nihe", weights, value_heads, preferred_element_type=jnp.float32
    ).astype(jnp.bfloat16)
    return (mixed_win.reshape(window_count, length, width), qkv_all, probabilities, weights)


def attend_back(grad_mixed, qkv_all, probabilities, weights):
    window_count, length, width = grad_mixed.shape
    split_heads = qkv_all.reshape(window_count, length, 3, HEADS, HEAD_DIM)
    query_heads, key_heads, value_heads = (
        split_heads[:, :, 0],
        split_heads[:, :, 1],
        split_heads[:, :, 2],
    )
    grad_heads = grad_mixed.reshape(window_count, length, HEADS, HEAD_DIM)
    grad_probs = jnp.einsum(
        "nihe,njhe->nhij", grad_heads, value_heads, preferred_element_type=jnp.float32
    )
    grad_value = jnp.einsum(
        "nhij,nihe->njhe", weights, grad_heads, preferred_element_type=jnp.float32
    )
    grad_scores = probabilities * (
        grad_probs - jnp.sum(probabilities * grad_probs, axis=-1, keepdims=True)
    )
    bias_part = jnp.sum(grad_scores, axis=0)
    grad_scores_b = grad_scores.astype(jnp.bfloat16)
    score_scale = HEAD_DIM ** (-0.5)
    grad_query = (
        jnp.einsum("nhij,njhe->nihe", grad_scores_b, key_heads, preferred_element_type=jnp.float32)
        * score_scale
    )
    grad_key = (
        jnp.einsum(
            "nhij,nihe->njhe", grad_scores_b, query_heads, preferred_element_type=jnp.float32
        )
        * score_scale
    )
    stacked = jnp.stack([grad_query, grad_key, grad_value], axis=2)
    return (stacked.reshape(window_count, length, 3 * width).astype(jnp.bfloat16), bias_part)


def forward_shift(values_grid):
    lon_rim = passed_along(values_grid[..., :SHIFT, :, :], "lon", -1)
    values_grid = jnp.concatenate([values_grid[..., SHIFT:, :, :], lon_rim], axis=-3)
    lat_rim = passed_along(values_grid[..., :, :SHIFT, :], "lat", -1)
    return jnp.concatenate([values_grid[..., :, SHIFT:, :], lat_rim], axis=-2)


def back_shift(values_grid):
    lat_rim = passed_along(values_grid[..., :, -SHIFT:, :], "lat", 1)
    values_grid = jnp.concatenate([lat_rim, values_grid[..., :, :-SHIFT, :]], axis=-2)
    lon_rim = passed_along(values_grid[..., -SHIFT:, :, :], "lon", 1)
    return jnp.concatenate([lon_rim, values_grid[..., :-SHIFT, :, :]], axis=-3)


def pad_rim(values_grid):
    return extended(values_grid, (("lon", 0), ("lat", 1)), 1)


def seam_masks(col_count, lat_total):
    positions = lax.axis_index("lat") * col_count - 1 + jnp.arange(col_count + 2, dtype=jnp.int32)
    positions = jnp.remainder(positions, lat_total)
    before = positions != lat_total - SHIFT
    after = positions != lat_total - SHIFT - 1
    return jnp.stack([before, jnp.ones_like(before), after]).astype(jnp.bfloat16)


def conv_forward(padded, conv_weight, keep_pad):
    row_count = padded.shape[0] - 2
    col_count = padded.shape[1] - 2
    summed = jnp.zeros((row_count, col_count, conv_weight.shape[2]), jnp.float32)
    for tap_row in range(3):
        for tap_col in range(3):
            window_part = padded[tap_row : tap_row + row_count, tap_col : tap_col + col_count]
            product = jnp.dot(
                window_part, conv_weight[3 * tap_row + tap_col], preferred_element_type=jnp.float32
            )
            summed = summed + product * keep_pad[tap_col, 1:-1][None, :, None]
    return summed


def conv_weight_sum(padded, grad_field, keep_pad):
    row_count = padded.shape[0] - 2
    col_count = padded.shape[1] - 2
    pieces = []
    for tap_row in range(3):
        for tap_col in range(3):
            window_part = padded[tap_row : tap_row + row_count, tap_col : tap_col + col_count]
            masked = grad_field * keep_pad[tap_col, 1:-1][None, :, None]
            pieces.append(
                jnp.einsum("lwc,lwd->cd", window_part, masked, preferred_element_type=jnp.float32)
            )
    return jnp.stack(pieces)


def conv_input_grad(grad_padded, conv_weight, keep_pad):
    row_count = grad_padded.shape[0] - 2
    col_count = grad_padded.shape[1] - 2
    summed = jnp.zeros((row_count, col_count, conv_weight.shape[1]), jnp.float32)
    for tap_row in range(3):
        for tap_col in range(3):
            start_row = 2 - tap_row
            start_col = 2 - tap_col
            window_part = grad_padded[
                start_row : start_row + row_count, start_col : start_col + col_count
            ]
            window_part = (
                window_part * keep_pad[tap_col, start_col : start_col + col_count][None, :, None]
            )
            summed = summed + jnp.einsum(
                "lwd,cd->lwc",
                window_part,
                conv_weight[3 * tap_row + tap_col],
                preferred_element_type=jnp.float32,
            )
    return summed


def per_device(
    tokens,
    grad_out,
    window_ids,
    qkv_weight,
    proj_weight,
    up_weight,
    down_weight,
    conv_weight,
    gain_one,
    gain_two,
    position_bias,
):
    row_count, col_count, width = tokens.shape
    lon_count = lax.axis_size("lon")
    lat_total = col_count * lax.axis_size("lat")
    tokens_all = row_count * col_count * lon_count * lax.axis_size("lat")
    moved_in = forward_shift(jnp.stack([tokens, grad_out]))
    source = moved_in[0].astype(jnp.float32)
    grad_shifted_out = moved_in[1]
    columns = lax.axis_index("lat") * col_count + jnp.arange(col_count, dtype=jnp.int32)
    seam_flag = (columns >= lat_total - SHIFT).astype(jnp.int32)
    labels = window_ids * 2 + seam_flag[None, :]
    biases = bias_matrix(position_bias)
    ln_one, normed_one, inverse_one = layer_norm(source, gain_one)
    mixed_win, qkv_all, probabilities, weights = attend(
        to_windows(ln_one), to_windows(labels), qkv_weight, biases
    )
    mixed_grid = from_windows(mixed_win, row_count, col_count)
    projected = jnp.dot(mixed_grid, proj_weight, preferred_element_type=jnp.float32).astype(
        jnp.bfloat16
    )
    middle = source + projected.astype(jnp.float32)
    ln_two, normed_two, inverse_two = layer_norm(middle, gain_two)
    pre_act = jnp.dot(ln_two, up_weight, preferred_element_type=jnp.float32)
    hidden = jax.nn.gelu(pre_act, approximate=False).astype(jnp.bfloat16)
    block_out = (middle + jnp.dot(hidden, down_weight, preferred_element_type=jnp.float32)).astype(
        jnp.bfloat16
    )
    keep_pad = seam_masks(col_count, lat_total)
    padded = pad_rim(block_out)
    downscaled = conv_forward(padded, conv_weight, keep_pad).astype(jnp.bfloat16)
    conv_sum = conv_weight_sum(padded, grad_shifted_out, keep_pad)
    grad_block = conv_input_grad(pad_rim(grad_shifted_out), conv_weight, keep_pad)
    grad_block_b = grad_block.astype(jnp.bfloat16)
    down_sum = jnp.einsum("lwf,lwc->fc", hidden, grad_block_b, preferred_element_type=jnp.float32)
    grad_hidden = jnp.einsum(
        "lwc,fc->lwf", grad_block_b, down_weight, preferred_element_type=jnp.float32
    )
    grad_pre = (grad_hidden * gelu_slope(pre_act)).astype(jnp.bfloat16)
    up_sum = jnp.einsum("lwc,lwf->cf", ln_two, grad_pre, preferred_element_type=jnp.float32)
    grad_ln_two = jnp.einsum("lwf,cf->lwc", grad_pre, up_weight, preferred_element_type=jnp.float32)
    gain_two_sum = jnp.sum(grad_ln_two * normed_two, axis=(0, 1))
    grad_middle = grad_block + layer_norm_back(grad_ln_two, normed_two, inverse_two, gain_two)
    grad_att = grad_middle.astype(jnp.bfloat16)
    proj_sum = jnp.einsum("lwc,lwd->cd", mixed_grid, grad_att, preferred_element_type=jnp.float32)
    grad_mixed = jnp.einsum(
        "lwd,cd->lwc", grad_att, proj_weight, preferred_element_type=jnp.float32
    ).astype(jnp.bfloat16)
    grad_qkv_win, bias_sum = attend_back(to_windows(grad_mixed), qkv_all, probabilities, weights)
    grad_qkv_all = from_windows(grad_qkv_win, row_count, col_count)
    qkv_sum = jnp.einsum("lwc,lwk->ck", ln_one, grad_qkv_all, preferred_element_type=jnp.float32)
    grad_ln_one = jnp.einsum(
        "lwk,ck->lwc", grad_qkv_all, qkv_weight, preferred_element_type=jnp.float32
    )
    gain_one_sum = jnp.sum(grad_ln_one * normed_one, axis=(0, 1))
    grad_tokens = (
        grad_middle + layer_norm_back(grad_ln_one, normed_one, inverse_one, gain_one)
    ).astype(jnp.bfloat16)
    onehot = offsets_onehot()
    table_sum = jnp.einsum(
        "habcd,acm,bdn->hmn",
        bias_sum.reshape(HEADS, WIN, WIN, WIN, WIN),
        onehot,
        onehot,
        precision=lax.Precision.HIGHEST,
    )
    partials = [
        qkv_sum,
        proj_sum,
        up_sum,
        down_sum,
        conv_sum,
        gain_one_sum,
        gain_two_sum,
        table_sum,
    ]
    flat_grads = jnp.concatenate([piece_part.reshape(-1) for piece_part in partials])
    totals = lax.psum(flat_grads, ("lon", "lat"))
    grad_scale = 1.0 / math.sqrt(tokens_all)
    results = []
    offset = 0
    for piece_part in partials:
        length = math.prod(piece_part.shape)
        results.append(totals[offset : offset + length].reshape(piece_part.shape) * grad_scale)
        offset = offset + length
    moved_out = back_shift(jnp.stack([downscaled, grad_tokens]))
    return (
        moved_out[0],
        moved_out[1],
        results[0],
        results[1],
        results[2],
        results[3],
        results[4],
        results[5],
        results[6],
        results[7],
    )


def solution(mesh):
    return jax.shard_map(
        per_device,
        mesh=mesh,
        in_specs=(
            P("lon", "lat", None),
            P("lon", "lat", None),
            P("lon", "lat"),
            P(),
            P(),
            P(),
            P(),
            P(),
            P(),
            P(),
            P(),
        ),
        out_specs=(
            P("lon", "lat", None),
            P("lon", "lat", None),
            P(),
            P(),
            P(),
            P(),
            P(),
            P(),
            P(),
            P(),
        ),
        check_vma=False,
    )
```

profile of v0, /device:TPU:1, one launch (start us, length us, event | category | flops | bytes accessed | tf_op | source)
XLA Modules:
  0.0 620.5 jit_solution(17798014019079919352)
XLA Ops:
  8.1 12.4 %collective-permute-start = (bf16[2,4,32,128]{3,2,1,0:T(8,128)(2,1)S(1)}, bf16[2,4,32,128]{3,2,1,0:T(8,128)(2,1)S(1)}, u32[]{:S(2)}, u32[]{:S(2)}) collective-permute-start(bf16[2,4,32,128]{3,2,1,0:T(8,128)(2,1)S(1)} %pad_maximum_fusion.14), channel_id=1, source_target_pairs={{0,752},{16,0},{32,16},{48,32},{64,48},{80,64},{96,80},{112,96},{1... | collective-permute-start | bytes 196616 | tf_op jit(solution)/shard_map/ppermute | solution.py:21
  22.3 1.0 convolution_bitcast_fusion.6
  25.0 8.8 %collective-permute-start.1 = (bf16[2,16,4,128]{3,2,1,0:T(4,128)(2,1)S(1)}, bf16[2,16,4,128]{3,2,1,0:T(4,128)(2,1)S(1)}, u32[]{:S(2)}, u32[]{:S(2)}) collective-permute-start(bf16[2,16,4,128]{3,2,1,0:T(4,128)(2,1)S(1)} %pad_maximum_fusion.16), channel_id=1, source_target_pairs={{0,15},{1,0},{2,1},{3,2},{4,3},{5,4},{6,5},{7,6},{8,7},{9,8},{10,9... | collective-permute-start | bytes 98312 | tf_op jit(solution)/shard_map/ppermute | solution.py:21
  33.8 1.3 collective-permute-done.1
  35.1 3.5 collective-permute-start.6
  38.6 8.2 %collective-permute-start.7 = (bf16[1,32,128]{2,1,0:T(8,128)(2,1)S(1)}, bf16[1,32,128]{2,1,0:T(8,128)(2,1)S(1)}, u32[]{:S(2)}, u32[]{:S(2)}) collective-permute-start(bf16[1,32,128]{2,1,0:T(8,128)(2,1)S(1)} %get-tuple-element.67), channel_id=1, source_target_pairs={{16,0},{32,16},{48,32},{64,48},{80,64},{96,80},{112,96},{128,112},... | collective-permute-start | bytes 24584 | tf_op jit(solution)/shard_map/ppermute | solution.py:33
  48.9 1.0 copy-done.7
  52.1 2.4 fusion.39
  54.9 1.9 collective-permute-start.2
  56.8 10.6 %collective-permute-start.3 = (bf16[1,32,128]{2,1,0:T(8,128)(2,1)S(1)}, bf16[1,32,128]{2,1,0:T(8,128)(2,1)S(1)}, u32[]{:S(2)}, u32[]{:S(2)}) collective-permute-start(bf16[1,32,128]{2,1,0:T(8,128)(2,1)S(1)} %get-tuple-element.79), channel_id=1, source_target_pairs={{16,0},{32,16},{48,32},{64,48},{80,64},{96,80},{112,96},{128,112},... | collective-permute-start | bytes 24584 | tf_op jit(solution)/shard_map/ppermute | solution.py:33
  67.5 12.4 %collective-permute-start.8 = (bf16[18,1,128]{2,1,0:T(2,128)(2,1)S(1)}, bf16[18,1,128]{2,1,0:T(2,128)(2,1)S(1)}, u32[]{:S(2)}, u32[]{:S(2)}) collective-permute-start(bf16[18,1,128]{2,1,0:T(2,128)(2,1)S(1)} %get-tuple-element.76), channel_id=1, source_target_pairs={{1,0},{2,1},{3,2},{4,3},{5,4},{6,5},{7,6},{8,7},{9,8},{10,9},{11,1... | collective-permute-start | bytes 13832 | tf_op jit(solution)/shard_map/ppermute | solution.py:33
  79.8 1.9 collective-permute-start.9
  81.8 1.9 collective-permute-start.4
  83.7 12.0 %collective-permute-start.5 = (bf16[18,1,128]{2,1,0:T(2,128)(2,1)S(1)}, bf16[18,1,128]{2,1,0:T(2,128)(2,1)S(1)}, u32[]{:S(2)}, u32[]{:S(2)}) collective-permute-start(bf16[18,1,128]{2,1,0:T(2,128)(2,1)S(1)} %get-tuple-element.73), channel_id=1, source_target_pairs={{1,0},{2,1},{3,2},{4,3},{5,4},{6,5},{7,6},{8,7},{9,8},{10,9},{11,1... | collective-permute-start | bytes 13832 | tf_op jit(solution)/shard_map/ppermute | solution.py:33
  100.2 1.1 convolution_bitcast_fusion.3
  105.0 1.4 fusion.11
  108.6 1.2 copy.111
  111.6 1.0 multiply_reduce_fusion.2
  119.5 1.0 convolution_bitcast_fusion.5
  123.3 1.0 fusion.1
  125.2 1.4 constant_dynamic-update-slice_fusion.3
  126.5 1.3 constant_dynamic-update-slice_fusion.2
  127.8 1.3 constant_dynamic-update-slice_fusion.1
  129.8 1.9 collective-permute-start.10
  131.7 11.2 %collective-permute-done.10 = bf16[2,16,4,128]{3,2,1,0:T(4,128)(2,1)S(1)} collective-permute-done((bf16[2,16,4,128]{3,2,1,0:T(4,128)(2,1)S(1)}, bf16[2,16,4,128]{3,2,1,0:T(4,128)(2,1)S(1)}, u32[]{:S(2)}, u32[]{:S(2)}) %collective-permute-start.10) | collective-permute-done | bytes 32800 | tf_op jit(solution)/shard_map/ppermute | solution.py:21
  142.9 1.9 collective-permute-start.11
  144.8 11.4 %collective-permute-done.11 = bf16[2,4,32,128]{3,2,1,0:T(8,128)(2,1)S(1)} collective-permute-done((bf16[2,4,32,128]{3,2,1,0:T(8,128)(2,1)S(1)}, bf16[2,4,32,128]{3,2,1,0:T(8,128)(2,1)S(1)}, u32[]{:S(2)}, u32[]{:S(2)}) %collective-permute-start.11) | collective-permute-done | bytes 65568 | tf_op jit(solution)/shard_map/ppermute | solution.py:21
  157.0 446.3 %all-reduce.2.cloned.1.call-done = f32[345220]{0:T(1024)} async-done(((f32[345220]{0:T(1024)}), f32[345220]{0:T(1024)}) %all-reduce.2.cloned.1.call-update) | async-done | bytes 1380896 | tf_op jit(solution)/shard_map/psum | solution.py:318
  606.4 1.8 fusion.54
  608.9 1.3 slice_multiply_fusion.18
  610.2 1.5 fusion.110
  611.7 1.9 slice_multiply_fusion
  (205 shorter events, 36.3 us)
Async XLA Ops:
  7.2 44.4 %copy-start = (bf16[128,512]{1,0:T(8,128)(2,1)S(1)}, bf16[128,512]{1,0:T(8,128)(2,1)}, u32[]{:S(2)}) copy-start(bf16[128,512]{1,0:T(8,128)(2,1)} %param.16) | copy-start | bytes 393220
  7.2 596.1 %all-reduce.2.cloned.1.call-start = ((), (), s32[]{:S(2)}) async-start(), calls=%async_computation | async-start | bytes 2768896 | tf_op jit(solution)/shard_map/psum | solution.py:318
  8.1 16.9 %collective-permute-start = (bf16[2,4,32,128]{3,2,1,0:T(8,128)(2,1)S(1)}, bf16[2,4,32,128]{3,2,1,0:T(8,128)(2,1)S(1)}, u32[]{:S(2)}, u32[]{:S(2)}) collective-permute-start(bf16[2,4,32,128]{3,2,1,0:T(8,128)(2,1)S(1)} %pad_maximum_fusion.14), channel_id=1, source_target_pairs={{0,752},{16,0},{32,16},{48,32},{64,48},{80,64},{96,80},{112,96},{1... | collective-permute-start | bytes 196616 | tf_op jit(solution)/shard_map/ppermute | solution.py:21
  21.3 74.7 %copy-start.32 = (f32[32]{0:T(128)}, f32[32]{0:T(128)S(1)}, u32[]{:S(2)}) copy-start(f32[32]{0:T(128)S(1)} %get-tuple-element.82) | copy-start | bytes 388
  21.3 81.0 %copy-start.30 = (f32[32]{0:T(128)}, f32[32]{0:T(128)S(1)}, u32[]{:S(2)}) copy-start(f32[32]{0:T(128)S(1)} %get-tuple-element.81) | copy-start | bytes 388
  24.9 22.5 %copy-start.36 = (f32[128]{0:T(128)S(1)}, f32[128]{0:T(128)}, u32[]{:S(2)}) copy-start(f32[128]{0:T(128)} %param.19) | copy-start | bytes 1540
  24.9 22.7 %copy-start.28 = (bf16[128,384]{1,0:T(8,128)(2,1)S(1)}, bf16[128,384]{1,0:T(8,128)(2,1)}, u32[]{:S(2)}) copy-start(bf16[128,384]{1,0:T(8,128)(2,1)} %param.14) | copy-start | bytes 294916
  25.0 10.1 %collective-permute-start.1 = (bf16[2,16,4,128]{3,2,1,0:T(4,128)(2,1)S(1)}, bf16[2,16,4,128]{3,2,1,0:T(4,128)(2,1)S(1)}, u32[]{:S(2)}, u32[]{:S(2)}) collective-permute-start(bf16[2,16,4,128]{3,2,1,0:T(4,128)(2,1)S(1)} %pad_maximum_fusion.16), channel_id=1, source_target_pairs={{0,15},{1,0},{2,1},{3,2},{4,3},{5,4},{6,5},{7,6},{8,7},{9,8},{10,9... | collective-permute-start | bytes 98312 | tf_op jit(solution)/shard_map/ppermute | solution.py:21
  35.1 32.3 %collective-permute-start.6 = (bf16[1,32,128]{2,1,0:T(8,128)(2,1)S(1)}, bf16[1,32,128]{2,1,0:T(8,128)(2,1)S(1)}, u32[]{:S(2)}, u32[]{:S(2)}) collective-permute-start(bf16[1,32,128]{2,1,0:T(8,128)(2,1)S(1)} %get-tuple-element.66), channel_id=1, source_target_pairs={{0,16},{16,32},{32,48},{48,64},{64,80},{80,96},{96,112},{112,128},... | collective-permute-start | bytes 24584 | tf_op jit(solution)/shard_map/ppermute | solution.py:30
  38.6 28.8 %collective-permute-start.7 = (bf16[1,32,128]{2,1,0:T(8,128)(2,1)S(1)}, bf16[1,32,128]{2,1,0:T(8,128)(2,1)S(1)}, u32[]{:S(2)}, u32[]{:S(2)}) collective-permute-start(bf16[1,32,128]{2,1,0:T(8,128)(2,1)S(1)} %get-tuple-element.67), channel_id=1, source_target_pairs={{16,0},{32,16},{48,32},{64,48},{80,64},{96,80},{112,96},{128,112},... | collective-permute-start | bytes 24584 | tf_op jit(solution)/shard_map/ppermute | solution.py:33
  52.1 43.6 %copy-start.5 = (bf16[9,128,128]{2,1,0:T(8,128)(2,1)S(1)}, bf16[9,128,128]{2,1,0:T(8,128)(2,1)}, u32[]{:S(2)}) copy-start(bf16[9,128,128]{2,1,0:T(8,128)(2,1)} %param.18) | copy-start | bytes 884740
  54.6 42.4 %copy-start.1 = (bf16[16,32,512]{2,1,0:T(8,128)(2,1)}, bf16[16,32,512]{2,1,0:T(8,128)(2,1)S(1)}, u32[]{:S(2)}) copy-start(bf16[16,32,512]{2,1,0:T(8,128)(2,1)S(1)} %fusion.39) | copy-start | bytes 1572868
  54.9 26.9 %collective-permute-start.2 = (bf16[1,32,128]{2,1,0:T(8,128)(2,1)S(1)}, bf16[1,32,128]{2,1,0:T(8,128)(2,1)S(1)}, u32[]{:S(2)}, u32[]{:S(2)}) collective-permute-start(bf16[1,32,128]{2,1,0:T(8,128)(2,1)S(1)} %get-tuple-element.78), channel_id=1, source_target_pairs={{0,16},{16,32},{32,48},{48,64},{64,80},{80,96},{96,112},{112,128},... | collective-permute-start | bytes 24584 | tf_op jit(solution)/shard_map/ppermute | solution.py:30
  56.8 25.0 %collective-permute-start.3 = (bf16[1,32,128]{2,1,0:T(8,128)(2,1)S(1)}, bf16[1,32,128]{2,1,0:T(8,128)(2,1)S(1)}, u32[]{:S(2)}, u32[]{:S(2)}) collective-permute-start(bf16[1,32,128]{2,1,0:T(8,128)(2,1)S(1)} %get-tuple-element.79), channel_id=1, source_target_pairs={{16,0},{32,16},{48,32},{64,48},{80,64},{96,80},{112,96},{128,112},... | collective-permute-start | bytes 24584 | tf_op jit(solution)/shard_map/ppermute | solution.py:33
  67.5 29.4 %collective-permute-start.8 = (bf16[18,1,128]{2,1,0:T(2,128)(2,1)S(1)}, bf16[18,1,128]{2,1,0:T(2,128)(2,1)S(1)}, u32[]{:S(2)}, u32[]{:S(2)}) collective-permute-start(bf16[18,1,128]{2,1,0:T(2,128)(2,1)S(1)} %get-tuple-element.76), channel_id=1, source_target_pairs={{1,0},{2,1},{3,2},{4,3},{5,4},{6,5},{7,6},{8,7},{9,8},{10,9},{11,1... | collective-permute-start | bytes 13832 | tf_op jit(solution)/shard_map/ppermute | solution.py:33
  79.8 17.0 %collective-permute-start.9 = (bf16[18,1,128]{2,1,0:T(2,128)(2,1)S(1)}, bf16[18,1,128]{2,1,0:T(2,128)(2,1)S(1)}, u32[]{:S(2)}, u32[]{:S(2)}) collective-permute-start(bf16[18,1,128]{2,1,0:T(2,128)(2,1)S(1)} %get-tuple-element.77), channel_id=1, source_target_pairs={{0,1},{1,2},{2,3},{3,4},{4,5},{5,6},{6,7},{7,8},{8,9},{9,10},{10,1... | collective-permute-start | bytes 13832 | tf_op jit(solution)/shard_map/ppermute | solution.py:30
  81.8 19.5 %collective-permute-start.4 = (bf16[18,1,128]{2,1,0:T(2,128)(2,1)S(1)}, bf16[18,1,128]{2,1,0:T(2,128)(2,1)S(1)}, u32[]{:S(2)}, u32[]{:S(2)}) collective-permute-start(bf16[18,1,128]{2,1,0:T(2,128)(2,1)S(1)} %get-tuple-element.72), channel_id=1, source_target_pairs={{0,1},{1,2},{2,3},{3,4},{4,5},{5,6},{6,7},{7,8},{8,9},{9,10},{10,1... | collective-permute-start | bytes 13832 | tf_op jit(solution)/shard_map/ppermute | solution.py:30
  83.7 17.6 %collective-permute-start.5 = (bf16[18,1,128]{2,1,0:T(2,128)(2,1)S(1)}, bf16[18,1,128]{2,1,0:T(2,128)(2,1)S(1)}, u32[]{:S(2)}, u32[]{:S(2)}) collective-permute-start(bf16[18,1,128]{2,1,0:T(2,128)(2,1)S(1)} %get-tuple-element.73), channel_id=1, source_target_pairs={{1,0},{2,1},{3,2},{4,3},{5,4},{6,5},{7,6},{8,7},{9,8},{10,9},{11,1... | collective-permute-start | bytes 13832 | tf_op jit(solution)/shard_map/ppermute | solution.py:33
  98.8 4.4 copy-start.9
  100.2 3.0 copy-start.35
  110.8 2.6 copy-start.6
  110.8 2.8 copy-start.13
  110.8 2.8 copy-start.16
  119.5 3.0 copy-start.11
  119.5 3.8 copy-start.2
  119.5 3.7 copy-start.10
  123.2 3.3 copy-start.38
  124.3 4.9 copy-start.25
  125.2 4.3 copy-start.12
  125.2 4.3 copy-start.14
  129.8 13.1 %collective-permute-start.10 = (bf16[2,16,4,128]{3,2,1,0:T(4,128)(2,1)S(1)}, bf16[2,16,4,128]{3,2,1,0:T(4,128)(2,1)S(1)}, u32[]{:S(2)}, u32[]{:S(2)}) collective-permute-start(bf16[2,16,4,128]{3,2,1,0:T(4,128)(2,1)S(1)} %pad_maximum_fusion.15), channel_id=1, source_target_pairs={{0,1},{1,2},{2,3},{3,4},{4,5},{5,6},{6,7},{7,8},{8,9},{9,10},{10,1... | collective-permute-start | bytes 98312 | tf_op jit(solution)/shard_map/ppermute | solution.py:21
  142.9 13.3 %collective-permute-start.11 = (bf16[2,4,32,128]{3,2,1,0:T(8,128)(2,1)S(1)}, bf16[2,4,32,128]{3,2,1,0:T(8,128)(2,1)S(1)}, u32[]{:S(2)}, u32[]{:S(2)}) collective-permute-start(bf16[2,4,32,128]{3,2,1,0:T(8,128)(2,1)S(1)} %pad_maximum_fusion.13), channel_id=1, source_target_pairs={{0,16},{16,32},{32,48},{48,64},{64,80},{80,96},{96,112},{112,128},... | collective-permute-start | bytes 196616 | tf_op jit(solution)/shard_map/ppermute | solution.py:21
  (22 other events, 32.9 us)
Sparse Core Ops, SparseCore 0:
  129.3 473.9 all-reduce.1
where the time goes:
time: 622 us; the launch traced here: 620 us
  waiting for transfers between devices  470 us (76%)
  starting transfers between devices  77.4 us (12%)
  matrix products  22.3 us (4%)
  local copies, waits for them, and re-layouts  19.4 us (3%)
  other arithmetic  16 us (3%)
  between operations  15.2 us (2%)
    psum x1, waiting for transfers between devices, per_device(): totals = lax.psum(flat_grads, ('lon', 'lat'))  446 us
    ppermute x4, starting transfers between devices, extended(): lax.ppermute(lax.slice_in_dim(block, 0, width, axis=dim), axis, backward)  43.1 us
    ppermute x4, starting transfers between devices, passed_along(): return lax.ppermute(value, axis, pairs)  25 us
    ppermute x4, waiting for transfers between devices, passed_along(): return lax.ppermute(value, axis, pairs)  23.8 us
  transfers between devices with their start and end apart: 13, of which 4 were waited for; matrix products, arithmetic and copies ran while one was open for 3% of the time, Pallas kernels for 0%

commit v1 on v0

v1 whole, which is shorter than its diff:
```python
import math

import jax
import jax.numpy as jnp
from jax import lax
from jax.sharding import Mesh
from jax.sharding import PartitionSpec as P

HEADS = 4
WIN = 8
SHIFT = 4
SPAN = 15
HEAD_DIM = 32
TOKEN_RIM = 4
GRAD_RIM = 5
LABEL_RIM = 8

LON = ("zl", "x", "c")
LAT = ("zh", "y")
NEAR = ("x", "c")
FAR = ("y", "zl", "zh")

epsilon = 1e-05


def swapped(value, axes, first):
    count = lax.axis_size(axes)
    pairs = []
    for source in range(count):
        up = (source % 2 == 0) == first
        pairs.append((source, (source + 1) % count if up else (source - 1) % count))
    return lax.ppermute(value, axes, pairs)


def traded(to_next, to_prev, axes):
    even = lax.axis_index(axes) % 2 == 0
    later = swapped(jnp.where(even, to_prev, to_next), axes, False)
    near = swapped(jnp.where(even, to_next, to_prev), axes, True)
    return jnp.where(even, later, near), jnp.where(even, near, later)


def lon_halo(tokens, grad_out, ids):
    row_count, col_count, width = tokens.shape
    id_rows = jnp.pad(ids[row_count - LABEL_RIM :].T, ((0, 0), (0, width - LABEL_RIM)))[None]
    to_next = jnp.concatenate([tokens[-TOKEN_RIM:], grad_out[-GRAD_RIM:], id_rows])
    to_prev = jnp.concatenate([tokens[:TOKEN_RIM], grad_out[:GRAD_RIM], jnp.zeros_like(id_rows)])
    before, after = traded(to_next, to_prev, LON)
    split = TOKEN_RIM + GRAD_RIM
    tokens = jnp.concatenate([before[:TOKEN_RIM], tokens, after[:TOKEN_RIM]])
    grad_out = jnp.concatenate([before[TOKEN_RIM:split], grad_out, after[TOKEN_RIM:split]])
    ids = jnp.concatenate([before[split, :, :LABEL_RIM].T, ids])
    return tokens, grad_out, ids


def lat_halo(tokens, grad_out, ids):
    token_rows, col_count, width = tokens.shape
    grad_rows = grad_out.shape[0]
    token_size, grad_size = token_rows * TOKEN_RIM, grad_rows * GRAD_RIM
    id_cols = jnp.pad(ids[:, col_count - LABEL_RIM :], ((0, 0), (0, width - LABEL_RIM)))

    def packed(token_part, grad_part, id_part):
        return jnp.concatenate(
            [token_part.reshape(token_size, width), grad_part.reshape(grad_size, width), id_part]
        )

    def unpacked(message):
        return (
            message[:token_size].reshape(token_rows, TOKEN_RIM, width),
            message[token_size : token_size + grad_size].reshape(grad_rows, GRAD_RIM, width),
            message[token_size + grad_size :, :LABEL_RIM],
        )

    to_next = packed(tokens[:, -TOKEN_RIM:], grad_out[:, -GRAD_RIM:], id_cols)
    to_prev = packed(tokens[:, :TOKEN_RIM], grad_out[:, :GRAD_RIM], jnp.zeros_like(id_cols))
    before, after = traded(to_next, to_prev, LAT)
    tokens_before, grad_before, ids_before = unpacked(before)
    tokens_after, grad_after, _ = unpacked(after)
    return (
        jnp.concatenate([tokens_before, tokens, tokens_after], axis=1),
        jnp.concatenate([grad_before, grad_out, grad_after], axis=1),
        jnp.concatenate([ids_before, ids], axis=1),
    )


def scattered_sum(partial, axes):
    count = lax.axis_size(axes)
    chunks = partial.reshape(count, partial.shape[0] // count, partial.shape[1])
    received = lax.all_to_all(chunks, axes, 0, 0, tiled=True)
    return jnp.sum(received.astype(jnp.float32), axis=0)


def gathered(chunk, axes):
    count = lax.axis_size(axes)
    copies = jnp.broadcast_to(chunk[None], (count,) + chunk.shape)
    return lax.all_to_all(copies, axes, 0, 0, tiled=True).reshape(-1, chunk.shape[1])


def total_over_devices(rows, grad_scale):
    count = lax.axis_size(NEAR) * lax.axis_size(FAR)
    total_rows = rows.shape[0]
    rows = jnp.pad(rows, ((0, -total_rows % count), (0, 0))).astype(jnp.bfloat16)
    near = scattered_sum(rows, NEAR).astype(jnp.bfloat16)
    own = (scattered_sum(near, FAR) * grad_scale).astype(jnp.bfloat16)
    for axes in GATHERS:
        own = gathered(own, axes)
    return own[:total_rows].astype(jnp.float32)


GATHERS = (("zl", "zh"), ("y",), ("x", "c"))


def blocks_of(matrix):
    height, width = matrix.shape
    return matrix.reshape(height, width // 128, 128).transpose(1, 0, 2).reshape(-1, 128)


def from_blocks(rows, width):
    count = width // 128
    return rows.reshape(count, -1, 128).transpose(1, 0, 2).reshape(-1, width)


def layer_norm(values, gain_vec):
    average = jnp.mean(values, axis=-1, keepdims=True)
    centred = values - average
    variance = jnp.mean(centred * centred, axis=-1, keepdims=True)
    inverse = lax.rsqrt(variance + epsilon)
    normed = centred * inverse
    return ((normed * gain_vec).astype(jnp.bfloat16), normed, inverse)


def layer_norm_back(grad_in, normed, inverse, gain_vec):
    scaled = grad_in * gain_vec
    first_mean = jnp.mean(scaled, axis=-1, keepdims=True)
    second = jnp.mean(scaled * normed, axis=-1, keepdims=True)
    return inverse * (scaled - first_mean - normed * second)


def gelu_slope(pre_act):
    cumulative = 0.5 * (1.0 + jax.scipy.special.erf(pre_act * 0.7071067811865476))
    density = jnp.exp(-0.5 * pre_act * pre_act) * 0.3989422804014327
    return cumulative + pre_act * density


def offsets_onehot():
    places = jnp.arange(WIN, dtype=jnp.int32)
    distance = places[:, None] - places[None, :] + WIN - 1
    return (distance[:, :, None] == jnp.arange(SPAN, dtype=jnp.int32)[None, None, :]).astype(
        jnp.float32
    )


def bias_matrix(position_bias):
    onehot = offsets_onehot()
    spread = jnp.einsum(
        "hmn,acm,bdn->habcd", position_bias, onehot, onehot, precision=lax.Precision.HIGHEST
    )
    return spread.reshape(HEADS, WIN * WIN, WIN * WIN)


def to_windows(values_grid):
    row_count, col_count = (values_grid.shape[0], values_grid.shape[1])
    trailing = values_grid.shape[2:]
    reshaped = values_grid.reshape((row_count // WIN, WIN, col_count // WIN, WIN) + trailing)
    permute = (0, 2, 1, 3) + tuple(range(4, 4 + len(trailing)))
    return reshaped.transpose(permute).reshape(
        (row_count // WIN * (col_count // WIN), WIN * WIN) + trailing
    )


def from_windows(blocks, row_count, col_count):
    trailing = blocks.shape[2:]
    reshaped = blocks.reshape((row_count // WIN, col_count // WIN, WIN, WIN) + trailing)
    permute = (0, 2, 1, 3) + tuple(range(4, 4 + len(trailing)))
    return reshaped.transpose(permute).reshape((row_count, col_count) + trailing)


def attend(windows, labels_win, qkv_weight, biases):
    window_count, length, width = windows.shape
    qkv_all = jnp.dot(windows, qkv_weight, preferred_element_type=jnp.float32).astype(jnp.bfloat16)
    split_heads = qkv_all.reshape(window_count, length, 3, HEADS, HEAD_DIM)
    query_heads, key_heads, value_heads = (
        split_heads[:, :, 0],
        split_heads[:, :, 1],
        split_heads[:, :, 2],
    )
    score_scale = HEAD_DIM ** (-0.5)
    scores = (
        jnp.einsum("nihe,njhe->nhij", query_heads, key_heads, preferred_element_type=jnp.float32)
        * score_scale
        + biases[None]
    )
    allowed = labels_win[:, None, :, None] == labels_win[:, None, None, :]
    scores = jnp.where(allowed, scores, -jnp.inf)
    probabilities = jax.nn.softmax(scores, axis=-1)
    weights = probabilities.astype(jnp.bfloat16)
    mixed_win = jnp.einsum(
        "nhij,njhe->nihe", weights, value_heads, preferred_element_type=jnp.float32
    ).astype(jnp.bfloat16)
    return (mixed_win.reshape(window_count, length, width), qkv_all, probabilities, weights)


def attend_back(grad_mixed, qkv_all, probabilities, weights):
    window_count, length, width = grad_mixed.shape
    split_heads = qkv_all.reshape(window_count, length, 3, HEADS, HEAD_DIM)
    query_heads, key_heads, value_heads = (
        split_heads[:, :, 0],
        split_heads[:, :, 1],
        split_heads[:, :, 2],
    )
    grad_heads = grad_mixed.reshape(window_count, length, HEADS, HEAD_DIM)
    grad_probs = jnp.einsum(
        "nihe,njhe->nhij", grad_heads, value_heads, preferred_element_type=jnp.float32
    )
    grad_value = jnp.einsum(
        "nhij,nihe->njhe", weights, grad_heads, preferred_element_type=jnp.float32
    )
    grad_scores = probabilities * (
        grad_probs - jnp.sum(probabilities * grad_probs, axis=-1, keepdims=True)
    )
    grad_scores_b = grad_scores.astype(jnp.bfloat16)
    score_scale = HEAD_DIM ** (-0.5)
    grad_query = (
        jnp.einsum("nhij,njhe->nihe", grad_scores_b, key_heads, preferred_element_type=jnp.float32)
        * score_scale
    )
    grad_key = (
        jnp.einsum(
            "nhij,nihe->njhe", grad_scores_b, query_heads, preferred_element_type=jnp.float32
        )
        * score_scale
    )
    stacked = jnp.stack([grad_query, grad_key, grad_value], axis=2)
    return (stacked.reshape(window_count, length, 3 * width).astype(jnp.bfloat16), grad_scores)


def conv_forward(padded, conv_weight, keep):
    row_count = padded.shape[0] - 2
    col_count = padded.shape[1] - 2
    summed = jnp.zeros((row_count, col_count, conv_weight.shape[2]), jnp.float32)
    for tap_row in range(3):
        for tap_col in range(3):
            window_part = padded[tap_row : tap_row + row_count, tap_col : tap_col + col_count]
            product = jnp.dot(
                window_part, conv_weight[3 * tap_row + tap_col], preferred_element_type=jnp.float32
            )
            summed = summed + product * keep[tap_col][None, :, None]
    return summed


def conv_weight_sum(padded, grad_field, keep):
    row_count = padded.shape[0] - 2
    col_count = padded.shape[1] - 2
    pieces = []
    for tap_row in range(3):
        for tap_col in range(3):
            window_part = padded[tap_row : tap_row + row_count, tap_col : tap_col + col_count]
            masked = grad_field * keep[tap_col][None, :, None]
            pieces.append(
                jnp.einsum("lwc,lwd->cd", window_part, masked, preferred_element_type=jnp.float32)
            )
    return jnp.stack(pieces)


def conv_input_grad(grad_padded, conv_weight, keep):
    row_count = grad_padded.shape[0] - 2
    col_count = grad_padded.shape[1] - 2
    summed = jnp.zeros((row_count, col_count, conv_weight.shape[1]), jnp.float32)
    for tap_row in range(3):
        for tap_col in range(3):
            start_row = 2 - tap_row
            start_col = 2 - tap_col
            window_part = grad_padded[
                start_row : start_row + row_count, start_col : start_col + col_count
            ]
            window_part = (
                window_part * keep[start_col][None, :, None]
            )
            summed = summed + jnp.einsum(
                "lwd,cd->lwc",
                window_part,
                conv_weight[3 * tap_row + tap_col],
                preferred_element_type=jnp.float32,
            )
    return summed


def local_work(
    tokens_ext,
    grad_ext,
    labels,
    positions,
    lat_total,
    qkv_weight,
    proj_weight,
    up_weight,
    down_weight,
    conv_weight,
    gain_one,
    gain_two,
    position_bias,
):
    row_count, col_count, width = tokens_ext.shape
    own_rows, own_cols = row_count - 2 * TOKEN_RIM, col_count - 2 * TOKEN_RIM
    keep = jnp.stack(
        [positions != 0, jnp.ones_like(positions, jnp.bool_), positions != lat_total - 1]
    ).astype(jnp.bfloat16)
    keep_own = keep[:, TOKEN_RIM:-TOKEN_RIM]
    owned = lambda grid: grid[WIN:, WIN:]
    source = tokens_ext.astype(jnp.float32)
    biases = bias_matrix(position_bias)
    ln_one, normed_one, inverse_one = layer_norm(source, gain_one)
    mixed_win, qkv_all, probabilities, weights = attend(
        to_windows(ln_one), to_windows(labels), qkv_weight, biases
    )
    mixed_grid = from_windows(mixed_win, row_count, col_count)
    projected = jnp.dot(mixed_grid, proj_weight, preferred_element_type=jnp.float32).astype(
        jnp.bfloat16
    )
    middle = source + projected.astype(jnp.float32)
    ln_two, normed_two, inverse_two = layer_norm(middle, gain_two)
    pre_act = jnp.dot(ln_two, up_weight, preferred_element_type=jnp.float32)
    hidden = jax.nn.gelu(pre_act, approximate=False).astype(jnp.bfloat16)
    block_out = (middle + jnp.dot(hidden, down_weight, preferred_element_type=jnp.float32)).astype(
        jnp.bfloat16
    )
    rim = TOKEN_RIM - 1
    padded = block_out[rim:-rim, rim:-rim]
    downscaled = conv_forward(padded, conv_weight, keep_own).astype(jnp.bfloat16)
    conv_sum = conv_weight_sum(
        padded, grad_ext[GRAD_RIM:-GRAD_RIM, GRAD_RIM:-GRAD_RIM], keep_own
    )
    grad_block = conv_input_grad(grad_ext, conv_weight, keep)
    grad_block_b = grad_block.astype(jnp.bfloat16)
    down_sum = jnp.einsum(
        "lwf,lwc->fc", owned(hidden), owned(grad_block_b), preferred_element_type=jnp.float32
    )
    grad_hidden = jnp.einsum(
        "lwc,fc->lwf", grad_block_b, down_weight, preferred_element_type=jnp.float32
    )
    grad_pre = (grad_hidden * gelu_slope(pre_act)).astype(jnp.bfloat16)
    up_sum = jnp.einsum(
        "lwc,lwf->cf", owned(ln_two), owned(grad_pre), preferred_element_type=jnp.float32
    )
    grad_ln_two = jnp.einsum("lwf,cf->lwc", grad_pre, up_weight, preferred_element_type=jnp.float32)
    gain_two_sum = jnp.sum(owned(grad_ln_two * normed_two), axis=(0, 1))
    grad_middle = grad_block + layer_norm_back(grad_ln_two, normed_two, inverse_two, gain_two)
    grad_att = grad_middle.astype(jnp.bfloat16)
    proj_sum = jnp.einsum(
        "lwc,lwd->cd", owned(mixed_grid), owned(grad_att), preferred_element_type=jnp.float32
    )
    grad_mixed = jnp.einsum(
        "lwd,cd->lwc", grad_att, proj_weight, preferred_element_type=jnp.float32
    ).astype(jnp.bfloat16)
    grad_qkv_win, grad_scores = attend_back(
        to_windows(grad_mixed), qkv_all, probabilities, weights
    )
    length = WIN * WIN
    by_place = grad_scores.reshape(row_count // WIN, col_count // WIN, HEADS, length, length)
    bias_sum = jnp.sum(by_place[1:, 1:], axis=(0, 1))
    grad_qkv_all = from_windows(grad_qkv_win, row_count, col_count)
    qkv_sum = jnp.einsum(
        "lwc,lwk->ck", owned(ln_one), owned(grad_qkv_all), preferred_element_type=jnp.float32
    )
    grad_ln_one = jnp.einsum(
        "lwk,ck->lwc", grad_qkv_all, qkv_weight, preferred_element_type=jnp.float32
    )
    gain_one_sum = jnp.sum(owned(grad_ln_one * normed_one), axis=(0, 1))
    grad_tokens = (
        grad_middle + layer_norm_back(grad_ln_one, normed_one, inverse_one, gain_one)
    ).astype(jnp.bfloat16)[TOKEN_RIM:-TOKEN_RIM, TOKEN_RIM:-TOKEN_RIM]
    onehot = offsets_onehot()
    table_sum = jnp.einsum(
        "habcd,acm,bdn->hmn",
        bias_sum.reshape(HEADS, WIN, WIN, WIN, WIN),
        onehot,
        onehot,
        precision=lax.Precision.HIGHEST,
    )
    rows = jnp.concatenate(
        [
            conv_sum.reshape(-1, 128),
            blocks_of(qkv_sum),
            proj_sum,
            blocks_of(up_sum),
            down_sum,
            gain_one_sum[None],
            gain_two_sum[None],
            jnp.pad(table_sum.reshape(-1), (0, 124)).reshape(8, 128),
        ]
    )
    return downscaled, grad_tokens, rows


def per_device(
    tokens,
    grad_out,
    window_ids,
    qkv_weight,
    proj_weight,
    up_weight,
    down_weight,
    conv_weight,
    gain_one,
    gain_two,
    position_bias,
):
    row_count, col_count, width = tokens.shape
    lat_total = col_count * lax.axis_size(LAT)
    tokens_all = row_count * lat_total * lax.axis_size(LON)
    ids = window_ids.astype(jnp.bfloat16)
    tokens_ext, grad_ext, ids_ext = lat_halo(*lon_halo(tokens, grad_out, ids))
    first_col = lax.axis_index(LAT) * col_count
    steps = jnp.arange(col_count + 2 * TOKEN_RIM, dtype=jnp.int32)
    positions = jnp.remainder(first_col + steps - TOKEN_RIM, lat_total)
    shifted_cols = jnp.remainder(first_col + steps - LABEL_RIM, lat_total)
    seam_flag = (shifted_cols >= lat_total - SHIFT).astype(jnp.int32)
    labels = ids_ext.astype(jnp.int32) * 2 + seam_flag[None, :]
    downscaled, grad_tokens, rows = local_work(
        tokens_ext,
        grad_ext,
        labels,
        positions,
        lat_total,
        qkv_weight,
        proj_weight,
        up_weight,
        down_weight,
        conv_weight,
        gain_one,
        gain_two,
        position_bias,
    )
    totals = total_over_devices(rows, 1.0 / math.sqrt(tokens_all))
    sizes = (9 * width, 3 * width, width, 4 * width, 4 * width, 1, 1, 8)
    pieces = []
    offset = 0
    for size in sizes:
        pieces.append(totals[offset : offset + size])
        offset = offset + size
    return (
        downscaled,
        grad_tokens,
        from_blocks(pieces[1], 3 * width),
        pieces[2],
        from_blocks(pieces[3], 4 * width),
        pieces[4],
        pieces[0].reshape(9, width, width),
        pieces[5][0],
        pieces[6][0],
        pieces[7].reshape(-1)[: HEADS * SPAN * SPAN].reshape(HEADS, SPAN, SPAN),
    )


def solution(mesh):
    lon_count, lat_count = mesh.devices.shape
    near = math.gcd(lon_count, 8)
    parts = (lon_count // near, near // 2, 2, 2, lat_count // 2)
    fine = Mesh(mesh.devices.reshape(parts), ("zl", "x", "c", "zh", "y"))
    grid = P(LON, LAT, None)
    return jax.shard_map(
        per_device,
        mesh=fine,
        in_specs=(grid, grid, P(LON, LAT)) + (P(),) * 8,
        out_specs=(grid, grid) + (P(),) * 8,
        check_vma=False,
    )
```

time: 622 us -> 200 us (0.32)
  waiting for transfers between devices: 470 us -> 55.1 us
  starting transfers between devices: 77.4 us -> 61.8 us
  between operations: 15.2 us -> 1.8 us
  local copies, waits for them, and re-layouts: 19.4 us -> 32.7 us
  matrix products: 22.3 us -> 31.5 us
    psum x1 -> x0, waiting for transfers between devices: 446 us -> none  [per_device(): totals = lax.psum(flat_grads, ('lon', 'lat'))]
    all_to_all x0 -> x5, waiting for transfers between devices: none -> 51.8 us  [the longest x3 27.1 us: gathered(): lax.all_to_all(copies, axes, 0, 0, tiled=True).reshape(-1, chunk.shape[1])]
    ppermute x12 -> x4, starting transfers between devices: 77.3 us -> 32.4 us  [swapped(): return lax.ppermute(value, axes, pairs)]
    all_to_all x0 -> x5, starting transfers between devices: none -> 29.4 us  [the longest x3 15.4 us: gathered(): lax.all_to_all(copies, axes, 0, 0, tiled=True).reshape(-1, chunk.shape[1])]
    ppermute x12 -> x4, waiting for transfers between devices: 23.8 us -> 3.34 us  [swapped(): return lax.ppermute(value, axes, pairs)]
    mul x6 -> x2, other arithmetic: 8.1 us -> 0.71 us  [the longest x1 0.63 us: attend_back(): probabilities * (grad_probs - jnp.sum(probabilities * grad_probs, axis=-1...]
  transfers between devices with their start and end apart: 13 -> 9, of which waited for: 4 -> 6; matrix products, arithmetic and copies ran while one was open for 3% -> 3% of each run, Pallas kernels for 0% -> 0%
where the time goes in v1:
time: 200 us; the launch traced here: 198 us
  starting transfers between devices  61.8 us (31%)
  waiting for transfers between devices  55.1 us (28%)
  local copies, waits for them, and re-layouts  32.7 us (16%)
  matrix products  31.5 us (16%)
  other arithmetic  15.5 us (8%)
    ppermute x4, starting transfers between devices, swapped(): return lax.ppermute(value, axes, pairs)  32.4 us
    all_to_all x3, waiting for transfers between devices, gathered(): lax.all_to_all(copies, axes, 0, 0, tiled=True).reshape(-1, chunk.shape[1])  27.1 us
    all_to_all x2, waiting for transfers between devices, scattered_sum(): received = lax.all_to_all(chunks, axes, 0, 0, tiled=True)  24.7 us
    all_to_all x3, starting transfers between devices, gathered(): lax.all_to_all(copies, axes, 0, 0, tiled=True).reshape(-1, chunk.shape[1])  15.4 us
    all_to_all x2, starting transfers between devices, scattered_sum(): received = lax.all_to_all(chunks, axes, 0, 0, tiled=True)  14.1 us
    convert_element_type x1, other arithmetic, local_work(): hidden = jax.nn.gelu(pre_act, approximate=False).astype(jnp.bfloat16)  4.45 us
    unnamed x73, local copies, waits for them, and re-layouts  4.06 us
  transfers between devices with their start and end apart: 9, of which 6 were waited for; matrix products, arithmetic and copies ran while one was open for 3% of the time, Pallas kernels for 0%

profile of v1, /device:TPU:1, one launch (start us, length us, event | category | flops | bytes accessed | tf_op | source)
XLA Modules:
  0.0 198.4 jit_solution(12854267178524896636)
XLA Ops:
  3.3 4.5 %collective-permute-start = (bf16[10,32,128]{2,1,0:T(8,128)(2,1)S(1)}, bf16[10,32,128]{2,1,0:T(8,128)(2,1)S(1)}, u32[]{:S(2)}, u32[]{:S(2)}) collective-permute-start(bf16[10,32,128]{2,1,0:T(8,128)(2,1)S(1)} %get-tuple-element.116), channel_id=1, source_target_pairs={{0,752},{16,32},{32,16},{48,64},{64,48},{80,96},{96,80},{112,128},... | collective-permute-start | bytes 245768 | tf_op jit(solution)/shard_map/ppermute | solution.py:32
  7.9 13.3 %collective-permute-start.1 = (bf16[10,32,128]{2,1,0:T(8,128)(2,1)S(1)}, bf16[10,32,128]{2,1,0:T(8,128)(2,1)S(1)}, u32[]{:S(2)}, u32[]{:S(2)}) collective-permute-start(bf16[10,32,128]{2,1,0:T(8,128)(2,1)S(1)} %get-tuple-element.117), channel_id=1, source_target_pairs={{0,16},{16,0},{32,48},{48,32},{64,80},{80,64},{96,112},{112,96},{1... | collective-permute-start | bytes 245768 | tf_op jit(solution)/shard_map/ppermute | solution.py:32
  25.4 12.7 %collective-permute-start.2 = (bf16[250,128]{0,1:T(8,128)(2,1)S(1)}, bf16[250,128]{0,1:T(8,128)(2,1)S(1)}, u32[]{:S(2)}, u32[]{:S(2)}) collective-permute-start(bf16[250,128]{0,1:T(8,128)(2,1)S(1)} %get-tuple-element.108), channel_id=1, source_target_pairs={{0,15},{1,2},{2,1},{3,4},{4,3},{5,6},{6,5},{7,8},{8,7},{9,10},{10,... | collective-permute-start | bytes 192008 | tf_op jit(solution)/shard_map/ppermute | solution.py:32
  38.1 1.9 collective-permute-start.3
  40.1 3.3 %collective-permute-done.3 = bf16[250,128]{0,1:T(8,128)(2,1)S(1)} collective-permute-done((bf16[250,128]{0,1:T(8,128)(2,1)S(1)}, bf16[250,128]{0,1:T(8,128)(2,1)S(1)}, u32[]{:S(2)}, u32[]{:S(2)}) %collective-permute-start.3) | collective-permute-done | bytes 64032 | tf_op jit(solution)/shard_map/ppermute | solution.py:32
  50.0 1.0 fusion.218
  51.7 1.9 copy.362
  53.6 3.3 %fusion.216 = (f32[15,4,64]{2,1,0:T(4,128)S(1)}, f32[15,4,64,64]{2,3,1,0:T(8,128)}) fusion(f32[4,64,64]{1,2,0:T(8,128)S(1)} %reshape.388, pred[15,64,64]{1,2,0:T(8,128)(4,1)} %broadcast_compare_fusion, bf16[15,64,3,4,32]{1,4,3,2,0:T(8,128)(2,1)S(1)} %bitcast.405), kind=kOutput, calls=%fused_computation.368 | convolution fusion | flops 16957504 | bytes 2173952 | tf_op jit(solution)/shard_map/sub | solution.py:194
  57.6 2.7 %fusion.19 = bf16[15,64,4,32]{1,3,2,0:T(8,128)(2,1)} fusion(bf16[15,64,3,4,32]{1,4,3,2,0:T(8,128)(2,1)S(1)} %bitcast.406, f32[15,4,64,64]{2,3,1,0:T(8,128)} %get-tuple-element.134, f32[15,4,64]{2,1,0:T(4,128)S(1)} %get-tuple-element.133), kind=kOutput, calls=%fused_computation.44 | convolution fusion | flops 16343040 | bytes 1751040 | tf_op jit(solution)/shard_map/nhij,njhe->nihe/dot_general | solution.py:196
  60.3 1.9 copy.371
  62.8 1.1 fusion.217
  65.5 4.4 %fusion.3 = bf16[24,40,512]{2,1,0:T(8,128)(2,1)S(1)} fusion(f32[24,40,512]{2,1,0:T(8,128)S(1)} %get-tuple-element.137, u32[40,512]{1,0:T(8,128)S(1)} %get-tuple-element.91, u32[40,512]{1,0:T(8,128)S(1)} %get-tuple-element.90), kind=kLoop, calls=%fused_computation.5 | loop fusion | flops 33423360 | bytes 3112960 | tf_op jit(solution)/shard_map/convert_element_type | solution.py:322
  70.0 1.1 fusion.9
  73.9 1.2 fusion.212
  76.7 1.6 copy.376
  78.3 3.3 %fusion.20 = bf16[15,64,1,4,32]{1,4,3,0,2:T(8,128)(2,1)} fusion(bf16[15,64,4,32]{1,3,2,0:T(8,128)(2,1)} %copy.376, f32[15,4,64,64]{2,3,1,0:T(8,128)} %get-tuple-element.134, f32[15,4,64]{2,1,0:T(4,128)S(1)} %copy-done.25), kind=kOutput, calls=%fused_computation.45 | convolution fusion | flops 16343040 | bytes 1489920 | tf_op jit(solution)/shard_map/nhij,nihe->njhe/dot_general | solution.py:214
  84.3 1.2 fusion.22
  91.7 2.7 %pad_maximum_fusion = bf16[15,64,3,4,32]{1,4,3,0,2:T(8,128)(2,1)} fusion(bf16[15,64,1,4,32]{1,4,3,0,2:T(8,128)(2,1)} %fusion.20, bf16[15,64,1,4,32]{1,4,3,0,2:T(8,128)(2,1)S(1)} %fusion.21, bf16[15,64,1,4,32]{1,4,3,0,2:T(8,128)(2,1)} %fusion.22), kind=kLoop, calls=%fused_computation.35 | loop fusion | flops 737280 | bytes 1474560 | tf_op jit(solution)/shard_map/stack | solution.py:232
  94.3 3.8 %copy.381 = bf16[15,64,3,4,32]{4,3,2,1,0:T(4,128)(2,1)S(1)} copy(bf16[15,64,3,4,32]{1,4,3,0,2:T(8,128)(2,1)} %pad_maximum_fusion) | data formatting | bytes 1474560 | tf_op jit(solution)/shard_map/stack | solution.py:232
  98.1 2.5 %convert_element_type.168 = bf16[3,5,8,8,384]{4,3,2,1,0:T(8,128)(2,1)} reshape(bf16[15,64,3,4,32]{4,3,2,1,0:T(4,128)(2,1)S(1)} %copy.381) | data formatting | bytes 1474560 | tf_op jit(solution)/shard_map/convert_element_type | solution.py:233
  100.6 1.2 copy.382
  101.9 1.6 fusion.211
  106.5 4.7 %all-to-all-start = ((bf16[8,384,128]{2,1,0:T(8,128)(2,1)}), bf16[8,384,128]{2,1,0:T(8,128)(2,1)S(1)}, u32[]{:S(2)}, u32[]{:S(2)}) async-start(bf16[8,384,128]{2,1,0:T(8,128)(2,1)} %bitcast.103), calls=%async_computation | async-start | bytes 1572864 | tf_op jit(solution)/shard_map/all_to_all | solution.py:88
  111.7 11.9 %all-to-all-done = bf16[8,384,128]{2,1,0:T(8,128)(2,1)S(1)} async-done(((bf16[8,384,128]{2,1,0:T(8,128)(2,1)}), bf16[8,384,128]{2,1,0:T(8,128)(2,1)S(1)}, u32[]{:S(2)}, u32[]{:S(2)}) %all-to-all-start) | async-done | bytes 786464 | tf_op jit(solution)/shard_map/all_to_all | solution.py:88
  124.4 9.3 %all-to-all-start.1 = ((bf16[96,4,128]{2,1,0:T(4,128)(2,1)}), bf16[96,4,128]{2,1,0:T(4,128)(2,1)S(1)}, u32[]{:S(2)}, u32[]{:S(2)}) async-start(bf16[96,4,128]{2,1,0:T(4,128)(2,1)} %bitcast.104), calls=%async_computation.1 | async-start | bytes 196608 | tf_op jit(solution)/shard_map/all_to_all | solution.py:88
  134.1 12.8 %all-to-all-done.1 = bf16[96,4,128]{2,1,0:T(4,128)(2,1)S(1)} async-done(((bf16[96,4,128]{2,1,0:T(4,128)(2,1)}), bf16[96,4,128]{2,1,0:T(4,128)(2,1)S(1)}, u32[]{:S(2)}, u32[]{:S(2)}) %all-to-all-start.1) | async-done | bytes 98336 | tf_op jit(solution)/shard_map/all_to_all | solution.py:88
  147.5 3.5 %all-to-all-start.2 = ((bf16[12,4,128]{2,1,0:T(4,128)(2,1)}), bf16[12,4,128]{2,1,0:T(4,128)(2,1)S(1)}, u32[]{:S(2)}, u32[]{:S(2)}) async-start(bf16[12,4,128]{2,1,0:T(4,128)(2,1)} %broadcast_in_dim.41), calls=%async_computation.2 | async-start | bytes 24576 | tf_op jit(solution)/shard_map/all_to_all | solution.py:95
  151.2 8.7 %all-to-all-done.2 = bf16[12,4,128]{2,1,0:T(4,128)(2,1)S(1)} async-done(((bf16[12,4,128]{2,1,0:T(4,128)(2,1)}), bf16[12,4,128]{2,1,0:T(4,128)(2,1)S(1)}, u32[]{:S(2)}, u32[]{:S(2)}) %all-to-all-start.2) | async-done | bytes 12320 | tf_op jit(solution)/shard_map/all_to_all | solution.py:95
  160.5 3.4 %all-to-all-start.3 = ((bf16[8,48,128]{2,1,0:T(8,128)(2,1)}), bf16[8,48,128]{2,1,0:T(8,128)(2,1)S(1)}, u32[]{:S(2)}, u32[]{:S(2)}) async-start(bf16[8,48,128]{2,1,0:T(8,128)(2,1)} %broadcast_in_dim.43), calls=%async_computation.3 | async-start | bytes 196608 | tf_op jit(solution)/shard_map/all_to_all | solution.py:95
  164.0 7.3 %all-to-all-done.3 = bf16[8,48,128]{2,1,0:T(8,128)(2,1)S(1)} async-done(((bf16[8,48,128]{2,1,0:T(8,128)(2,1)}), bf16[8,48,128]{2,1,0:T(8,128)(2,1)S(1)}, u32[]{:S(2)}, u32[]{:S(2)}) %all-to-all-start.3) | async-done | bytes 98336 | tf_op jit(solution)/shard_map/all_to_all | solution.py:95
  172.3 8.5 %all-to-all-start.4 = ((bf16[8,384,128]{2,1,0:T(8,128)(2,1)}), bf16[8,384,128]{2,1,0:T(8,128)(2,1)S(1)}, u32[]{:S(2)}, u32[]{:S(2)}) async-start(bf16[8,384,128]{2,1,0:T(8,128)(2,1)} %broadcast_in_dim.45), calls=%async_computation.4 | async-start | bytes 1572864 | tf_op jit(solution)/shard_map/all_to_all | solution.py:95
  182.0 11.1 %all-to-all-done.4 = bf16[8,384,128]{2,1,0:T(8,128)(2,1)S(1)} async-done(((bf16[8,384,128]{2,1,0:T(8,128)(2,1)}), bf16[8,384,128]{2,1,0:T(8,128)(2,1)S(1)}, u32[]{:S(2)}, u32[]{:S(2)}) %all-to-all-start.4) | async-done | bytes 786464 | tf_op jit(solution)/shard_map/all_to_all | solution.py:95
  (224 shorter events, 43.2 us)
Async XLA Ops:
  0.6 64.0 %copy-start = (bf16[128,512]{1,0:T(8,128)(2,1)S(1)}, bf16[128,512]{1,0:T(8,128)(2,1)}, u32[]{:S(2)}) copy-start(bf16[128,512]{1,0:T(8,128)(2,1)} %param.16) | copy-start | bytes 393220
  3.3 21.2 %collective-permute-start = (bf16[10,32,128]{2,1,0:T(8,128)(2,1)S(1)}, bf16[10,32,128]{2,1,0:T(8,128)(2,1)S(1)}, u32[]{:S(2)}, u32[]{:S(2)}) collective-permute-start(bf16[10,32,128]{2,1,0:T(8,128)(2,1)S(1)} %get-tuple-element.116), channel_id=1, source_target_pairs={{0,752},{16,32},{32,16},{48,64},{64,48},{80,96},{96,80},{112,128},... | collective-permute-start | bytes 245768 | tf_op jit(solution)/shard_map/ppermute | solution.py:32
  7.9 16.7 %collective-permute-start.1 = (bf16[10,32,128]{2,1,0:T(8,128)(2,1)S(1)}, bf16[10,32,128]{2,1,0:T(8,128)(2,1)S(1)}, u32[]{:S(2)}, u32[]{:S(2)}) collective-permute-start(bf16[10,32,128]{2,1,0:T(8,128)(2,1)S(1)} %get-tuple-element.117), channel_id=1, source_target_pairs={{0,16},{16,0},{32,48},{48,32},{64,80},{80,64},{96,112},{112,96},{1... | collective-permute-start | bytes 245768 | tf_op jit(solution)/shard_map/ppermute | solution.py:32
  25.4 14.6 %collective-permute-start.2 = (bf16[250,128]{0,1:T(8,128)(2,1)S(1)}, bf16[250,128]{0,1:T(8,128)(2,1)S(1)}, u32[]{:S(2)}, u32[]{:S(2)}) collective-permute-start(bf16[250,128]{0,1:T(8,128)(2,1)S(1)} %get-tuple-element.108), channel_id=1, source_target_pairs={{0,15},{1,2},{2,1},{3,4},{4,3},{5,6},{6,5},{7,8},{8,7},{9,10},{10,... | collective-permute-start | bytes 192008 | tf_op jit(solution)/shard_map/ppermute | solution.py:32
  38.1 5.3 %collective-permute-start.3 = (bf16[250,128]{0,1:T(8,128)(2,1)S(1)}, bf16[250,128]{0,1:T(8,128)(2,1)S(1)}, u32[]{:S(2)}, u32[]{:S(2)}) collective-permute-start(bf16[250,128]{0,1:T(8,128)(2,1)S(1)} %get-tuple-element.109), channel_id=1, source_target_pairs={{0,1},{1,0},{2,3},{3,2},{4,5},{5,4},{6,7},{7,6},{8,9},{9,8},{10,11... | collective-permute-start | bytes 192008 | tf_op jit(solution)/shard_map/ppermute | solution.py:32
  40.1 7.2 %copy-start.6 = (bf16[9,128,128]{2,1,0:T(8,128)(2,1)S(1)}, bf16[9,128,128]{2,1,0:T(8,128)(2,1)}, u32[]{:S(2)}) copy-start(bf16[9,128,128]{2,1,0:T(8,128)(2,1)} %param.18) | copy-start | bytes 884740
  43.9 3.7 %copy-start.12 = (bf16[96,128]{1,0:T(8,128)(2,1)}, bf16[96,128]{1,0:T(8,128)(2,1)S(1)}, u32[]{:S(2)}) copy-start(bf16[96,128]{1,0:T(8,128)(2,1)S(1)} %copy.355) | copy-start | bytes 73732
  44.2 3.8 %copy-start.18 = (f32[24,40]{1,0:T(8,128)}, f32[24,40]{1,0:T(8,128)S(1)}, u32[]{:S(2)}) copy-start(f32[24,40]{1,0:T(8,128)S(1)} %broadcast_multiply_fusion.6) | copy-start | bytes 11524
  44.6 3.4 %copy-start.20 = (f32[24,40]{1,0:T(8,128)}, f32[24,40]{1,0:T(8,128)S(1)}, u32[]{:S(2)}) copy-start(f32[24,40]{1,0:T(8,128)S(1)} %add_rsqrt_fusion.1) | copy-start | bytes 11524
  49.6 1.8 copy-start.19
  53.6 28.0 %copy-start.1 = (bf16[15,64,384]{1,2,0:T(8,128)(2,1)}, bf16[15,64,384]{1,2,0:T(8,128)(2,1)S(1)}, u32[]{:S(2)}) copy-start(bf16[15,64,384]{1,2,0:T(8,128)(2,1)S(1)} %copy.362) | copy-start | bytes 2211844
  65.5 4.5 %copy-start.15 = (bf16[24,40,128]{2,1,0:T(8,128)(2,1)S(1)}, bf16[24,40,128]{2,1,0:T(8,128)(2,1)}, u32[]{:S(2)}) copy-start(bf16[24,40,128]{2,1,0:T(8,128)(2,1)} %get-tuple-element.138) | copy-start | bytes 737284
  65.5 4.5 %copy-start.16 = (bf16[512,128]{1,0:T(8,128)(2,1)S(1)}, bf16[512,128]{1,0:T(8,128)(2,1)}, u32[]{:S(2)}) copy-start(bf16[512,128]{1,0:T(8,128)(2,1)} %param.17) | copy-start | bytes 393220
  73.3 2.7 %copy-start.22 = (bf16[128,128]{1,0:T(8,128)(2,1)S(1)}, bf16[128,128]{1,0:T(8,128)(2,1)}, u32[]{:S(2)}) copy-start(bf16[128,128]{1,0:T(8,128)(2,1)} %param.15) | copy-start | bytes 98308
  76.0 2.3 %copy-start.25 = (f32[15,4,64]{2,1,0:T(4,128)S(1)}, f32[15,4,64]{2,1,0:T(4,128)}, u32[]{:S(2)}) copy-start(f32[15,4,64]{2,1,0:T(4,128)} %copy-done.24) | copy-start | bytes 46084
  78.3 3.3 %copy-start.4 = (f32[15,4,64,64]{2,3,1,0:T(8,128)S(1)}, f32[15,4,64,64]{2,3,1,0:T(8,128)}, u32[]{:S(2)}) copy-start(f32[15,4,64,64]{2,3,1,0:T(8,128)} %get-tuple-element.134) | copy-start | bytes 2949124
  78.3 3.3 %copy-start.11 = (bf16[15,64,4,32]{1,3,2,0:T(8,128)(2,1)S(1)}, bf16[15,64,4,32]{1,3,2,0:T(8,128)(2,1)}, u32[]{:S(2)}) copy-start(bf16[15,64,4,32]{1,3,2,0:T(8,128)(2,1)} %copy.376) | copy-start | bytes 737284
  84.2 1.9 copy-start.9
  84.2 1.9 copy-start.34
  84.2 2.2 %copy-start.33 = (bf16[32]{0:T(256)(128)(2,1)S(1)}, bf16[32]{0:T(256)(128)(2,1)}, u32[]{:S(2)}) copy-start(bf16[32]{0:T(256)(128)(2,1)} %get-tuple-element.128) | copy-start | bytes 196
  84.2 2.4 %copy-start.32 = (bf16[32]{0:T(256)(128)(2,1)S(1)}, bf16[32]{0:T(256)(128)(2,1)}, u32[]{:S(2)}) copy-start(bf16[32]{0:T(256)(128)(2,1)} %get-tuple-element.124) | copy-start | bytes 196
  100.6 2.9 %copy-start.30 = (f32[128]{0:T(128)S(1)}, f32[128]{0:T(128)}, u32[]{:S(2)}) copy-start(f32[128]{0:T(128)} %param.19) | copy-start | bytes 1540
  101.9 2.4 %copy-start.5 = (f32[24,40,128]{2,1,0:T(8,128)S(1)}, f32[24,40,128]{2,1,0:T(8,128)}, u32[]{:S(2)}) copy-start(f32[24,40,128]{2,1,0:T(8,128)} %get-tuple-element.98) | copy-start | bytes 1474564
  101.9 2.4 %copy-start.21 = (f32[16,32]{1,0:T(8,128)S(1)}, f32[16,32]{1,0:T(8,128)}, u32[]{:S(2)}) copy-start(f32[16,32]{1,0:T(8,128)} %slice.404) | copy-start | bytes 6148
  105.2 6.1 %copy-start.7 = (bf16[9,128,128]{2,1,0:T(8,128)(2,1)S(1)}, bf16[9,128,128]{2,1,0:T(8,128)(2,1)}, u32[]{:S(2)}) copy-start(bf16[9,128,128]{2,1,0:T(8,128)(2,1)} %param.18) | copy-start | bytes 884740
  105.2 6.1 %copy-start.28 = (f32[32]{0:T(128)S(1)}, f32[32]{0:T(128)}, u32[]{:S(2)}) copy-start(f32[32]{0:T(128)} %get-tuple-element.127) | copy-start | bytes 388
  106.5 27.1 %copy-start.27 = (f32[32]{0:T(128)S(1)}, f32[32]{0:T(128)}, u32[]{:S(2)}) copy-start(f32[32]{0:T(128)} %get-tuple-element.125) | copy-start | bytes 388
  106.5 17.1 %all-to-all-start = ((bf16[8,384,128]{2,1,0:T(8,128)(2,1)}), bf16[8,384,128]{2,1,0:T(8,128)(2,1)S(1)}, u32[]{:S(2)}, u32[]{:S(2)}) async-start(bf16[8,384,128]{2,1,0:T(8,128)(2,1)} %bitcast.103), calls=%async_computation | async-start | bytes 1572864 | tf_op jit(solution)/shard_map/all_to_all | solution.py:88
  124.4 22.5 %all-to-all-start.1 = ((bf16[96,4,128]{2,1,0:T(4,128)(2,1)}), bf16[96,4,128]{2,1,0:T(4,128)(2,1)S(1)}, u32[]{:S(2)}, u32[]{:S(2)}) async-start(bf16[96,4,128]{2,1,0:T(4,128)(2,1)} %bitcast.104), calls=%async_computation.1 | async-start | bytes 196608 | tf_op jit(solution)/shard_map/all_to_all | solution.py:88
  147.5 12.4 %all-to-all-start.2 = ((bf16[12,4,128]{2,1,0:T(4,128)(2,1)}), bf16[12,4,128]{2,1,0:T(4,128)(2,1)S(1)}, u32[]{:S(2)}, u32[]{:S(2)}) async-start(bf16[12,4,128]{2,1,0:T(4,128)(2,1)} %broadcast_in_dim.41), calls=%async_computation.2 | async-start | bytes 24576 | tf_op jit(solution)/shard_map/all_to_all | solution.py:95
  160.5 10.9 %all-to-all-start.3 = ((bf16[8,48,128]{2,1,0:T(8,128)(2,1)}), bf16[8,48,128]{2,1,0:T(8,128)(2,1)S(1)}, u32[]{:S(2)}, u32[]{:S(2)}) async-start(bf16[8,48,128]{2,1,0:T(8,128)(2,1)} %broadcast_in_dim.43), calls=%async_computation.3 | async-start | bytes 196608 | tf_op jit(solution)/shard_map/all_to_all | solution.py:95
  172.3 20.8 %all-to-all-start.4 = ((bf16[8,384,128]{2,1,0:T(8,128)(2,1)}), bf16[8,384,128]{2,1,0:T(8,128)(2,1)S(1)}, u32[]{:S(2)}, u32[]{:S(2)}) async-start(bf16[8,384,128]{2,1,0:T(8,128)(2,1)} %broadcast_in_dim.45), calls=%async_computation.4 | async-start | bytes 1572864 | tf_op jit(solution)/shard_map/all_to_all | solution.py:95
  (12 other events, 16.6 us)

commit v2 on v1

v2 whole, which is shorter than its diff:
```python
import math

import jax
import jax.numpy as jnp
from jax import lax
from jax.experimental import pallas as pl
from jax.experimental.pallas import tpu as pltpu
from jax.sharding import Mesh
from jax.sharding import PartitionSpec as P

HEADS = 4
WIN = 8
SHIFT = 4
SPAN = 15
HEAD_DIM = 32
AREA = WIN * WIN
WIN_ROWS = 3
WIN_COLS = 5
PAD_COLS = 48
ROWS = 3072
TOKEN_RIM = 4
GRAD_RIM = 5
LABEL_RIM = 8

LON = ("zl", "x", "c")
LAT = ("zh", "y")
NEAR = ("x", "c")
DEEP = ("zl", "zh")

epsilon = 1e-05


def swapped(value, axes, first):
    count = lax.axis_size(axes)
    pairs = []
    for source in range(count):
        up = (source % 2 == 0) == first
        pairs.append((source, (source + 1) % count if up else (source - 1) % count))
    return lax.ppermute(value, axes, pairs)


def traded(to_next, to_prev, axes):
    even = lax.axis_index(axes) % 2 == 0
    later = swapped(jnp.where(even, to_prev, to_next), axes, False)
    near = swapped(jnp.where(even, to_next, to_prev), axes, True)
    return jnp.where(even, later, near), jnp.where(even, near, later)


def lon_halo(tokens, grad_out, ids):
    row_count, col_count, width = tokens.shape
    id_rows = jnp.pad(ids[row_count - LABEL_RIM :].T, ((0, 0), (0, width - LABEL_RIM)))[None]
    to_next = jnp.concatenate([tokens[-TOKEN_RIM:], grad_out[-GRAD_RIM:], id_rows])
    to_prev = jnp.concatenate([tokens[:TOKEN_RIM], grad_out[:GRAD_RIM], jnp.zeros_like(id_rows)])
    before, after = traded(to_next, to_prev, LON)
    split = TOKEN_RIM + GRAD_RIM
    tokens = jnp.concatenate([before[:TOKEN_RIM], tokens, after[:TOKEN_RIM]])
    grad_out = jnp.concatenate([before[TOKEN_RIM:split], grad_out, after[TOKEN_RIM:split]])
    ids = jnp.concatenate([before[split, :, :LABEL_RIM].T, ids])
    return tokens, grad_out, ids


def lat_halo(tokens, grad_out, ids):
    token_rows, col_count, width = tokens.shape
    grad_rows = grad_out.shape[0]
    token_size, grad_size = token_rows * TOKEN_RIM, grad_rows * GRAD_RIM
    id_cols = jnp.pad(ids[:, col_count - LABEL_RIM :], ((0, 0), (0, width - LABEL_RIM)))

    def packed(token_part, grad_part, id_part):
        return jnp.concatenate(
            [token_part.reshape(token_size, width), grad_part.reshape(grad_size, width), id_part]
        )

    def unpacked(message):
        return (
            message[:token_size].reshape(token_rows, TOKEN_RIM, width),
            message[token_size : token_size + grad_size].reshape(grad_rows, GRAD_RIM, width),
            message[token_size + grad_size :, :LABEL_RIM],
        )

    to_next = packed(tokens[:, -TOKEN_RIM:], grad_out[:, -GRAD_RIM:], id_cols)
    to_prev = packed(tokens[:, :TOKEN_RIM], grad_out[:, :GRAD_RIM], jnp.zeros_like(id_cols))
    before, after = traded(to_next, to_prev, LAT)
    tokens_before, grad_before, ids_before = unpacked(before)
    tokens_after, grad_after, _ = unpacked(after)
    return (
        jnp.concatenate([tokens_before, tokens, tokens_after], axis=1),
        jnp.concatenate([grad_before, grad_out, grad_after], axis=1),
        jnp.concatenate([ids_before, ids], axis=1),
    )


def scattered_sum(partial, axes):
    count = lax.axis_size(axes)
    chunks = partial.reshape(count, partial.shape[0] // count, partial.shape[1])
    received = lax.all_to_all(chunks, axes, 0, 0, tiled=True)
    return jnp.sum(received.astype(jnp.float32), axis=0)


def gathered(chunk, axes):
    count = lax.axis_size(axes)
    copies = jnp.broadcast_to(chunk[None], (count,) + chunk.shape)
    return lax.all_to_all(copies, axes, 0, 0, tiled=True).reshape(-1, chunk.shape[1])


def total_over_devices(rows, grad_scale):
    own = scattered_sum(rows, NEAR).astype(jnp.bfloat16)
    own = scattered_sum(own, ("y",)).astype(jnp.bfloat16)
    count = lax.axis_size(DEEP)
    copies = jnp.broadcast_to(own[None], (count,) + own.shape)
    parts = lax.all_to_all(copies, DEEP, 0, 0, tiled=True)
    own = (jnp.sum(parts.astype(jnp.float32), axis=0) * grad_scale).astype(jnp.bfloat16)
    own = gathered(own, ("y",))
    return gathered(own, NEAR).astype(jnp.float32)


def from_blocks(rows, width):
    count = width // 128
    return rows.reshape(count, -1, 128).transpose(1, 0, 2).reshape(-1, width)


def lane_mean(values):
    return jnp.sum(values, axis=-1, keepdims=True) * (1.0 / 128.0)


def layer_norm(values, gain):
    centred = values - lane_mean(values)
    inverse = lax.rsqrt(lane_mean(centred * centred) + epsilon)
    normed = centred * inverse
    return (normed * gain).astype(jnp.bfloat16), normed, inverse


def layer_norm_back(grad_in, normed, inverse, gain):
    scaled = grad_in * gain
    return inverse * (scaled - lane_mean(scaled) - normed * lane_mean(scaled * normed))


def matmul(left, right):
    return jnp.dot(left, right, preferred_element_type=jnp.float32)


def matmul_nt(left, right):
    return lax.dot_general(left, right, (((1,), (1,)), ((), ())), preferred_element_type=jnp.float32)


def matmul_tn(left, right):
    return lax.dot_general(left, right, (((0,), (0,)), ((), ())), preferred_element_type=jnp.float32)


def by_heads(rows, head_masks):
    return jnp.concatenate([rows * mask for mask in head_masks], axis=0)


def own_heads(stacked, head_lanes):
    total = jnp.zeros((AREA, 128), jnp.float32)
    for head in range(HEADS):
        part = stacked[head * AREA : (head + 1) * AREA]
        total = total + jnp.where(head_lanes[head], part, 0.0)
    return total


def table_rows(bias_sum):
    lane = lax.broadcasted_iota(jnp.int32, (WIN, 128), 1)
    pieces = []
    for head in range(HEADS):
        half = head % 2
        tile = bias_sum[:, (head // 2) * 128 : (head // 2 + 1) * 128]
        tile_sum = jnp.zeros((WIN, 128), jnp.float32)
        for row in range(WIN):
            part = jnp.where(lane // AREA == half, tile[row * WIN : (row + 1) * WIN], 0.0)
            steps = (WIN * (WIN - 1 - row) - AREA * half) % 128
            tile_sum = tile_sum + (pltpu.roll(part, steps, 1) if steps else part)
        pieces.append(tile_sum)
    stacked = jnp.concatenate(pieces, axis=0)
    source = lax.broadcasted_iota(jnp.int32, (128, 256), 0)
    target = lax.broadcasted_iota(jnp.int32, (128, 256), 1)
    hit = jnp.logical_and(source // WIN == target // 16, source % WIN == target % 16)
    spread_to = jnp.where(hit, 1.0, 0.0).astype(jnp.bfloat16)
    spread = jnp.zeros((HEADS * WIN, 256), jnp.float32)
    rest = stacked
    for _ in range(3):
        part = rest.astype(jnp.bfloat16)
        spread = spread + matmul(part, spread_to)
        rest = rest - part.astype(jnp.float32)
    place = lax.broadcasted_iota(jnp.int32, (HEADS * WIN, 256), 0) % WIN
    table = jnp.zeros((HEADS * WIN, 256), jnp.float32)
    for row in range(WIN):
        part = jnp.where(place == row, spread, 0.0)
        table = table + (pltpu.roll(part, WIN - 1 - row, 1) if row < WIN - 1 else part)
    rows = []
    for head in range(HEADS):
        head_sum = jnp.sum(table[head * WIN : (head + 1) * WIN], axis=0, keepdims=True)
        rows.extend([head_sum[:, :128], head_sum[:, 128:]])
    return rows


def block_kernel(
    tokens_ref,
    gcat_ref,
    grad_own_ref,
    label_col_ref,
    label_row_ref,
    keep_ref,
    bias_ref,
    qkv_ref,
    proj_ref,
    up_ref,
    down_ref,
    conv_ref,
    conv_back_ref,
    gain_one_ref,
    gain_two_ref,
    down_out_ref,
    grad_tokens_ref,
    rows_ref,
    block_out_s,
    grad_tokens_s,
    ln_one_s,
    ln_two_s,
    hidden_s,
    grad_pre_s,
    grad_block_s,
    mixed_s,
    grad_att_s,
    grad_qkv_s,
):
    gain_one, gain_two = gain_one_ref[...], gain_two_ref[...]
    lane = lax.broadcasted_iota(jnp.int32, (AREA, 128), 1)
    head_lanes = [lane // HEAD_DIM == head for head in range(HEADS)]
    head_masks = [jnp.where(hit, 1.0, 0.0).astype(jnp.bfloat16) for hit in head_lanes]
    biases = bias_ref[...]
    score_scale = HEAD_DIM ** (-0.5)
    length = WIN_COLS * AREA
    bias_sum = jnp.zeros((AREA, HEADS * AREA), jnp.float32)
    gain_one_sum = jnp.zeros((1, 128), jnp.float32)
    gain_two_sum = jnp.zeros((1, 128), jnp.float32)
    for chunk in range(WIN_ROWS):
        start = chunk * length
        source = tokens_ref[start : start + length, :].astype(jnp.float32)
        ln_one, normed_one, inverse_one = layer_norm(source, gain_one)
        qkv_all = matmul(ln_one, qkv_ref[...]).astype(jnp.bfloat16)
        saved, mixed_parts = [], []
        for win in range(WIN_COLS):
            part = qkv_all[win * AREA : (win + 1) * AREA]
            query, key, value = part[:, :128], part[:, 128:256], part[:, 256:]
            query_heads = by_heads(query, head_masks)
            place = (chunk * WIN_COLS + win) * AREA
            column = label_col_ref[place : place + AREA, :].astype(jnp.float32)
            allowed = jnp.concatenate([column, column], axis=1) == label_row_ref[chunk * WIN_COLS + win]
            scores = matmul_nt(key, query_heads) * score_scale + biases
            scores = jnp.where(allowed, scores, -1e30)
            raised = jnp.exp(scores - jnp.max(scores, axis=0, keepdims=True))
            probabilities = raised * (1.0 / jnp.sum(raised, axis=0, keepdims=True))
            weights = probabilities.astype(jnp.bfloat16)
            mixed_parts.append(own_heads(matmul_tn(weights, value), head_lanes).astype(jnp.bfloat16))
            saved.append((query_heads, key, value, probabilities, weights))
        mixed = jnp.concatenate(mixed_parts, axis=0)
        projected = matmul(mixed, proj_ref[...]).astype(jnp.bfloat16)
        middle = source + projected.astype(jnp.float32)
        ln_two, normed_two, inverse_two = layer_norm(middle, gain_two)
        pre_act = matmul(ln_two, up_ref[...])
        cumulative = 0.5 * (1.0 + lax.erf(pre_act * 0.7071067811865476))
        hidden = (pre_act * cumulative).astype(jnp.bfloat16)
        slope = cumulative + pre_act * (jnp.exp(-0.5 * pre_act * pre_act) * 0.3989422804014327)
        block_out = (middle + matmul(hidden, down_ref[...])).astype(jnp.bfloat16).astype(jnp.float32)
        top = chunk * WIN
        for win in range(WIN_COLS):
            piece = block_out[win * AREA : (win + 1) * AREA].reshape(WIN, WIN, 128)
            block_out_s[top : top + WIN, win * WIN : (win + 1) * WIN, :] = piece

        grad_grid = jnp.zeros((WIN * PAD_COLS, 128), jnp.float32)
        for tap in range(3):
            first = (top + 2 - tap) * PAD_COLS
            grad_grid = grad_grid + matmul(
                gcat_ref[first : first + WIN * PAD_COLS, :], conv_back_ref[tap]
            )
        grad_grid = grad_grid.reshape(WIN, PAD_COLS, 128)
        grad_block = jnp.concatenate(
            [
                grad_grid[:, win * WIN : (win + 1) * WIN, :].reshape(AREA, 128)
                for win in range(WIN_COLS)
            ],
            axis=0,
        )
        grad_block_b = grad_block.astype(jnp.bfloat16)
        grad_hidden = matmul_nt(grad_block_b, down_ref[...])
        grad_pre = (grad_hidden * slope).astype(jnp.bfloat16)
        grad_ln_two = matmul_nt(grad_pre, up_ref[...])
        grad_middle = grad_block + layer_norm_back(grad_ln_two, normed_two, inverse_two, gain_two)
        grad_att = grad_middle.astype(jnp.bfloat16)
        grad_mixed = matmul_nt(grad_att, proj_ref[...]).astype(jnp.bfloat16)
        grad_parts = []
        for win in range(WIN_COLS):
            query_heads, key, value, probabilities, weights = saved[win]
            grad_heads = by_heads(grad_mixed[win * AREA : (win + 1) * AREA], head_masks)
            grad_probs = matmul_nt(value, grad_heads)
            grad_value = matmul(weights, grad_heads)
            centre = jnp.sum(probabilities * grad_probs, axis=0, keepdims=True)
            grad_scores = probabilities * (grad_probs - centre)
            if chunk and win:
                bias_sum = bias_sum + grad_scores
            grad_scores_b = grad_scores.astype(jnp.bfloat16)
            grad_key = matmul(grad_scores_b, query_heads) * score_scale
            grad_query = own_heads(matmul_tn(grad_scores_b, key), head_lanes) * score_scale
            grad_parts.append(
                jnp.concatenate([grad_query, grad_key, grad_value], axis=1).astype(jnp.bfloat16)
            )
        grad_qkv = jnp.concatenate(grad_parts, axis=0)
        grad_ln_one = matmul_nt(grad_qkv, qkv_ref[...])
        grad_tokens = grad_middle + layer_norm_back(grad_ln_one, normed_one, inverse_one, gain_one)
        for win in range(WIN_COLS):
            piece = grad_tokens[win * AREA : (win + 1) * AREA].reshape(WIN, WIN, 128)
            grad_tokens_s[top : top + WIN, win * WIN : (win + 1) * WIN, :] = piece
        if chunk:
            gain_one_sum = gain_one_sum + jnp.sum(
                (grad_ln_one * normed_one)[AREA:], axis=0, keepdims=True
            )
            gain_two_sum = gain_two_sum + jnp.sum(
                (grad_ln_two * normed_two)[AREA:], axis=0, keepdims=True
            )
            kept = slice((chunk - 1) * (length - AREA), chunk * (length - AREA))
            ln_one_s[kept, :] = ln_one[AREA:]
            ln_two_s[kept, :] = ln_two[AREA:]
            hidden_s[kept, :] = hidden[AREA:]
            grad_pre_s[kept, :] = grad_pre[AREA:]
            grad_block_s[kept, :] = grad_block_b[AREA:]
            mixed_s[kept, :] = mixed[AREA:]
            grad_att_s[kept, :] = grad_att[AREA:]
            grad_qkv_s[kept, :] = grad_qkv[AREA:]

    own_rows, own_cols = 16, 32
    shifted = []
    for tap in range(3):
        piece = block_out_s[3 : own_rows + 5, 3 + tap : 3 + tap + own_cols, :]
        if tap != 1:
            piece = piece * keep_ref[tap // 2][None]
        shifted.append(piece.reshape((own_rows + 2) * own_cols, 128).astype(jnp.bfloat16))
    patches = jnp.concatenate(shifted, axis=1)
    count = own_rows * own_cols
    downscaled = jnp.zeros((count, 128), jnp.float32)
    grad_own = grad_own_ref[...]
    for tap in range(3):
        rows = patches[tap * own_cols : tap * own_cols + count]
        downscaled = downscaled + matmul(rows, conv_ref[tap])
        rows_ref[tap * 384 : (tap + 1) * 384, :] = matmul_tn(rows, grad_own).astype(jnp.bfloat16)
    down_out_ref[...] = downscaled.astype(jnp.bfloat16)
    grad_tokens_ref[...] = (
        grad_tokens_s[4 : own_rows + 4, 4 : own_cols + 4, :].reshape(count, 128).astype(jnp.bfloat16)
    )
    place = 1152
    for left, right, flipped in (
        (ln_one_s, grad_qkv_s, False),
        (mixed_s, grad_att_s, False),
        (ln_two_s, grad_pre_s, False),
        (hidden_s, grad_block_s, True),
    ):
        product = matmul_tn(left[...], right[...]).astype(jnp.bfloat16)
        if flipped:
            rows_ref[place : place + product.shape[0], :] = product
            place = place + product.shape[0]
        else:
            for tile in range(product.shape[1] // 128):
                rows_ref[place : place + 128, :] = product[:, tile * 128 : (tile + 1) * 128]
                place = place + 128
    small = [gain_one_sum, gain_two_sum] + table_rows(bias_sum)
    small.append(jnp.zeros((16 - len(small), 128), jnp.float32))
    rows_ref[place : place + 16, :] = jnp.concatenate(small, axis=0).astype(jnp.bfloat16)
    place = place + 16
    rows_ref[place:, :] = jnp.zeros((ROWS - place, 128), jnp.bfloat16)


def bias_matrix(position_bias):
    places = jnp.arange(WIN, dtype=jnp.int32)
    distance = places[:, None] - places[None, :] + WIN - 1
    onehot = (distance[:, :, None] == jnp.arange(SPAN, dtype=jnp.int32)).astype(jnp.float32)
    spread = jnp.einsum(
        "hmn,acm,bdn->cdhab", position_bias, onehot, onehot, precision=lax.Precision.HIGHEST
    )
    return spread.reshape(AREA, HEADS * AREA)


def to_windows(grid):
    height, width = grid.shape[0] // WIN, grid.shape[1] // WIN
    split = grid.reshape((height, WIN, width, WIN) + grid.shape[2:])
    return split.swapaxes(1, 2).reshape((height * width, AREA) + grid.shape[2:])


def local_work(
    tokens_ext,
    grad_ext,
    grad_out,
    labels,
    positions,
    lat_total,
    qkv_weight,
    proj_weight,
    up_weight,
    down_weight,
    conv_weight,
    gain_one,
    gain_two,
    position_bias,
):
    row_count, col_count, width = tokens_ext.shape
    keep_before = (positions != 0).astype(jnp.float32)
    keep_after = (positions != lat_total - 1).astype(jnp.float32)
    own = slice(TOKEN_RIM, col_count - TOKEN_RIM)
    keep = jnp.stack([keep_before[own], keep_after[own]])
    keep = jnp.broadcast_to(keep[:, :, None], keep.shape + (width,))
    after = grad_ext[:, 2:] * keep_after.astype(jnp.bfloat16)[None, :, None]
    before = grad_ext[:, :-2] * keep_before.astype(jnp.bfloat16)[None, :, None]
    gcat = jnp.concatenate([after, grad_ext[:, 1:-1], before], axis=2)
    gcat = jnp.pad(gcat, ((0, 0), (0, PAD_COLS - col_count), (0, 0))).reshape(-1, 3 * width)
    tokens_win = to_windows(tokens_ext).reshape(-1, width)
    label_win = to_windows(labels)
    label_row = jnp.tile(label_win, (1, HEADS))[:, None, :]
    label_col = jnp.broadcast_to(
        label_win.astype(jnp.bfloat16).reshape(-1, 1), (row_count * col_count, width)
    )
    conv_fwd = conv_weight.reshape(3, 3 * width, width)
    conv_back = conv_weight.reshape(3, 3, width, width).swapaxes(2, 3).reshape(3, 3 * width, width)
    count = grad_out.shape[0] * grad_out.shape[1]
    kept = WIN * WIN * (WIN_ROWS - 1) * (WIN_COLS - 1)
    bf16 = lambda *shape: pltpu.VMEM(shape, jnp.bfloat16)
    grid_shape = (row_count, col_count, width)
    downscaled, grad_tokens, rows = pl.pallas_call(
        block_kernel,
        out_shape=(
            jax.ShapeDtypeStruct((count, width), jnp.bfloat16),
            jax.ShapeDtypeStruct((count, width), jnp.bfloat16),
            jax.ShapeDtypeStruct((ROWS, width), jnp.bfloat16),
        ),
        in_specs=[pl.BlockSpec(memory_space=pltpu.VMEM)] * 15,
        out_specs=[pl.BlockSpec(memory_space=pltpu.VMEM)] * 3,
        scratch_shapes=[
            pltpu.VMEM(grid_shape, jnp.float32),
            pltpu.VMEM(grid_shape, jnp.float32),
            bf16(kept, width),
            bf16(kept, width),
            bf16(kept, 4 * width),
            bf16(kept, 4 * width),
            bf16(kept, width),
            bf16(kept, width),
            bf16(kept, width),
            bf16(kept, 3 * width),
        ],
        compiler_params=pltpu.CompilerParams(vmem_limit_bytes=48 * 1024 * 1024),
        cost_estimate=pl.CostEstimate(
            flops=3_000_000_000, bytes_accessed=8_000_000, transcendentals=2_000_000
        ),
    )(
        tokens_win,
        gcat,
        grad_out.reshape(count, width),
        label_col,
        label_row,
        keep,
        bias_matrix(position_bias),
        qkv_weight,
        proj_weight,
        up_weight,
        down_weight,
        conv_fwd,
        conv_back,
        gain_one[None],
        gain_two[None],
    )
    return downscaled.reshape(grad_out.shape), grad_tokens.reshape(grad_out.shape), rows


def per_device(
    tokens,
    grad_out,
    window_ids,
    qkv_weight,
    proj_weight,
    up_weight,
    down_weight,
    conv_weight,
    gain_one,
    gain_two,
    position_bias,
):
    row_count, col_count, width = tokens.shape
    lat_total = col_count * lax.axis_size(LAT)
    tokens_all = row_count * lat_total * lax.axis_size(LON)
    ids = window_ids.astype(jnp.bfloat16)
    tokens_ext, grad_ext, ids_ext = lat_halo(*lon_halo(tokens, grad_out, ids))
    first_col = lax.axis_index(LAT) * col_count
    steps = jnp.arange(col_count + 2 * TOKEN_RIM, dtype=jnp.int32)
    positions = jnp.remainder(first_col + steps - TOKEN_RIM, lat_total)
    shifted_cols = jnp.remainder(first_col + steps - LABEL_RIM, lat_total)
    seam_flag = (shifted_cols >= lat_total - SHIFT).astype(jnp.float32)
    labels = ids_ext.astype(jnp.float32) * 2.0 + seam_flag[None, :]
    downscaled, grad_tokens, rows = local_work(
        tokens_ext,
        grad_ext,
        grad_out,
        labels,
        positions,
        lat_total,
        qkv_weight,
        proj_weight,
        up_weight,
        down_weight,
        conv_weight,
        gain_one,
        gain_two,
        position_bias,
    )
    totals = total_over_devices(rows, 1.0 / math.sqrt(tokens_all))
    sizes = (9 * width, 3 * width, width, 4 * width, 4 * width, 1, 1, 8)
    pieces = []
    offset = 0
    for size in sizes:
        pieces.append(totals[offset : offset + size])
        offset = offset + size
    return (
        downscaled,
        grad_tokens,
        from_blocks(pieces[1], 3 * width),
        pieces[2],
        from_blocks(pieces[3], 4 * width),
        pieces[4],
        pieces[0].reshape(9, width, width),
        pieces[5][0],
        pieces[6][0],
        pieces[7].reshape(HEADS, 16, 16)[:, :SPAN, :SPAN],
    )


def solution(mesh):
    lon_count, lat_count = mesh.devices.shape
    near = math.gcd(lon_count, 8)
    parts = (lon_count // near, near // 2, 2, 2, lat_count // 2)
    fine = Mesh(mesh.devices.reshape(parts), ("zl", "x", "c", "zh", "y"))
    grid = P(LON, LAT, None)
    return jax.shard_map(
        per_device,
        mesh=fine,
        in_specs=(grid, grid, P(LON, LAT)) + (P(),) * 8,
        out_specs=(grid, grid) + (P(),) * 8,
        check_vma=False,
    )
```

time: 200 us -> 137 us (0.69)
  blocking collectives: 0 us -> 72.3 us
  waiting for transfers between devices: 55.1 us -> 3.18 us
  matrix products: 31.5 us -> 0.9 us
  starting transfers between devices: 61.8 us -> 32.5 us
  local copies, waits for them, and re-layouts: 32.7 us -> 11.1 us
  other arithmetic: 15.5 us -> 3.14 us
  Pallas kernels: 0 us -> 11.7 us
    all_to_all x0 -> x5, blocking collectives: none -> 72.3 us  [the longest x2 29.6 us: gathered(): lax.all_to_all(copies, axes, 0, 0, tiled=True).reshape(-1, chunk.shape[1])]
    all_to_all x5 -> x0, waiting for transfers between devices: 51.8 us -> none  [the longest x3 27.1 us: gathered(): lax.all_to_all(copies, axes, 0, 0, tiled=True).reshape(-1, chunk.shape[1])]
    all_to_all x5 -> x0, starting transfers between devices: 29.4 us -> none  [the longest x3 15.4 us: gathered(): lax.all_to_all(copies, axes, 0, 0, tiled=True).reshape(-1, chunk.shape[1])]
    dot_general x48 -> x2, matrix products: 28.2 us -> 0.9 us  [bias_matrix(): jnp.einsum('hmn,acm,bdn->cdhab', position_bias, onehot, onehot, precision...]
    pallas_call x0 -> x1, Pallas kernels: none -> 11.7 us  [local_work(): pl.pallas_call(block_kernel, out_shape=(jax.ShapeDtypeStruct((count, widt...]
    convert_element_type x3 -> x1, local copies, waits for them, and re-layouts: 6.31 us -> 0.1 us  [local_work(): label_win.astype(jnp.bfloat16).reshape(-1, 1)]
    convert_element_type x8 -> x6, other arithmetic: 6.29 us -> 0.17 us  [the longest x1 0.1 us: total_over_devices(): return gathered(own, NEAR).astype(jnp.float32)]
    another operation x6 -> x5, local copies, waits for them, and re-layouts: 6.41 us -> 0.33 us  [the longest x3 0.18 us: local_work(): label_row = jnp.tile(label_win, (1, HEADS))[:, None, :]]
  transfers between devices with their start and end apart: 9 -> 4, of which waited for: 6 -> 1; matrix products, arithmetic and copies ran while one was open for 3% -> 2% of each run, Pallas kernels for 0% -> 0%
where the time goes in v2:
time: 137 us; the launch traced here: 136 us
  blocking collectives  72.3 us (53%)
  starting transfers between devices  32.5 us (24%)
  Pallas kernels  11.7 us (9%)
  local copies, waits for them, and re-layouts  11.1 us (8%)
  waiting for transfers between devices  3.18 us (2%)
  other arithmetic  3.14 us (2%)
    ppermute x4, starting transfers between devices, swapped(): return lax.ppermute(value, axes, pairs)  32.5 us
    all_to_all x2, blocking collectives, gathered(): lax.all_to_all(copies, axes, 0, 0, tiled=True).reshape(-1, chunk.shape[1])  29.6 us
    all_to_all x2, blocking collectives, scattered_sum(): received = lax.all_to_all(chunks, axes, 0, 0, tiled=True)  26.9 us
    all_to_all x1, blocking collectives, total_over_devices(): parts = lax.all_to_all(copies, DEEP, 0, 0, tiled=True)  15.8 us
    pallas_call x1, Pallas kernels, local_work(): pl.pallas_call(block_kernel, out_shape=(jax.ShapeDtypeStruct((count, widt...  11.7 us
    ppermute x4, waiting for transfers between devices, swapped(): return lax.ppermute(value, axes, pairs)  3.18 us
  transfers between devices with their start and end apart: 4, of which 1 were waited for; matrix products, arithmetic and copies ran while one was open for 2% of the time, Pallas kernels for 0%

profile of v2, /device:TPU:1, one launch (start us, length us, event | category | flops | bytes accessed | tf_op | source)
XLA Modules:
  0.0 136.0 jit_solution(15671301633129049364)
XLA Ops:
  0.7 0.8 fusion.27
  1.5 0.8 fusion.26
  2.4 0.2 copy.111
  2.7 0.7 convert_element_type.80
  3.4 0.2 copy.133
  3.8 4.5 %collective-permute-start = (bf16[10,32,128]{1,2,0:T(8,128)(2,1)S(1)}, bf16[10,32,128]{1,2,0:T(8,128)(2,1)S(1)}, u32[]{:S(2)}, u32[]{:S(2)}) collective-permute-start(bf16[10,32,128]{1,2,0:T(8,128)(2,1)S(1)} %get-tuple-element.74), channel_id=1, source_target_pairs={{0,752},{16,32},{32,16},{48,64},{64,48},{80,96},{96,80},{112,128},... | collective-permute-start | bytes 245768 | tf_op jit(solution)/shard_map/ppermute | solution.py:39
  8.3 13.3 %collective-permute-start.1 = (bf16[10,32,128]{1,2,0:T(8,128)(2,1)S(1)}, bf16[10,32,128]{1,2,0:T(8,128)(2,1)}, u32[]{:S(2)}, u32[]{:S(2)}) collective-permute-start(bf16[10,32,128]{1,2,0:T(8,128)(2,1)S(1)} %get-tuple-element.75), channel_id=1, source_target_pairs={{0,16},{16,0},{32,48},{48,32},{64,80},{80,64},{96,112},{112,96},{1... | collective-permute-start | bytes 245768 | tf_op jit(solution)/shard_map/ppermute | solution.py:39
  21.9 0.2 convolution_bitcast_fusion.1
  22.1 0.7 convolution_bitcast_fusion
  22.8 0.9 copy.121
  23.7 0.5 reshape.198.bias_ref
  24.3 0.2 copy.122
  24.5 1.1 broadcast_select_fusion.1
  26.5 12.7 %collective-permute-start.2 = (bf16[250,128]{1,0:T(8,128)(2,1)S(1)}, bf16[250,128]{1,0:T(8,128)(2,1)S(1)}, u32[]{:S(2)}, u32[]{:S(2)}) collective-permute-start(bf16[250,128]{1,0:T(8,128)(2,1)S(1)} %get-tuple-element.89), channel_id=1, source_target_pairs={{0,15},{1,2},{2,1},{3,4},{4,3},{5,6},{6,5},{7,8},{8,7},{9,10},{10,... | collective-permute-start | bytes 192008 | tf_op jit(solution)/shard_map/ppermute | solution.py:39
  39.2 2.1 %collective-permute-start.3 = (bf16[250,128]{1,0:T(8,128)(2,1)S(1)}, bf16[250,128]{1,0:T(8,128)(2,1)S(1)}, u32[]{:S(2)}, u32[]{:S(2)}) collective-permute-start(bf16[250,128]{1,0:T(8,128)(2,1)S(1)} %get-tuple-element.90), channel_id=1, source_target_pairs={{0,1},{1,0},{2,3},{3,2},{4,5},{5,4},{6,7},{7,6},{8,9},{9,8},{10,11... | collective-permute-start | bytes 192008 | tf_op jit(solution)/shard_map/ppermute | solution.py:39
  41.3 3.2 %collective-permute-done.3 = bf16[250,128]{1,0:T(8,128)(2,1)S(1)} collective-permute-done((bf16[250,128]{1,0:T(8,128)(2,1)S(1)}, bf16[250,128]{1,0:T(8,128)(2,1)S(1)}, u32[]{:S(2)}, u32[]{:S(2)}) %collective-permute-start.3) | collective-permute-done | bytes 64032 | tf_op jit(solution)/shard_map/ppermute | solution.py:39
  45.5 0.1 slice_multiply_fusion.1
  45.7 0.2 broadcast_in_dim.25.label_col_ref
  46.0 0.3 copy-done.2
  46.4 11.7 %shard_map.186 = (bf16[512,128]{1,0:T(8,128)(2,1)}, bf16[512,128]{1,0:T(8,128)(2,1)}, bf16[3072,128]{1,0:T(8,128)(2,1)S(1)}) custom-call(bf16[960,128]{1,0:T(8,128)(2,1)S(1)} %bitcast.88, bf16[1248,384]{1,0:T(8,128)(2,1)S(1)} %bitcast.82, bf16[512,128]{1,0:T(8,128)(2,1)S(1)} %bitcast.83, bf16[960,128]{1,0:T(8,128)(2,1)S(1)} %broadcast_in_dim.25.label_col_ref, ...), custom_call_target="tpu_custom_call" | custom-call | flops 3000000000 | bytes 8000000 | tf_op jit(solution)/shard_map/pallas_call | solution.py:425
  58.1 16.8 %all_to_all.25 = bf16[8,384,128]{2,1,0:T(8,128)(2,1)S(1)} all-to-all(bf16[8,384,128]{2,1,0:T(8,128)(2,1)S(1)} %bitcast.84), channel_id=1, replica_groups=mesh['zl'=6,'x'=4,'c'=2,'zh'=2,'y'=8] {'x','c'}, dimensions={0} | all-to-all | bytes 1572864 | tf_op jit(solution)/shard_map/all_to_all | solution.py:95
  75.0 10.1 %all_to_all.26 = bf16[8,48,128]{2,1,0:T(8,128)(2,1)S(1)} all-to-all(bf16[8,48,128]{2,1,0:T(8,128)(2,1)S(1)} %bitcast.100), channel_id=1, replica_groups=mesh['zl'=6,'x'=4,'c'=2,'zh'=2,'y'=8] {'y'}, dimensions={0} | all-to-all | bytes 196608 | tf_op jit(solution)/shard_map/all_to_all | solution.py:95
  85.2 15.8 %all_to_all.27 = bf16[12,48,128]{2,1,0:T(8,128)(2,1)S(1)} all-to-all(bf16[12,48,128]{2,1,0:T(8,128)(2,1)S(1)} %broadcast_in_dim.29), channel_id=1, replica_groups=mesh['zl'=6,'x'=4,'c'=2,'zh'=2,'y'=8] {'zl','zh'}, dimensions={0} | all-to-all | bytes 294912 | tf_op jit(solution)/shard_map/all_to_all | solution.py:110
  101.0 10.0 %all_to_all.28 = bf16[8,48,128]{2,1,0:T(8,128)(2,1)S(1)} all-to-all(bf16[8,48,128]{2,1,0:T(8,128)(2,1)S(1)} %broadcast_in_dim.60), channel_id=1, replica_groups=mesh['zl'=6,'x'=4,'c'=2,'zh'=2,'y'=8] {'y'}, dimensions={0} | all-to-all | bytes 196608 | tf_op jit(solution)/shard_map/all_to_all | solution.py:102
  111.0 19.7 %all_to_all.29 = bf16[8,384,128]{2,1,0:T(8,128)(2,1)S(1)} all-to-all(bf16[8,384,128]{2,1,0:T(8,128)(2,1)S(1)} %broadcast_in_dim.62), channel_id=1, replica_groups=mesh['zl'=6,'x'=4,'c'=2,'zh'=2,'y'=8] {'x','c'}, dimensions={0} | all-to-all | bytes 1572864 | tf_op jit(solution)/shard_map/all_to_all | solution.py:102
  130.9 0.7 fusion.25
  131.6 0.6 slice.153
  132.2 0.5 slice_bitcast_fusion.2
  132.7 0.7 copy.144
  133.5 0.6 copy.126
  134.3 0.8 copy.125
  135.1 0.9 slice.156
  (84 shorter events, 3.3 us)
Async XLA Ops:
  0.6 21.2 %copy-start.9 = (f32[4,15,15]{2,0,1:T(4,128)S(1)}, f32[4,15,15]{2,0,1:T(4,128)}, u32[]{:S(2)}) copy-start(f32[4,15,15]{2,0,1:T(4,128)} %param.21) | copy-start | bytes 10804
  3.8 20.7 %collective-permute-start = (bf16[10,32,128]{1,2,0:T(8,128)(2,1)S(1)}, bf16[10,32,128]{1,2,0:T(8,128)(2,1)S(1)}, u32[]{:S(2)}, u32[]{:S(2)}) collective-permute-start(bf16[10,32,128]{1,2,0:T(8,128)(2,1)S(1)} %get-tuple-element.74), channel_id=1, source_target_pairs={{0,752},{16,32},{32,16},{48,64},{64,48},{80,96},{96,80},{112,128},... | collective-permute-start | bytes 245768 | tf_op jit(solution)/shard_map/ppermute | solution.py:39
  8.3 16.2 %collective-permute-start.1 = (bf16[10,32,128]{1,2,0:T(8,128)(2,1)S(1)}, bf16[10,32,128]{1,2,0:T(8,128)(2,1)}, u32[]{:S(2)}, u32[]{:S(2)}) collective-permute-start(bf16[10,32,128]{1,2,0:T(8,128)(2,1)S(1)} %get-tuple-element.75), channel_id=1, source_target_pairs={{0,16},{16,0},{32,48},{48,32},{64,80},{80,64},{96,112},{112,96},{1... | collective-permute-start | bytes 245768 | tf_op jit(solution)/shard_map/ppermute | solution.py:39
  22.8 1.5 %copy-start.1 = (bf16[9,128,128]{2,1,0:T(8,128)(2,1)S(1)}, bf16[9,128,128]{2,1,0:T(8,128)(2,1)}, u32[]{:S(2)}) copy-start(bf16[9,128,128]{2,1,0:T(8,128)(2,1)} %param.18) | copy-start | bytes 884740
  24.5 1.7 %copy-start = (bf16[16,32,128]{2,1,0:T(8,128)(2,1)S(1)}, bf16[16,32,128]{2,1,0:T(8,128)(2,1)}, u32[]{:S(2)}) copy-start(bf16[16,32,128]{2,1,0:T(8,128)(2,1)} %param.12) | copy-start | bytes 393220
  24.5 1.8 %copy-start.8 = (bf16[16,32,128]{2,1,0:T(8,128)(2,1)S(1)}, bf16[16,32,128]{2,1,0:T(8,128)(2,1)}, u32[]{:S(2)}) copy-start(bf16[16,32,128]{2,1,0:T(8,128)(2,1)} %param.11) | copy-start | bytes 393220
  26.5 14.8 %collective-permute-start.2 = (bf16[250,128]{1,0:T(8,128)(2,1)S(1)}, bf16[250,128]{1,0:T(8,128)(2,1)S(1)}, u32[]{:S(2)}, u32[]{:S(2)}) collective-permute-start(bf16[250,128]{1,0:T(8,128)(2,1)S(1)} %get-tuple-element.89), channel_id=1, source_target_pairs={{0,15},{1,2},{2,1},{3,4},{4,3},{5,6},{6,5},{7,8},{8,7},{9,10},{10,... | collective-permute-start | bytes 192008 | tf_op jit(solution)/shard_map/ppermute | solution.py:39
  39.2 5.3 %collective-permute-start.3 = (bf16[250,128]{1,0:T(8,128)(2,1)S(1)}, bf16[250,128]{1,0:T(8,128)(2,1)S(1)}, u32[]{:S(2)}, u32[]{:S(2)}) collective-permute-start(bf16[250,128]{1,0:T(8,128)(2,1)S(1)} %get-tuple-element.90), channel_id=1, source_target_pairs={{0,1},{1,0},{2,3},{3,2},{4,5},{5,4},{6,7},{7,6},{8,9},{9,8},{10,11... | collective-permute-start | bytes 192008 | tf_op jit(solution)/shard_map/ppermute | solution.py:39
  45.4 0.9 copy-start.2
  45.4 1.0 copy-start.3
  45.4 1.0 copy-start.4
  45.4 1.0 copy-start.5
  45.4 1.0 copy-start.6
  45.5 1.0 copy-start.7

commit v3 on v2

v3 whole, which is shorter than its diff:
```python
import functools
import math

import jax
import jax.numpy as jnp
from jax import lax
from jax.experimental import pallas as pl
from jax.experimental.pallas import tpu as pltpu
from jax.sharding import Mesh
from jax.sharding import PartitionSpec as P

HEADS = 4
WIN = 8
SHIFT = 4
SPAN = 15
HEAD_DIM = 32
AREA = WIN * WIN
WIN_ROWS = 3
WIN_COLS = 5
PAD_COLS = 48
ROWS = 3072
TOKEN_RIM = 4
GRAD_RIM = 5
LABEL_RIM = 8

LON = ("zl", "x", "c")
LAT = ("zh", "y")
DEEP = ("zl", "zh")
TOKEN_ROWS = 24
GRAD_ROWS = 26
MESSAGE = (TOKEN_ROWS + GRAD_ROWS) * WIN + 32

epsilon = 1e-05


def swapped(value, axes, first):
    count = lax.axis_size(axes)
    pairs = []
    for source in range(count):
        up = (source % 2 == 0) == first
        pairs.append((source, (source + 1) % count if up else (source - 1) % count))
    return lax.ppermute(value, axes, pairs)


def place_along(axes):
    place = 0
    for axis in axes:
        place = place * lax.axis_size(axis) + lax.axis_index(axis)
    return place


def either(choice, first, second):
    return jnp.where(choice, jnp.int32(first), jnp.int32(second))


def lon_pack_kernel(tokens_ref, grad_ref, ids_ref, far_ref, near_ref, ids_s):
    even = place_along(LON) % 2 == 0
    rows = tokens_ref.shape[0]
    ids_s[...] = jnp.zeros_like(ids_s)
    ids_s[0:LABEL_RIM, 0 : ids_ref.shape[1]] = ids_ref[rows - LABEL_RIM :, :].astype(jnp.float32)
    ids = ids_s[...].astype(jnp.bfloat16)
    for ref, upper in ((near_ref, even), (far_ref, jnp.logical_not(even))):
        ref[0:TOKEN_RIM] = tokens_ref[pl.ds(either(upper, rows - TOKEN_RIM, 0), TOKEN_RIM)]
        ref[TOKEN_RIM : TOKEN_RIM + GRAD_RIM] = grad_ref[
            pl.ds(either(upper, rows - GRAD_RIM, 0), GRAD_RIM)
        ]
        ref[TOKEN_RIM + GRAD_RIM] = ids


def lon_labels(ids_ref, lon_near_ref, lon_far_ref, even, ids_s):
    row = TOKEN_RIM + GRAD_RIM
    before = jnp.where(
        even, lon_far_ref[row].astype(jnp.float32), lon_near_ref[row].astype(jnp.float32)
    )
    ids_s[...] = jnp.zeros_like(ids_s)
    ids_s[0:LABEL_RIM, :] = before[0:LABEL_RIM]
    ids_s[LABEL_RIM : LABEL_RIM + ids_ref.shape[0], 0 : ids_ref.shape[1]] = ids_ref[...].astype(
        jnp.float32
    )


def lat_pack_kernel(
    tokens_ref,
    grad_ref,
    ids_ref,
    lon_near_ref,
    lon_far_ref,
    far_ref,
    near_ref,
    tokens_s,
    grad_s,
    ids_s,
):
    lon_even = place_along(LON) % 2 == 0
    lat_even = place_along(LAT) % 2 == 0
    cols = tokens_ref.shape[1]

    def edges(scratch, row, values):
        values = values.astype(jnp.float32)
        count = values.shape[0]
        scratch[0, pl.ds(row, count)] = values[:, 0:WIN]
        scratch[1, pl.ds(row, count)] = values[:, cols - WIN :]

    edges(tokens_s, TOKEN_RIM, tokens_ref[...])
    edges(grad_s, GRAD_RIM, grad_ref[...])
    split = TOKEN_RIM + GRAD_RIM
    for ref, below in ((lon_near_ref, lon_even), (lon_far_ref, jnp.logical_not(lon_even))):
        edges(tokens_s, either(below, TOKEN_ROWS - TOKEN_RIM, 0), ref[0:TOKEN_RIM])
        edges(grad_s, either(below, GRAD_ROWS - GRAD_RIM, 0), ref[TOKEN_RIM:split])
    lon_labels(ids_ref, lon_near_ref, lon_far_ref, lon_even, ids_s)
    ids = ids_s[...].astype(jnp.bfloat16)
    first, second = TOKEN_ROWS * WIN, (TOKEN_ROWS + GRAD_ROWS) * WIN
    for ref, side in ((near_ref, either(lat_even, 1, 0)), (far_ref, either(lat_even, 0, 1))):
        ref[0:first, :] = tokens_s[side].reshape(first, 128).astype(jnp.bfloat16)
        ref[first:second, :] = grad_s[side].reshape(second - first, 128).astype(jnp.bfloat16)
        ref[second:, :] = ids


def assembled(
    tokens_ref,
    grad_ref,
    ids_ref,
    lon_near_ref,
    lon_far_ref,
    lat_near_ref,
    lat_far_ref,
    tokens_s,
    grad_s,
    ids_s,
    first_col,
    lat_total,
):
    lon_even = place_along(LON) % 2 == 0
    lat_even = place_along(LAT) % 2 == 0
    rows, cols = tokens_ref.shape[0], tokens_ref.shape[1]
    middle = slice(WIN, WIN + cols)
    tokens_s[TOKEN_RIM : TOKEN_RIM + rows, middle, :] = tokens_ref[...].astype(jnp.float32)
    grad_s[GRAD_RIM : GRAD_RIM + rows, middle, :] = grad_ref[...].astype(jnp.float32)
    split = TOKEN_RIM + GRAD_RIM
    for ref, below in ((lon_near_ref, lon_even), (lon_far_ref, jnp.logical_not(lon_even))):
        row = either(below, TOKEN_ROWS - TOKEN_RIM, 0)
        tokens_s[pl.ds(row, TOKEN_RIM), middle, :] = ref[0:TOKEN_RIM].astype(jnp.float32)
        row = either(below, GRAD_ROWS - GRAD_RIM, 0)
        grad_s[pl.ds(row, GRAD_RIM), middle, :] = ref[TOKEN_RIM:split].astype(jnp.float32)
    first, second = TOKEN_ROWS * WIN, (TOKEN_ROWS + GRAD_ROWS) * WIN
    for ref, below in ((lat_near_ref, lat_even), (lat_far_ref, jnp.logical_not(lat_even))):
        side = pl.ds(pl.multiple_of(either(below, WIN + cols, 0), WIN), WIN)
        tokens_s[:, side, :] = ref[0:first].astype(jnp.float32).reshape(TOKEN_ROWS, WIN, 128)
        grad_s[:, side, :] = ref[first:second].astype(jnp.float32).reshape(GRAD_ROWS, WIN, 128)
    lon_labels(ids_ref, lon_near_ref, lon_far_ref, lon_even, ids_s)
    before = jnp.where(
        lat_even, lat_far_ref[second:].astype(jnp.float32), lat_near_ref[second:].astype(jnp.float32)
    )
    lane = lax.broadcasted_iota(jnp.int32, ids_s.shape, 1)
    own = pltpu.roll(ids_s[...], LABEL_RIM, 1)
    ids = jnp.where(lane < LABEL_RIM, pltpu.roll(before, 128 - (cols - LABEL_RIM), 1), own)
    shifted = first_col + lane - LABEL_RIM
    shifted = jnp.where(shifted < 0, shifted + lat_total, shifted)
    return ids * 2.0 + jnp.where(shifted >= lat_total - SHIFT, 1.0, 0.0)


def bias_rows(table_ref):
    lane = lax.broadcasted_iota(jnp.int32, (WIN, 128), 1)
    source = lax.broadcasted_iota(jnp.int32, (256, 128), 0)
    target = lax.broadcasted_iota(jnp.int32, (256, 128), 1)
    hit = jnp.logical_and(source // 16 == target // WIN, source % 16 == target % WIN)
    narrow = jnp.where(hit, 1.0, 0.0).astype(jnp.bfloat16)
    pieces = []
    for head in range(HEADS):
        table = jnp.broadcast_to(table_ref[head : head + 1, :], (WIN, 256))
        place = lax.broadcasted_iota(jnp.int32, (WIN, 256), 0)
        moved = jnp.zeros((WIN, 256), jnp.float32)
        for row in range(WIN):
            steps = (256 - (WIN - 1 - row)) % 256
            part = pltpu.roll(table, steps, 1) if steps else table
            moved = jnp.where(place == row, part, moved)
        pieces.append(moved)
    rest = jnp.concatenate(pieces, axis=0)
    packed = jnp.zeros((HEADS * WIN, 128), jnp.float32)
    for _ in range(3):
        part = rest.astype(jnp.bfloat16)
        packed = packed + matmul(part, narrow)
        rest = rest - part.astype(jnp.float32)
    rows = []
    for row in range(WIN):
        tiles = []
        for pair in range(HEADS // 2):
            halves = []
            for half in range(2):
                head = 2 * pair + half
                steps = (AREA * half - WIN * (WIN - 1 - row)) % 128
                part = packed[head * WIN : (head + 1) * WIN]
                halves.append(pltpu.roll(part, steps, 1) if steps else part)
            tiles.append(jnp.where(lane < AREA, halves[0], halves[1]))
        rows.append(jnp.concatenate(tiles, axis=1))
    return jnp.concatenate(rows, axis=0)


def scattered_sum(partial, axes):
    count = lax.axis_size(axes)
    chunks = partial.reshape(count, partial.shape[0] // count, partial.shape[1])
    received = lax.all_to_all(chunks, axes, 0, 0, tiled=True)
    return jnp.sum(received.astype(jnp.float32), axis=0)


def spread(chunk, axes):
    count = lax.axis_size(axes)
    copies = jnp.broadcast_to(chunk[None], (count,) + chunk.shape)
    return lax.all_to_all(copies, axes, 0, 0, tiled=True)


def total_over_devices(kept, sent, grad_scale):
    cores = [(0, 1), (1, 0)]
    other = lax.ppermute(sent, "c", cores)
    own = (kept.astype(jnp.float32) + other.astype(jnp.float32)).astype(jnp.bfloat16)
    own = scattered_sum(own, ("x",)).astype(jnp.bfloat16)
    own = scattered_sum(own, ("y",)).astype(jnp.bfloat16)
    parts = spread(own, DEEP)
    own = (jnp.sum(parts.astype(jnp.float32), axis=0) * grad_scale).astype(jnp.bfloat16)
    own = spread(own, ("y",)).reshape(-1, 128)
    own = spread(own, ("x",)).reshape(-1, 128)
    return own, lax.ppermute(own, "c", cores)


def unpack_kernel(
    own_ref,
    other_ref,
    qkv_ref,
    proj_ref,
    up_ref,
    down_ref,
    conv_ref,
    gain_one_ref,
    gain_two_ref,
    table_ref,
    rows_s,
):
    core = lax.axis_index("c")
    half = ROWS // 2
    rows_s[pl.ds(pl.multiple_of(core * half, half), half), :] = own_ref[...]
    rows_s[pl.ds(pl.multiple_of((1 - core) * half, half), half), :] = other_ref[...]

    def piece(first, count):
        return rows_s[first : first + count, :].astype(jnp.float32)

    conv_ref[...] = piece(0, 1152).reshape(9, 128, 128)
    place = 1152
    for ref, tiles in ((qkv_ref, 3), (proj_ref, 1), (up_ref, 4)):
        for tile in range(tiles):
            ref[:, tile * 128 : (tile + 1) * 128] = piece(place, 128)
            place = place + 128
    down_ref[...] = piece(place, 512)
    small = piece(place + 512, 16)
    gain_one_ref[...] = small[0:1]
    gain_two_ref[...] = small[1:2]
    for low in range(WIN):
        moved = pltpu.roll(small, (128 - 16 * low) % 128, 1) if low else small
        for head in range(HEADS):
            for high in range(2):
                row = high * WIN + low
                if row < SPAN:
                    line = 2 + 2 * head + high
                    table_ref[head, row : row + 1, :] = moved[line : line + 1, :SPAN]


def lane_mean(values):
    return jnp.sum(values, axis=-1, keepdims=True) * (1.0 / 128.0)


def layer_norm(values, gain):
    centred = values - lane_mean(values)
    inverse = lax.rsqrt(lane_mean(centred * centred) + epsilon)
    normed = centred * inverse
    return (normed * gain).astype(jnp.bfloat16), normed, inverse


def layer_norm_back(grad_in, normed, inverse, gain):
    scaled = grad_in * gain
    return inverse * (scaled - lane_mean(scaled) - normed * lane_mean(scaled * normed))


def matmul(left, right):
    return jnp.dot(left, right, preferred_element_type=jnp.float32)


def matmul_nt(left, right):
    return lax.dot_general(left, right, (((1,), (1,)), ((), ())), preferred_element_type=jnp.float32)


def matmul_tn(left, right):
    return lax.dot_general(left, right, (((0,), (0,)), ((), ())), preferred_element_type=jnp.float32)


def by_heads(rows, head_masks):
    return jnp.concatenate([rows * mask for mask in head_masks], axis=0)


def own_heads(stacked, head_lanes):
    total = jnp.zeros((AREA, 128), jnp.float32)
    for head in range(HEADS):
        part = stacked[head * AREA : (head + 1) * AREA]
        total = total + jnp.where(head_lanes[head], part, 0.0)
    return total


def table_rows(bias_sum):
    lane = lax.broadcasted_iota(jnp.int32, (WIN, 128), 1)
    pieces = []
    for head in range(HEADS):
        half = head % 2
        tile = bias_sum[:, (head // 2) * 128 : (head // 2 + 1) * 128]
        tile_sum = jnp.zeros((WIN, 128), jnp.float32)
        for row in range(WIN):
            part = jnp.where(lane // AREA == half, tile[row * WIN : (row + 1) * WIN], 0.0)
            steps = (WIN * (WIN - 1 - row) - AREA * half) % 128
            tile_sum = tile_sum + (pltpu.roll(part, steps, 1) if steps else part)
        pieces.append(tile_sum)
    stacked = jnp.concatenate(pieces, axis=0)
    source = lax.broadcasted_iota(jnp.int32, (128, 256), 0)
    target = lax.broadcasted_iota(jnp.int32, (128, 256), 1)
    hit = jnp.logical_and(source // WIN == target // 16, source % WIN == target % 16)
    spread_to = jnp.where(hit, 1.0, 0.0).astype(jnp.bfloat16)
    spread = jnp.zeros((HEADS * WIN, 256), jnp.float32)
    rest = stacked
    for _ in range(3):
        part = rest.astype(jnp.bfloat16)
        spread = spread + matmul(part, spread_to)
        rest = rest - part.astype(jnp.float32)
    place = lax.broadcasted_iota(jnp.int32, (HEADS * WIN, 256), 0) % WIN
    table = jnp.zeros((HEADS * WIN, 256), jnp.float32)
    for row in range(WIN):
        part = jnp.where(place == row, spread, 0.0)
        table = table + (pltpu.roll(part, WIN - 1 - row, 1) if row < WIN - 1 else part)
    rows = []
    for head in range(HEADS):
        head_sum = jnp.sum(table[head * WIN : (head + 1) * WIN], axis=0, keepdims=True)
        rows.extend([head_sum[:, :128], head_sum[:, 128:]])
    return rows


def block_kernel(
    lat_total,
    tokens_ref,
    grad_ref,
    ids_ref,
    lon_near_ref,
    lon_far_ref,
    lat_near_ref,
    lat_far_ref,
    table_ref,
    qkv_ref,
    proj_ref,
    up_ref,
    down_ref,
    conv_ref,
    gain_one_ref,
    gain_two_ref,
    down_out_ref,
    grad_tokens_ref,
    kept_ref,
    sent_ref,
    tokens_s,
    grad_s,
    ids_s,
    gcat_s,
    rows_s,
    block_out_s,
    grad_tokens_s,
    ln_one_s,
    ln_two_s,
    hidden_s,
    grad_pre_s,
    grad_block_s,
    mixed_s,
    grad_att_s,
    grad_qkv_s,
):
    own_rows, own_cols = tokens_ref.shape[0], tokens_ref.shape[1]
    first_col = place_along(LAT) * own_cols
    labels = assembled(
        tokens_ref,
        grad_ref,
        ids_ref,
        lon_near_ref,
        lon_far_ref,
        lat_near_ref,
        lat_far_ref,
        tokens_s,
        grad_s,
        ids_s,
        first_col,
        lat_total,
    )
    ids_s[...] = labels
    position = first_col - TOKEN_RIM + lax.broadcasted_iota(jnp.int32, (PAD_COLS, 128), 0)
    position = jnp.where(position < 0, position + lat_total, position)
    position = jnp.where(position >= lat_total, position - lat_total, position)
    keep_after = jnp.where(position != lat_total - 1, 1.0, 0.0)
    keep_before = jnp.where(position != 0, 1.0, 0.0)
    for tap, keep in ((0, keep_after), (1, None), (2, keep_before)):
        piece = grad_s[:, 5 - tap : 5 - tap + PAD_COLS, :]
        if keep is not None:
            piece = piece * keep[None]
        gcat_s[:, tap * 128 : (tap + 1) * 128] = piece.reshape(GRAD_ROWS * PAD_COLS, 128).astype(
            jnp.bfloat16
        )
    lane_row = lax.broadcasted_iota(jnp.int32, (AREA, 128), 0)
    diagonal = (
        lax.broadcasted_iota(jnp.int32, (AREA, HEADS * AREA), 1) % AREA
        == lax.broadcasted_iota(jnp.int32, (AREA, HEADS * AREA), 0)
    )
    gain_one, gain_two = gain_one_ref[...], gain_two_ref[...]
    lane = lax.broadcasted_iota(jnp.int32, (AREA, 128), 1)
    head_lanes = [lane // HEAD_DIM == head for head in range(HEADS)]
    head_masks = [jnp.where(hit, 1.0, 0.0).astype(jnp.bfloat16) for hit in head_lanes]
    biases = bias_rows(table_ref)
    score_scale = HEAD_DIM ** (-0.5)
    length = WIN_COLS * AREA
    bias_sum = jnp.zeros((AREA, HEADS * AREA), jnp.float32)
    gain_one_sum = jnp.zeros((1, 128), jnp.float32)
    gain_two_sum = jnp.zeros((1, 128), jnp.float32)
    for chunk in range(WIN_ROWS):
        top = chunk * WIN
        source = jnp.concatenate(
            [
                tokens_s[top : top + WIN, 4 + win * WIN : 12 + win * WIN, :].reshape(AREA, 128)
                for win in range(WIN_COLS)
            ],
            axis=0,
        )
        label_rows = jnp.concatenate(
            [
                jnp.broadcast_to(ids_s[top + row : top + row + 1, :], (WIN, 128))
                for row in range(WIN)
            ],
            axis=0,
        )
        ln_one, normed_one, inverse_one = layer_norm(source, gain_one)
        qkv_all = matmul(ln_one, qkv_ref[...]).astype(jnp.bfloat16)
        saved, mixed_parts = [], []
        for win in range(WIN_COLS):
            part = qkv_all[win * AREA : (win + 1) * AREA]
            query, key, value = part[:, :128], part[:, 128:256], part[:, 256:]
            query_heads = by_heads(query, head_masks)
            picked = jnp.where(lane == win * WIN + lane_row % WIN, label_rows, 0.0)
            column = jnp.broadcast_to(
                jnp.sum(picked, axis=1, keepdims=True), (AREA, HEADS * AREA)
            )
            across = jnp.sum(jnp.where(diagonal, column, 0.0), axis=0, keepdims=True)
            allowed = column == across
            scores = matmul_nt(key, query_heads) * score_scale + biases
            scores = jnp.where(allowed, scores, -1e30)
            raised = jnp.exp(scores - jnp.max(scores, axis=0, keepdims=True))
            probabilities = raised * (1.0 / jnp.sum(raised, axis=0, keepdims=True))
            weights = probabilities.astype(jnp.bfloat16)
            mixed_parts.append(own_heads(matmul_tn(weights, value), head_lanes).astype(jnp.bfloat16))
            saved.append((query_heads, key, value, probabilities, weights))
        mixed = jnp.concatenate(mixed_parts, axis=0)
        projected = matmul(mixed, proj_ref[...]).astype(jnp.bfloat16)
        middle = source + projected.astype(jnp.float32)
        ln_two, normed_two, inverse_two = layer_norm(middle, gain_two)
        pre_act = matmul(ln_two, up_ref[...])
        cumulative = 0.5 * (1.0 + lax.erf(pre_act * 0.7071067811865476))
        hidden = (pre_act * cumulative).astype(jnp.bfloat16)
        slope = cumulative + pre_act * (jnp.exp(-0.5 * pre_act * pre_act) * 0.3989422804014327)
        block_out = (middle + matmul(hidden, down_ref[...])).astype(jnp.bfloat16).astype(jnp.float32)
        for win in range(WIN_COLS):
            piece = block_out[win * AREA : (win + 1) * AREA].reshape(WIN, WIN, 128)
            block_out_s[top : top + WIN, win * WIN : (win + 1) * WIN, :] = piece

        grad_grid = jnp.zeros((WIN * PAD_COLS, 128), jnp.float32)
        for tap in range(3):
            first = (top + 2 - tap) * PAD_COLS
            taps = jnp.concatenate([conv_ref[3 * tap + side] for side in range(3)], axis=1)
            grad_grid = grad_grid + matmul_nt(gcat_s[first : first + WIN * PAD_COLS, :], taps)
        grad_grid = grad_grid.reshape(WIN, PAD_COLS, 128)
        grad_block = jnp.concatenate(
            [
                grad_grid[:, win * WIN : (win + 1) * WIN, :].reshape(AREA, 128)
                for win in range(WIN_COLS)
            ],
            axis=0,
        )
        grad_block_b = grad_block.astype(jnp.bfloat16)
        grad_hidden = matmul_nt(grad_block_b, down_ref[...])
        grad_pre = (grad_hidden * slope).astype(jnp.bfloat16)
        grad_ln_two = matmul_nt(grad_pre, up_ref[...])
        grad_middle = grad_block + layer_norm_back(grad_ln_two, normed_two, inverse_two, gain_two)
        grad_att = grad_middle.astype(jnp.bfloat16)
        grad_mixed = matmul_nt(grad_att, proj_ref[...]).astype(jnp.bfloat16)
        grad_parts = []
        for win in range(WIN_COLS):
            query_heads, key, value, probabilities, weights = saved[win]
            grad_heads = by_heads(grad_mixed[win * AREA : (win + 1) * AREA], head_masks)
            grad_probs = matmul_nt(value, grad_heads)
            grad_value = matmul(weights, grad_heads)
            centre = jnp.sum(probabilities * grad_probs, axis=0, keepdims=True)
            grad_scores = probabilities * (grad_probs - centre)
            if chunk and win:
                bias_sum = bias_sum + grad_scores
            grad_scores_b = grad_scores.astype(jnp.bfloat16)
            grad_key = matmul(grad_scores_b, query_heads) * score_scale
            grad_query = own_heads(matmul_tn(grad_scores_b, key), head_lanes) * score_scale
            grad_parts.append(
                jnp.concatenate([grad_query, grad_key, grad_value], axis=1).astype(jnp.bfloat16)
            )
        grad_qkv = jnp.concatenate(grad_parts, axis=0)
        grad_ln_one = matmul_nt(grad_qkv, qkv_ref[...])
        grad_tokens = grad_middle + layer_norm_back(grad_ln_one, normed_one, inverse_one, gain_one)
        for win in range(WIN_COLS):
            piece = grad_tokens[win * AREA : (win + 1) * AREA].reshape(WIN, WIN, 128)
            grad_tokens_s[top : top + WIN, win * WIN : (win + 1) * WIN, :] = piece
        if chunk:
            gain_one_sum = gain_one_sum + jnp.sum(
                (grad_ln_one * normed_one)[AREA:], axis=0, keepdims=True
            )
            gain_two_sum = gain_two_sum + jnp.sum(
                (grad_ln_two * normed_two)[AREA:], axis=0, keepdims=True
            )
            kept = slice((chunk - 1) * (length - AREA), chunk * (length - AREA))
            ln_one_s[kept, :] = ln_one[AREA:]
            ln_two_s[kept, :] = ln_two[AREA:]
            hidden_s[kept, :] = hidden[AREA:]
            grad_pre_s[kept, :] = grad_pre[AREA:]
            grad_block_s[kept, :] = grad_block_b[AREA:]
            mixed_s[kept, :] = mixed[AREA:]
            grad_att_s[kept, :] = grad_att[AREA:]
            grad_qkv_s[kept, :] = grad_qkv[AREA:]

    col = first_col + lax.broadcasted_iota(jnp.int32, (own_cols, 128), 0)
    keeps = (col != 0, None, col != lat_total - 1)
    shifted = []
    for tap in range(3):
        piece = block_out_s[3 : own_rows + 5, 3 + tap : 3 + tap + own_cols, :]
        if keeps[tap] is not None:
            piece = piece * jnp.where(keeps[tap], 1.0, 0.0)[None]
        shifted.append(piece.reshape((own_rows + 2) * own_cols, 128).astype(jnp.bfloat16))
    patches = jnp.concatenate(shifted, axis=1)
    count = own_rows * own_cols
    downscaled = jnp.zeros((count, 128), jnp.float32)
    grad_own = grad_ref[...].reshape(count, 128)
    for tap in range(3):
        rows = patches[tap * own_cols : tap * own_cols + count]
        downscaled = downscaled + matmul(rows, conv_ref[3 * tap : 3 * tap + 3].reshape(384, 128))
        rows_s[tap * 384 : (tap + 1) * 384, :] = matmul_tn(rows, grad_own).astype(jnp.bfloat16)
    down_out_ref[...] = downscaled.astype(jnp.bfloat16).reshape(own_rows, own_cols, 128)
    grad_tokens_ref[...] = (
        grad_tokens_s[4 : own_rows + 4, 4 : own_cols + 4, :].astype(jnp.bfloat16)
    )
    place = 1152
    for left, right, flipped in (
        (ln_one_s, grad_qkv_s, False),
        (mixed_s, grad_att_s, False),
        (ln_two_s, grad_pre_s, False),
        (hidden_s, grad_block_s, True),
    ):
        product = matmul_tn(left[...], right[...]).astype(jnp.bfloat16)
        if flipped:
            rows_s[place : place + product.shape[0], :] = product
            place = place + product.shape[0]
        else:
            for tile in range(product.shape[1] // 128):
                rows_s[place : place + 128, :] = product[:, tile * 128 : (tile + 1) * 128]
                place = place + 128
    small = [gain_one_sum, gain_two_sum] + table_rows(bias_sum)
    small.append(jnp.zeros((16 - len(small), 128), jnp.float32))
    rows_s[place : place + 16, :] = jnp.concatenate(small, axis=0).astype(jnp.bfloat16)
    place = place + 16
    rows_s[place:, :] = jnp.zeros((ROWS - place, 128), jnp.bfloat16)
    core = lax.axis_index("c")
    half = ROWS // 2
    kept_ref[...] = rows_s[pl.ds(pl.multiple_of(core * half, half), half), :]
    sent_ref[...] = rows_s[pl.ds(pl.multiple_of((1 - core) * half, half), half), :]


def per_device(
    tokens,
    grad_out,
    window_ids,
    qkv_weight,
    proj_weight,
    up_weight,
    down_weight,
    conv_weight,
    gain_one,
    gain_two,
    position_bias,
):
    row_count, col_count, width = tokens.shape
    lat_total = col_count * lax.axis_size(LAT)
    tokens_all = row_count * lat_total * lax.axis_size(LON)
    vmem = pl.BlockSpec(memory_space=pltpu.VMEM)
    params = pltpu.CompilerParams(vmem_limit_bytes=48 * 1024 * 1024)
    bf16 = lambda *shape: jax.ShapeDtypeStruct(shape, jnp.bfloat16)
    f32 = lambda *shape: jax.ShapeDtypeStruct(shape, jnp.float32)
    held = lambda *shape: pltpu.VMEM(shape, jnp.bfloat16)
    wide = lambda *shape: pltpu.VMEM(shape, jnp.float32)
    table = jnp.pad(position_bias, ((0, 0), (0, 1), (0, 1))).reshape(HEADS, 256)
    slabs = TOKEN_RIM + GRAD_RIM + 1
    far, near = pl.pallas_call(
        lon_pack_kernel,
        out_shape=(bf16(slabs, col_count, width),) * 2,
        in_specs=[vmem] * 3,
        out_specs=(vmem,) * 2,
        scratch_shapes=[wide(col_count, width)],
        compiler_params=params,
    )(tokens, grad_out, window_ids)
    lon_far = swapped(far, LON, False)
    lon_near = swapped(near, LON, True)
    far, near = pl.pallas_call(
        lat_pack_kernel,
        out_shape=(bf16(MESSAGE, width),) * 2,
        in_specs=[vmem] * 5,
        out_specs=(vmem,) * 2,
        scratch_shapes=[
            wide(2, TOKEN_ROWS, WIN, width),
            wide(2, GRAD_ROWS, WIN, width),
            wide(32, width),
        ],
        compiler_params=params,
    )(tokens, grad_out, window_ids, lon_near, lon_far)
    lat_far = swapped(far, LAT, False)
    lat_near = swapped(near, LAT, True)
    count = AREA * (WIN_ROWS - 1) * (WIN_COLS - 1)
    downscaled, grad_tokens, kept, sent = pl.pallas_call(
        functools.partial(block_kernel, lat_total),
        out_shape=(
            bf16(*tokens.shape),
            bf16(*tokens.shape),
            bf16(ROWS // 2, width),
            bf16(ROWS // 2, width),
        ),
        in_specs=[vmem] * 15,
        out_specs=(vmem,) * 4,
        scratch_shapes=[
            wide(TOKEN_ROWS, 48, width),
            wide(GRAD_ROWS, 56, width),
            wide(32, width),
            held(GRAD_ROWS * PAD_COLS, 3 * width),
            held(ROWS, width),
            wide(TOKEN_ROWS, 40, width),
            wide(TOKEN_ROWS, 40, width),
            held(count, width),
            held(count, width),
            held(count, 4 * width),
            held(count, 4 * width),
            held(count, width),
            held(count, width),
            held(count, width),
            held(count, 3 * width),
        ],
        compiler_params=params,
        cost_estimate=pl.CostEstimate(
            flops=3_000_000_000, bytes_accessed=8_000_000, transcendentals=2_000_000
        ),
    )(
        tokens,
        grad_out,
        window_ids,
        lon_near,
        lon_far,
        lat_near,
        lat_far,
        table,
        qkv_weight,
        proj_weight,
        up_weight,
        down_weight,
        conv_weight,
        gain_one[None],
        gain_two[None],
    )
    own, other = total_over_devices(kept, sent, 1.0 / math.sqrt(tokens_all))
    results = pl.pallas_call(
        unpack_kernel,
        out_shape=(
            f32(width, 3 * width),
            f32(width, width),
            f32(width, 4 * width),
            f32(4 * width, width),
            f32(9, width, width),
            f32(1, width),
            f32(1, width),
            f32(HEADS, SPAN, SPAN),
        ),
        in_specs=[vmem] * 2,
        out_specs=(vmem,) * 8,
        scratch_shapes=[held(ROWS, width)],
        compiler_params=params,
    )(own, other)
    return (downscaled, grad_tokens) + results[:5] + (results[5][0], results[6][0], results[7])


def solution(mesh):
    lon_count, lat_count = mesh.devices.shape
    near = math.gcd(lon_count, 8)
    parts = (lon_count // near, near // 2, 2, 2, lat_count // 2)
    fine = Mesh(mesh.devices.reshape(parts), ("zl", "x", "c", "zh", "y"))
    grid = P(LON, LAT, None)
    return jax.shard_map(
        per_device,
        mesh=fine,
        in_specs=(grid, grid, P(LON, LAT)) + (P(),) * 8,
        out_specs=(grid, grid) + (P(),) * 8,
        check_vma=False,
    )
```

time: 137 us -> 132 us (0.964)
  blocking collectives: 72.3 us -> 54.4 us
  starting transfers between devices: 32.5 us -> 46.7 us
  waiting for transfers between devices: 3.18 us -> 10.1 us
  local copies, waits for them, and re-layouts: 11.1 us -> 5.6 us
  other arithmetic: 3.14 us -> 0.22 us
  Pallas kernels: 11.7 us -> 13.8 us
    ppermute x0 -> x2, starting transfers between devices: none -> 20.2 us  [the longest x1 11.8 us: total_over_devices(): other = lax.ppermute(sent, 'c', cores)]
    all_to_all x3, blocking collectives: 45.4 us -> 34.2 us  [spread(): return lax.all_to_all(copies, axes, 0, 0, tiled=True)]
    all_to_all x2, blocking collectives: 26.9 us -> 20.2 us  [scattered_sum(): received = lax.all_to_all(chunks, axes, 0, 0, tiled=True)]
    ppermute x4, starting transfers between devices: 32.5 us -> 26.5 us  [swapped(): return lax.ppermute(value, axes, pairs)]
    slice x20 -> x0, local copies, waits for them, and re-layouts: 4.34 us -> none  [the longest x5 2.24 us: per_device(): pieces.append(totals[offset:offset + size])]
    ppermute x4, waiting for transfers between devices: 3.18 us -> 7.49 us  [swapped(): return lax.ppermute(value, axes, pairs)]
    unnamed x24 -> x28, local copies, waits for them, and re-layouts: 2.21 us -> 5.42 us
    ppermute x0 -> x2, waiting for transfers between devices: none -> 2.65 us  [the longest x1 1.33 us: total_over_devices(): other = lax.ppermute(sent, 'c', cores)]
  transfers between devices with their start and end apart: 4 -> 6, of which waited for: 1 -> 4; matrix products, arithmetic and copies ran while one was open for 2% -> 1% of each run, Pallas kernels for 0% -> 0%
where the time goes in v3:
time: 132 us
  blocking collectives  54.4 us (41%)
  starting transfers between devices  46.7 us (35%)
  Pallas kernels  13.8 us (10%)
  waiting for transfers between devices  10.1 us (8%)
  local copies, waits for them, and re-layouts  5.6 us (4%)
    all_to_all x3, blocking collectives, spread(): return lax.all_to_all(copies, axes, 0, 0, tiled=True)  34.2 us
    ppermute x4, starting transfers between devices, swapped(): return lax.ppermute(value, axes, pairs)  26.5 us
    all_to_all x2, blocking collectives, scattered_sum(): received = lax.all_to_all(chunks, axes, 0, 0, tiled=True)  20.2 us
    pallas_call x1, Pallas kernels, per_device(): pl.pallas_call(functools.partial(block_kernel, lat_total), out_shape=(bf1...  12.5 us
    ppermute x1, starting transfers between devices, total_over_devices(): other = lax.ppermute(sent, 'c', cores)  11.8 us
    ppermute x1, starting transfers between devices, total_over_devices(): return (own, lax.ppermute(own, 'c', cores))  8.48 us
    ppermute x4, waiting for transfers between devices, swapped(): return lax.ppermute(value, axes, pairs)  7.49 us
    unnamed x28, local copies, waits for them, and re-layouts  5.42 us
  transfers between devices with their start and end apart: 6, of which 4 were waited for; matrix products, arithmetic and copies ran while one was open for 1% of the time, Pallas kernels for 0%

profile of v3, /device:TPU:1, one launch (start us, length us, event | category | flops | bytes accessed | tf_op | source)
XLA Modules:
  0.0 131.7 jit_solution(13230187868904317883)
XLA Ops:
  0.6 0.0 copy-start
  0.7 0.9 copy-done
  1.6 0.9 copy-done.2
  2.5 0.7 copy-done.4
  3.2 12.6 %collective-permute-start = (bf16[10,32,128]{2,1,0:T(8,128)(2,1)S(1)}, bf16[10,32,128]{2,1,0:T(8,128)(2,1)S(1)}, u32[]{:S(2)}, u32[]{:S(2)}) collective-permute-start(bf16[10,32,128]{2,1,0:T(8,128)(2,1)S(1)} %get-tuple-element.26), channel_id=1, source_target_pairs={{0,16},{16,0},{32,48},{48,32},{64,80},{80,64},{96,112},{112,96},{1... | collective-permute-start | bytes 245768 | tf_op jit(solution)/shard_map/ppermute | solution.py:42
  15.8 2.1 %collective-permute-start.1 = (bf16[10,32,128]{2,1,0:T(8,128)(2,1)S(1)}, bf16[10,32,128]{2,1,0:T(8,128)(2,1)S(1)}, u32[]{:S(2)}, u32[]{:S(2)}) collective-permute-start(bf16[10,32,128]{2,1,0:T(8,128)(2,1)S(1)} %get-tuple-element.27), channel_id=1, source_target_pairs={{0,752},{16,32},{32,16},{48,64},{64,48},{80,96},{96,80},{112,128},... | collective-permute-start | bytes 245768 | tf_op jit(solution)/shard_map/ppermute | solution.py:42
  17.8 3.8 %collective-permute-done.1.lon_far_ref = bf16[10,32,128]{2,1,0:T(8,128)(2,1)S(1)} collective-permute-done((bf16[10,32,128]{2,1,0:T(8,128)(2,1)S(1)}, bf16[10,32,128]{2,1,0:T(8,128)(2,1)S(1)}, u32[]{:S(2)}, u32[]{:S(2)}) %collective-permute-start.1) | collective-permute-done | bytes 81952 | tf_op jit(solution)/shard_map/ppermute | solution.py:42
  21.7 0.1 shard_map.187
  21.7 2.1 %collective-permute-start.2 = (bf16[432,128]{1,0:T(8,128)(2,1)S(1)}, bf16[432,128]{1,0:T(8,128)(2,1)S(1)}, u32[]{:S(2)}, u32[]{:S(2)}) collective-permute-start(bf16[432,128]{1,0:T(8,128)(2,1)S(1)} %get-tuple-element.28), channel_id=1, source_target_pairs={{0,1},{1,0},{2,3},{3,2},{4,5},{5,4},{6,7},{7,6},{8,9},{9,8},{10,11... | collective-permute-start | bytes 331784 | tf_op jit(solution)/shard_map/ppermute | solution.py:42
  23.8 9.8 %collective-permute-start.3 = (bf16[432,128]{1,0:T(8,128)(2,1)S(1)}, bf16[432,128]{1,0:T(8,128)(2,1)S(1)}, u32[]{:S(2)}, u32[]{:S(2)}) collective-permute-start(bf16[432,128]{1,0:T(8,128)(2,1)S(1)} %get-tuple-element.29), channel_id=1, source_target_pairs={{0,15},{1,2},{2,1},{3,4},{4,3},{5,6},{6,5},{7,8},{8,7},{9,10},{10,... | collective-permute-start | bytes 331784 | tf_op jit(solution)/shard_map/ppermute | solution.py:42
  33.6 0.8 copy.25
  34.4 0.0 copy-start.5
  34.4 0.1 reshape.38.table_ref
  34.5 3.7 %collective-permute-done.3.lat_far_ref = bf16[432,128]{1,0:T(8,128)(2,1)S(1)} collective-permute-done((bf16[432,128]{1,0:T(8,128)(2,1)S(1)}, bf16[432,128]{1,0:T(8,128)(2,1)S(1)}, u32[]{:S(2)}, u32[]{:S(2)}) %collective-permute-start.3) | collective-permute-done | bytes 110624 | tf_op jit(solution)/shard_map/ppermute | solution.py:42
  38.2 0.6 copy-done.11
  38.8 0.0 copy-done.12
  38.8 0.9 copy-done.9
  39.7 12.5 %shard_map.188 = (bf16[16,32,128]{2,1,0:T(8,128)(2,1)}, bf16[16,32,128]{2,1,0:T(8,128)(2,1)}, bf16[1536,128]{1,0:T(8,128)(2,1)S(1)}, bf16[1536,128]{1,0:T(8,128)(2,1)S(1)}) custom-call(bf16[16,32,128]{2,1,0:T(8,128)(2,1)S(1)} %copy-done.1, bf16[16,32,128]{2,1,0:T(8,128)(2,1)S(1)} %copy-done.3, s32[16,32]{1,0:T(8,128)S(1)} %copy-done.5, ...), custom_call_target="tpu_custom_call" | custom-call | flops 3000000000 | bytes 8000000 | tf_op jit(solution)/shard_map/pallas_call | solution.py:625
  52.3 11.8 %collective-permute-start.4 = (bf16[1536,128]{1,0:T(8,128)(2,1)S(1)}, bf16[1536,128]{1,0:T(8,128)(2,1)S(1)}, u32[]{:S(2)}, u32[]{:S(2)}) collective-permute-start(bf16[1536,128]{1,0:T(8,128)(2,1)S(1)} %get-tuple-element.33), channel_id=1, source_target_pairs={{0,16},{16,0},{1,17},{17,1},{2,18},{18,2},{3,19},{19,3},{4,20},{20... | collective-permute-start | bytes 1179656 | tf_op jit(solution)/shard_map/ppermute | solution.py:214
  64.0 1.3 %collective-permute-done.4 = bf16[1536,128]{1,0:T(8,128)(2,1)S(1)} collective-permute-done((bf16[1536,128]{1,0:T(8,128)(2,1)S(1)}, bf16[1536,128]{1,0:T(8,128)(2,1)S(1)}, u32[]{:S(2)}, u32[]{:S(2)}) %collective-permute-start.4) | collective-permute-done | bytes 393248 | tf_op jit(solution)/shard_map/ppermute | solution.py:214
  65.4 0.1 add_convert_fusion
  65.5 10.2 %all_to_all.25 = bf16[4,384,128]{2,1,0:T(8,128)(2,1)S(1)} all-to-all(bf16[4,384,128]{2,1,0:T(8,128)(2,1)S(1)} %bitcast.12), channel_id=1, replica_groups=mesh['zl'=6,'x'=4,'c'=2,'zh'=2,'y'=8] {'x'}, dimensions={0} | all-to-all | bytes 786432 | tf_op jit(solution)/shard_map/all_to_all | solution.py:202
  75.7 0.1 reduce_sum.33
  75.7 10.0 %all_to_all.26 = bf16[8,48,128]{2,1,0:T(8,128)(2,1)S(1)} all-to-all(bf16[8,48,128]{2,1,0:T(8,128)(2,1)S(1)} %bitcast.13), channel_id=1, replica_groups=mesh['zl'=6,'x'=4,'c'=2,'zh'=2,'y'=8] {'y'}, dimensions={0} | all-to-all | bytes 196608 | tf_op jit(solution)/shard_map/all_to_all | solution.py:202
  85.8 15.7 %all_to_all.27 = bf16[12,48,128]{2,1,0:T(8,128)(2,1)S(1)} all-to-all(bf16[12,48,128]{2,1,0:T(8,128)(2,1)S(1)} %broadcast_in_dim.27), channel_id=1, replica_groups=mesh['zl'=6,'x'=4,'c'=2,'zh'=2,'y'=8] {'zl','zh'}, dimensions={0} | all-to-all | bytes 294912 | tf_op jit(solution)/shard_map/all_to_all | solution.py:209
  101.5 10.0 %all_to_all.28 = bf16[8,48,128]{2,1,0:T(8,128)(2,1)S(1)} all-to-all(bf16[8,48,128]{2,1,0:T(8,128)(2,1)S(1)} %broadcast_in_dim.28), channel_id=1, replica_groups=mesh['zl'=6,'x'=4,'c'=2,'zh'=2,'y'=8] {'y'}, dimensions={0} | all-to-all | bytes 196608 | tf_op jit(solution)/shard_map/all_to_all | solution.py:209
  111.4 0.1 broadcast_in_dim.30
  111.5 8.6 %all_to_all.29 = bf16[4,384,128]{2,1,0:T(8,128)(2,1)S(1)} all-to-all(bf16[4,384,128]{2,1,0:T(8,128)(2,1)S(1)} %broadcast_in_dim.30), channel_id=1, replica_groups=mesh['zl'=6,'x'=4,'c'=2,'zh'=2,'y'=8] {'x'}, dimensions={0} | all-to-all | bytes 786432 | tf_op jit(solution)/shard_map/all_to_all | solution.py:209
  120.1 8.5 %collective-permute-start.5 = (bf16[1536,128]{1,0:T(8,128)(2,1)S(1)}, bf16[1536,128]{1,0:T(8,128)(2,1)S(1)}, u32[]{:S(2)}, u32[]{:S(2)}) collective-permute-start(bf16[1536,128]{1,0:T(8,128)(2,1)S(1)} %bitcast.8), channel_id=1, source_target_pairs={{0,16},{16,0},{1,17},{17,1},{2,18},{18,2},{3,19},{19,3},{4,20},{20... | collective-permute-start | bytes 1179656 | tf_op jit(solution)/shard_map/ppermute | solution.py:222
  128.6 1.3 %collective-permute-done.5.other_ref = bf16[1536,128]{1,0:T(8,128)(2,1)S(1)} collective-permute-done((bf16[1536,128]{1,0:T(8,128)(2,1)S(1)}, bf16[1536,128]{1,0:T(8,128)(2,1)S(1)}, u32[]{:S(2)}, u32[]{:S(2)}) %collective-permute-start.5) | collective-permute-done | bytes 393248 | tf_op jit(solution)/shard_map/ppermute | solution.py:222
  129.9 1.1 shard_map.189
  131.1 0.6 copy.24
  (27 shorter events, 0.2 us)
Async XLA Ops:
  0.6 0.9 copy-start
  1.6 0.9 copy-start.2
  2.5 0.7 copy-start.4
  3.2 35.0 %copy-start.7 = (bf16[128,512]{1,0:T(8,128)(2,1)S(1)}, bf16[128,512]{1,0:T(8,128)(2,1)}, u32[]{:S(2)}) copy-start(bf16[128,512]{1,0:T(8,128)(2,1)} %up_ref.1) | copy-start | bytes 393220
  3.2 35.0 %copy-start.8 = (bf16[512,128]{1,0:T(8,128)(2,1)S(1)}, bf16[512,128]{1,0:T(8,128)(2,1)}, u32[]{:S(2)}) copy-start(bf16[512,128]{1,0:T(8,128)(2,1)} %down_ref.1) | copy-start | bytes 393220
  3.2 14.6 %collective-permute-start = (bf16[10,32,128]{2,1,0:T(8,128)(2,1)S(1)}, bf16[10,32,128]{2,1,0:T(8,128)(2,1)S(1)}, u32[]{:S(2)}, u32[]{:S(2)}) collective-permute-start(bf16[10,32,128]{2,1,0:T(8,128)(2,1)S(1)} %get-tuple-element.26), channel_id=1, source_target_pairs={{0,16},{16,0},{32,48},{48,32},{64,80},{80,64},{96,112},{112,96},{1... | collective-permute-start | bytes 245768 | tf_op jit(solution)/shard_map/ppermute | solution.py:42
  15.8 22.4 %copy-start.6 = (bf16[9,128,128]{2,1,0:T(8,128)(2,1)S(1)}, bf16[9,128,128]{2,1,0:T(8,128)(2,1)}, u32[]{:S(2)}) copy-start(bf16[9,128,128]{2,1,0:T(8,128)(2,1)} %conv_ref.1) | copy-start | bytes 884740
  15.8 5.9 %collective-permute-start.1 = (bf16[10,32,128]{2,1,0:T(8,128)(2,1)S(1)}, bf16[10,32,128]{2,1,0:T(8,128)(2,1)S(1)}, u32[]{:S(2)}, u32[]{:S(2)}) collective-permute-start(bf16[10,32,128]{2,1,0:T(8,128)(2,1)S(1)} %get-tuple-element.27), channel_id=1, source_target_pairs={{0,752},{16,32},{32,16},{48,64},{64,48},{80,96},{96,80},{112,128},... | collective-permute-start | bytes 245768 | tf_op jit(solution)/shard_map/ppermute | solution.py:42
  21.7 16.5 %copy-start.3 = (bf16[16,32,128]{2,1,0:T(8,128)(2,1)S(1)}, bf16[16,32,128]{2,1,0:T(8,128)(2,1)}, u32[]{:S(2)}) copy-start(bf16[16,32,128]{2,1,0:T(8,128)(2,1)} %grad_ref.5) | copy-start | bytes 393220
  21.7 16.5 %copy-start.1 = (bf16[16,32,128]{2,1,0:T(8,128)(2,1)S(1)}, bf16[16,32,128]{2,1,0:T(8,128)(2,1)}, u32[]{:S(2)}) copy-start(bf16[16,32,128]{2,1,0:T(8,128)(2,1)} %tokens_ref.5) | copy-start | bytes 393220
  21.7 12.7 %collective-permute-start.2 = (bf16[432,128]{1,0:T(8,128)(2,1)S(1)}, bf16[432,128]{1,0:T(8,128)(2,1)S(1)}, u32[]{:S(2)}, u32[]{:S(2)}) collective-permute-start(bf16[432,128]{1,0:T(8,128)(2,1)S(1)} %get-tuple-element.28), channel_id=1, source_target_pairs={{0,1},{1,0},{2,3},{3,2},{4,5},{5,4},{6,7},{7,6},{8,9},{9,8},{10,11... | collective-permute-start | bytes 331784 | tf_op jit(solution)/shard_map/ppermute | solution.py:42
  23.8 14.4 %collective-permute-start.3 = (bf16[432,128]{1,0:T(8,128)(2,1)S(1)}, bf16[432,128]{1,0:T(8,128)(2,1)S(1)}, u32[]{:S(2)}, u32[]{:S(2)}) collective-permute-start(bf16[432,128]{1,0:T(8,128)(2,1)S(1)} %get-tuple-element.29), channel_id=1, source_target_pairs={{0,15},{1,2},{2,1},{3,4},{4,3},{5,6},{6,5},{7,8},{8,7},{9,10},{10,... | collective-permute-start | bytes 331784 | tf_op jit(solution)/shard_map/ppermute | solution.py:42
  34.4 3.8 %copy-start.10 = (bf16[128,128]{1,0:T(8,128)(2,1)S(1)}, bf16[128,128]{1,0:T(8,128)(2,1)}, u32[]{:S(2)}) copy-start(bf16[128,128]{1,0:T(8,128)(2,1)} %proj_ref.1) | copy-start | bytes 98308
  34.4 3.8 %copy-start.5 = (s32[16,32]{1,0:T(8,128)S(1)}, s32[16,32]{1,0:T(8,128)}, u32[]{:S(2)}) copy-start(s32[16,32]{1,0:T(8,128)} %ids_ref.5) | copy-start | bytes 6148
  38.1 0.7 copy-start.11
  38.2 0.7 copy-start.12
  38.8 0.9 copy-start.9
  52.3 13.1 %collective-permute-start.4 = (bf16[1536,128]{1,0:T(8,128)(2,1)S(1)}, bf16[1536,128]{1,0:T(8,128)(2,1)S(1)}, u32[]{:S(2)}, u32[]{:S(2)}) collective-permute-start(bf16[1536,128]{1,0:T(8,128)(2,1)S(1)} %get-tuple-element.33), channel_id=1, source_target_pairs={{0,16},{16,0},{1,17},{17,1},{2,18},{18,2},{3,19},{19,3},{4,20},{20... | collective-permute-start | bytes 1179656 | tf_op jit(solution)/shard_map/ppermute | solution.py:214
  120.1 9.8 %collective-permute-start.5 = (bf16[1536,128]{1,0:T(8,128)(2,1)S(1)}, bf16[1536,128]{1,0:T(8,128)(2,1)S(1)}, u32[]{:S(2)}, u32[]{:S(2)}) collective-permute-start(bf16[1536,128]{1,0:T(8,128)(2,1)S(1)} %bitcast.8), channel_id=1, source_target_pairs={{0,16},{16,0},{1,17},{17,1},{2,18},{18,2},{3,19},{19,3},{4,20},{20... | collective-permute-start | bytes 1179656 | tf_op jit(solution)/shard_map/ppermute | solution.py:222

commit v4 on v3

--- a/solution.py
+++ b/solution.py
@@ -28,7 +28,9 @@
 DEEP = ("zl", "zh")
 TOKEN_ROWS = 24
 GRAD_ROWS = 26
-MESSAGE = (TOKEN_ROWS + GRAD_ROWS) * WIN + 32
+TOKEN_PART = TOKEN_ROWS * TOKEN_RIM
+ID_PLACE = 232
+MESSAGE = 240
 
 epsilon = 1e-05
 
@@ -53,10 +55,27 @@
     return jnp.where(choice, jnp.int32(first), jnp.int32(second))
 
 
-def lon_pack_kernel(tokens_ref, grad_ref, ids_ref, far_ref, near_ref, ids_s):
+def fetched(pairs, sems):
+    copies = [
+        pltpu.make_async_copy(source, target, sems.at[place])
+        for place, (source, target) in enumerate(pairs)
+    ]
+    for copy in copies:
+        copy.start()
+    return copies
+
+
+def lon_pack_kernel(
+    tokens_hbm, grad_hbm, ids_hbm, far_ref, near_ref, tokens_ref, grad_ref, ids_ref, ids_s, sems
+):
+    copies = fetched(
+        ((tokens_hbm, tokens_ref), (grad_hbm, grad_ref), (ids_hbm, ids_ref)), sems
+    )
     even = place_along(LON) % 2 == 0
     rows = tokens_ref.shape[0]
     ids_s[...] = jnp.zeros_like(ids_s)
+    for copy in copies:
+        copy.wait()
     ids_s[0:LABEL_RIM, 0 : ids_ref.shape[1]] = ids_ref[rows - LABEL_RIM :, :].astype(jnp.float32)
     ids = ids_s[...].astype(jnp.bfloat16)
     for ref, upper in ((near_ref, even), (far_ref, jnp.logical_not(even))):
@@ -83,13 +102,14 @@
     tokens_ref,
     grad_ref,
     ids_ref,
+    lon_far_ref,
     lon_near_ref,
-    lon_far_ref,
     far_ref,
     near_ref,
     tokens_s,
     grad_s,
     ids_s,
+    message_s,
 ):
     lon_even = place_along(LON) % 2 == 0
     lat_even = place_along(LAT) % 2 == 0
@@ -108,12 +128,30 @@
         edges(tokens_s, either(below, TOKEN_ROWS - TOKEN_RIM, 0), ref[0:TOKEN_RIM])
         edges(grad_s, either(below, GRAD_ROWS - GRAD_RIM, 0), ref[TOKEN_RIM:split])
     lon_labels(ids_ref, lon_near_ref, lon_far_ref, lon_even, ids_s)
-    ids = ids_s[...].astype(jnp.bfloat16)
-    first, second = TOKEN_ROWS * WIN, (TOKEN_ROWS + GRAD_ROWS) * WIN
-    for ref, side in ((near_ref, either(lat_even, 1, 0)), (far_ref, either(lat_even, 0, 1))):
-        ref[0:first, :] = tokens_s[side].reshape(first, 128).astype(jnp.bfloat16)
-        ref[first:second, :] = grad_s[side].reshape(second - first, 128).astype(jnp.bfloat16)
-        ref[second:, :] = ids
+    lane = lax.broadcasted_iota(jnp.int32, (WIN, 128), 1)
+    ids = jnp.zeros((WIN, 128), jnp.float32)
+    for part in range(TOKEN_ROWS // WIN):
+        moved = pltpu.roll(
+            ids_s[part * WIN : (part + 1) * WIN, :], (128 - (cols - WIN) + WIN * part) % 128, 1
+        )
+        ids = jnp.where(lane // WIN == part, moved, ids)
+    for side in range(2):
+        skip = side * (WIN - TOKEN_RIM)
+        for row in range(TOKEN_ROWS):
+            message_s[side, row * TOKEN_RIM : (row + 1) * TOKEN_RIM, :] = tokens_s[
+                side, row, skip : skip + TOKEN_RIM, :
+            ]
+        skip = side * (WIN - GRAD_RIM)
+        for row in range(GRAD_ROWS):
+            first = TOKEN_PART + row * GRAD_RIM
+            message_s[side, first : first + GRAD_RIM, :] = grad_s[
+                side, row, skip : skip + GRAD_RIM, :
+            ]
+        first = TOKEN_PART + GRAD_ROWS * GRAD_RIM
+        message_s[side, first:ID_PLACE, :] = jnp.zeros((ID_PLACE - first, 128), jnp.float32)
+        message_s[side, ID_PLACE:, :] = ids
+    near_ref[...] = message_s[either(lat_even, 1, 0)].astype(jnp.bfloat16)
+    far_ref[...] = message_s[either(lat_even, 0, 1)].astype(jnp.bfloat16)
 
 
 def assembled(
@@ -127,6 +165,7 @@
     tokens_s,
     grad_s,
     ids_s,
+    message_s,
     first_col,
     lat_total,
 ):
@@ -142,18 +181,33 @@
         tokens_s[pl.ds(row, TOKEN_RIM), middle, :] = ref[0:TOKEN_RIM].astype(jnp.float32)
         row = either(below, GRAD_ROWS - GRAD_RIM, 0)
         grad_s[pl.ds(row, GRAD_RIM), middle, :] = ref[TOKEN_RIM:split].astype(jnp.float32)
-    first, second = TOKEN_ROWS * WIN, (TOKEN_ROWS + GRAD_ROWS) * WIN
-    for ref, below in ((lat_near_ref, lat_even), (lat_far_ref, jnp.logical_not(lat_even))):
-        side = pl.ds(pl.multiple_of(either(below, WIN + cols, 0), WIN), WIN)
-        tokens_s[:, side, :] = ref[0:first].astype(jnp.float32).reshape(TOKEN_ROWS, WIN, 128)
-        grad_s[:, side, :] = ref[first:second].astype(jnp.float32).reshape(GRAD_ROWS, WIN, 128)
+    near, far = lat_near_ref[...].astype(jnp.float32), lat_far_ref[...].astype(jnp.float32)
+    message_s[0] = jnp.where(lat_even, far, near)
+    message_s[1] = jnp.where(lat_even, near, far)
+    for side, token_col, grad_col in (
+        (0, WIN - TOKEN_RIM, WIN - GRAD_RIM),
+        (1, WIN + cols, WIN + cols),
+    ):
+        for row in range(TOKEN_ROWS):
+            tokens_s[row, token_col : token_col + TOKEN_RIM, :] = message_s[
+                side, row * TOKEN_RIM : (row + 1) * TOKEN_RIM, :
+            ]
+        for row in range(GRAD_ROWS):
+            first = TOKEN_PART + row * GRAD_RIM
+            grad_s[row, grad_col : grad_col + GRAD_RIM, :] = message_s[
+                side, first : first + GRAD_RIM, :
+            ]
     lon_labels(ids_ref, lon_near_ref, lon_far_ref, lon_even, ids_s)
-    before = jnp.where(
-        lat_even, lat_far_ref[second:].astype(jnp.float32), lat_near_ref[second:].astype(jnp.float32)
+    packed = message_s[0, ID_PLACE:, :]
+    before = jnp.concatenate(
+        [packed]
+        + [pltpu.roll(packed, 128 - WIN * part, 1) for part in range(1, TOKEN_ROWS // WIN)]
+        + [jnp.zeros_like(packed)],
+        axis=0,
     )
     lane = lax.broadcasted_iota(jnp.int32, ids_s.shape, 1)
     own = pltpu.roll(ids_s[...], LABEL_RIM, 1)
-    ids = jnp.where(lane < LABEL_RIM, pltpu.roll(before, 128 - (cols - LABEL_RIM), 1), own)
+    ids = jnp.where(lane < LABEL_RIM, before, own)
     shifted = first_col + lane - LABEL_RIM
     shifted = jnp.where(shifted < 0, shifted + lat_total, shifted)
     return ids * 2.0 + jnp.where(shifted >= lat_total - SHIFT, 1.0, 0.0)
@@ -260,7 +314,7 @@
                 row = high * WIN + low
                 if row < SPAN:
                     line = 2 + 2 * head + high
-                    table_ref[head, row : row + 1, :] = moved[line : line + 1, :SPAN]
+                    table_ref[row, head : head + 1, :] = moved[line : line + 1, :SPAN]
 
 
 def lane_mean(values):
@@ -343,18 +397,18 @@
     tokens_ref,
     grad_ref,
     ids_ref,
+    lon_far_ref,
     lon_near_ref,
-    lon_far_ref,
+    lat_far_ref,
     lat_near_ref,
-    lat_far_ref,
     table_ref,
-    qkv_ref,
-    proj_ref,
-    up_ref,
-    down_ref,
-    conv_ref,
-    gain_one_ref,
-    gain_two_ref,
+    qkv_hbm,
+    proj_hbm,
+    up_hbm,
+    down_hbm,
+    conv_hbm,
+    gain_one_hbm,
+    gain_two_hbm,
     down_out_ref,
     grad_tokens_ref,
     kept_ref,
@@ -374,7 +428,28 @@
     mixed_s,
     grad_att_s,
     grad_qkv_s,
+    message_s,
+    qkv_ref,
+    proj_ref,
+    up_ref,
+    down_ref,
+    conv_ref,
+    gain_one_ref,
+    gain_two_ref,
+    sems,
 ):
+    copies = fetched(
+        (
+            (qkv_hbm, qkv_ref),
+            (gain_one_hbm, gain_one_ref),
+            (gain_two_hbm, gain_two_ref),
+            (proj_hbm, proj_ref),
+            (up_hbm, up_ref),
+            (down_hbm, down_ref),
+            (conv_hbm, conv_ref),
+        ),
+        sems,
+    )
     own_rows, own_cols = tokens_ref.shape[0], tokens_ref.shape[1]
     first_col = place_along(LAT) * own_cols
     labels = assembled(
@@ -388,6 +463,7 @@
         tokens_s,
         grad_s,
         ids_s,
+        message_s,
         first_col,
         lat_total,
     )
@@ -409,11 +485,13 @@
         lax.broadcasted_iota(jnp.int32, (AREA, HEADS * AREA), 1) % AREA
         == lax.broadcasted_iota(jnp.int32, (AREA, HEADS * AREA), 0)
     )
+    biases = bias_rows(table_ref)
+    for copy in copies:
+        copy.wait()
     gain_one, gain_two = gain_one_ref[...], gain_two_ref[...]
     lane = lax.broadcasted_iota(jnp.int32, (AREA, 128), 1)
     head_lanes = [lane // HEAD_DIM == head for head in range(HEADS)]
     head_masks = [jnp.where(hit, 1.0, 0.0).astype(jnp.bfloat16) for hit in head_lanes]
-    biases = bias_rows(table_ref)
     score_scale = HEAD_DIM ** (-0.5)
     length = WIN_COLS * AREA
     bias_sum = jnp.zeros((AREA, HEADS * AREA), jnp.float32)
@@ -597,12 +675,19 @@
     wide = lambda *shape: pltpu.VMEM(shape, jnp.float32)
     table = jnp.pad(position_bias, ((0, 0), (0, 1), (0, 1))).reshape(HEADS, 256)
     slabs = TOKEN_RIM + GRAD_RIM + 1
-    far, near = pl.pallas_call(
+    anywhere = pl.BlockSpec(memory_space=pltpu.HBM)
+    far, near, tokens, grad_out, window_ids = pl.pallas_call(
         lon_pack_kernel,
-        out_shape=(bf16(slabs, col_count, width),) * 2,
-        in_specs=[vmem] * 3,
-        out_specs=(vmem,) * 2,
-        scratch_shapes=[wide(col_count, width)],
+        out_shape=(
+            bf16(slabs, col_count, width),
+            bf16(slabs, col_count, width),
+            bf16(*tokens.shape),
+            bf16(*grad_out.shape),
+            jax.ShapeDtypeStruct(window_ids.shape, jnp.int32),
+        ),
+        in_specs=[anywhere] * 3,
+        out_specs=(vmem,) * 5,
+        scratch_shapes=[wide(col_count, width), pltpu.SemaphoreType.DMA((3,))],
         compiler_params=params,
     )(tokens, grad_out, window_ids)
     lon_far = swapped(far, LON, False)
@@ -616,9 +701,10 @@
             wide(2, TOKEN_ROWS, WIN, width),
             wide(2, GRAD_ROWS, WIN, width),
             wide(32, width),
+            wide(2, MESSAGE, width),
         ],
         compiler_params=params,
-    )(tokens, grad_out, window_ids, lon_near, lon_far)
+    )(tokens, grad_out, window_ids, lon_far, lon_near)
     lat_far = swapped(far, LAT, False)
     lat_near = swapped(near, LAT, True)
     count = AREA * (WIN_ROWS - 1) * (WIN_COLS - 1)
@@ -630,7 +716,7 @@
             bf16(ROWS // 2, width),
             bf16(ROWS // 2, width),
         ),
-        in_specs=[vmem] * 15,
+        in_specs=[vmem] * 8 + [anywhere] * 7,
         out_specs=(vmem,) * 4,
         scratch_shapes=[
             wide(TOKEN_ROWS, 48, width),
@@ -648,6 +734,15 @@
             held(count, width),
             held(count, width),
             held(count, 3 * width),
+            wide(2, MESSAGE, width),
+            held(*qkv_weight.shape),
+            held(*proj_weight.shape),
+            held(*up_weight.shape),
+            held(*down_weight.shape),
+            held(*conv_weight.shape),
+            wide(1, width),
+            wide(1, width),
+            pltpu.SemaphoreType.DMA((7,)),
         ],
         compiler_params=params,
         cost_estimate=pl.CostEstimate(
@@ -657,10 +752,10 @@
         tokens,
         grad_out,
         window_ids,
+        lon_far,
         lon_near,
-        lon_far,
+        lat_far,
         lat_near,
-        lat_far,
         table,
         qkv_weight,
         proj_weight,
@@ -681,14 +776,18 @@
             f32(9, width, width),
             f32(1, width),
             f32(1, width),
-            f32(HEADS, SPAN, SPAN),
+            f32(SPAN, HEADS, SPAN),
         ),
         in_specs=[vmem] * 2,
         out_specs=(vmem,) * 8,
         scratch_shapes=[held(ROWS, width)],
         compiler_params=params,
     )(own, other)
-    return (downscaled, grad_tokens) + results[:5] + (results[5][0], results[6][0], results[7])
+    return (downscaled, grad_tokens) + results[:5] + (
+        results[5][0],
+        results[6][0],
+        results[7].swapaxes(0, 1),
+    )
 
 
 def solution(mesh):

time: 132 us -> 126 us (0.955)
  waiting for transfers between devices: 10.1 us -> 6.74 us
  local copies, waits for them, and re-layouts: 5.6 us -> 3.34 us
  starting transfers between devices: 46.7 us -> 44.7 us
    ppermute x1, starting transfers between devices: 11.8 us -> 3.64 us  [total_over_devices(): other = lax.ppermute(sent, 'c', cores)]
    ppermute x4, starting transfers between devices: 26.5 us -> 32.5 us  [swapped(): return lax.ppermute(value, axes, pairs)]
    ppermute x4, waiting for transfers between devices: 7.49 us -> 4.09 us  [swapped(): return lax.ppermute(value, axes, pairs)]
    unnamed x28 -> x23, local copies, waits for them, and re-layouts: 5.42 us -> 3.16 us
  transfers between devices with their start and end apart: 6 -> 6, of which waited for: 4 -> 4; matrix products, arithmetic and copies ran while one was open for 1% -> 0% of each run, Pallas kernels for 0% -> 0%
where the time goes in v4:
time: 126 us; the launch traced here: 125 us
  blocking collectives  54.6 us (43%)
  starting transfers between devices  44.7 us (35%)
  Pallas kernels  15 us (12%)
  waiting for transfers between devices  6.74 us (5%)
  local copies, waits for them, and re-layouts  3.34 us (3%)
    all_to_all x3, blocking collectives, spread(): return lax.all_to_all(copies, axes, 0, 0, tiled=True)  34.3 us
    ppermute x4, starting transfers between devices, swapped(): return lax.ppermute(value, axes, pairs)  32.5 us
    all_to_all x2, blocking collectives, scattered_sum(): received = lax.all_to_all(chunks, axes, 0, 0, tiled=True)  20.3 us
    pallas_call x1, Pallas kernels, per_device(): pl.pallas_call(functools.partial(block_kernel, lat_total), out_shape=(bf1...  13.4 us
    ppermute x1, starting transfers between devices, total_over_devices(): return (own, lax.ppermute(own, 'c', cores))  8.58 us
    ppermute x4, waiting for transfers between devices, swapped(): return lax.ppermute(value, axes, pairs)  4.09 us
    ppermute x1, starting transfers between devices, total_over_devices(): other = lax.ppermute(sent, 'c', cores)  3.64 us
    unnamed x23, local copies, waits for them, and re-layouts  3.16 us
  transfers between devices with their start and end apart: 6, of which 4 were waited for; matrix products, arithmetic and copies ran while one was open for 0% of the time, Pallas kernels for 0%

profile of v4, /device:TPU:1, one launch (start us, length us, event | category | flops | bytes accessed | tf_op | source)
XLA Modules:
  0.0 125.5 jit_solution(1555679370602259812)
XLA Ops:
  0.6 0.0 copy-start
  0.7 0.9 copy-done
  1.6 0.9 copy-done.1
  2.5 0.7 copy-done.2
  3.2 0.4 shard_map.186
  3.6 4.5 %collective-permute-start = (bf16[10,32,128]{2,1,0:T(8,128)(2,1)S(1)}, bf16[10,32,128]{2,1,0:T(8,128)(2,1)S(1)}, u32[]{:S(2)}, u32[]{:S(2)}) collective-permute-start(bf16[10,32,128]{2,1,0:T(8,128)(2,1)S(1)} %get-tuple-element.32), channel_id=1, source_target_pairs={{0,752},{16,32},{32,16},{48,64},{64,48},{80,96},{96,80},{112,128},... | collective-permute-start | bytes 245768 | tf_op jit(solution)/shard_map/ppermute | solution.py:44
  8.1 13.3 %collective-permute-start.1 = (bf16[10,32,128]{2,1,0:T(8,128)(2,1)S(1)}, bf16[10,32,128]{2,1,0:T(8,128)(2,1)S(1)}, u32[]{:S(2)}, u32[]{:S(2)}) collective-permute-start(bf16[10,32,128]{2,1,0:T(8,128)(2,1)S(1)} %get-tuple-element.33), channel_id=1, source_target_pairs={{0,16},{16,0},{32,48},{48,32},{64,80},{80,64},{96,112},{112,96},{1... | collective-permute-start | bytes 245768 | tf_op jit(solution)/shard_map/ppermute | solution.py:44
  21.3 0.0 collective-permute-done.lon_far_ref
  21.4 0.9 collective-permute-done.1.lon_near_ref
  22.3 0.1 shard_map.187
  22.4 12.8 %collective-permute-start.2 = (bf16[240,128]{1,0:T(8,128)(2,1)S(1)}, bf16[240,128]{1,0:T(8,128)(2,1)S(1)}, u32[]{:S(2)}, u32[]{:S(2)}) collective-permute-start(bf16[240,128]{1,0:T(8,128)(2,1)S(1)} %get-tuple-element.34), channel_id=1, source_target_pairs={{0,15},{1,2},{2,1},{3,4},{4,3},{5,6},{6,5},{7,8},{8,7},{9,10},{10,... | collective-permute-start | bytes 184328 | tf_op jit(solution)/shard_map/ppermute | solution.py:44
  35.2 1.9 %collective-permute-start.3 = (bf16[240,128]{1,0:T(8,128)(2,1)S(1)}, bf16[240,128]{1,0:T(8,128)(2,1)S(1)}, u32[]{:S(2)}, u32[]{:S(2)}) collective-permute-start(bf16[240,128]{1,0:T(8,128)(2,1)S(1)} %get-tuple-element.35), channel_id=1, source_target_pairs={{0,1},{1,0},{2,3},{3,2},{4,5},{5,4},{6,7},{7,6},{8,9},{9,8},{10,11... | collective-permute-start | bytes 184328 | tf_op jit(solution)/shard_map/ppermute | solution.py:44
  37.1 0.0 copy-start.7
  37.1 0.1 reshape.38.table_ref
  37.2 0.0 collective-permute-done.2.lat_far_ref
  37.2 3.2 %collective-permute-done.3.lat_near_ref = bf16[240,128]{1,0:T(8,128)(2,1)S(1)} collective-permute-done((bf16[240,128]{1,0:T(8,128)(2,1)S(1)}, bf16[240,128]{1,0:T(8,128)(2,1)S(1)}, u32[]{:S(2)}, u32[]{:S(2)}) %collective-permute-start.3) | collective-permute-done | bytes 61472 | tf_op jit(solution)/shard_map/ppermute | solution.py:44
  40.5 0.6 copy-done.8
  41.1 0.0 copy-done.9
  41.1 13.4 %shard_map.188 = (bf16[16,32,128]{2,1,0:T(8,128)(2,1)}, bf16[16,32,128]{2,1,0:T(8,128)(2,1)}, bf16[1536,128]{1,0:T(8,128)(2,1)S(1)}, bf16[1536,128]{1,0:T(8,128)(2,1)S(1)}) custom-call(bf16[16,32,128]{2,1,0:T(8,128)(2,1)S(1)} %get-tuple-element.29.tokens_ref, bf16[16,32,128]{2,1,0:T(8,128)(2,1)S(1)} %get-tuple-element.30.grad_ref, ...), custom_call_target="tpu_custom_call" | custom-call | flops 3000000000 | bytes 8000000 | tf_op jit(solution)/shard_map/pallas_call | solution.py:711
  54.5 3.6 %collective-permute-start.4 = (bf16[1536,128]{1,0:T(8,128)(2,1)S(1)}, bf16[1536,128]{1,0:T(8,128)(2,1)S(1)}, u32[]{:S(2)}, u32[]{:S(2)}) collective-permute-start(bf16[1536,128]{1,0:T(8,128)(2,1)S(1)} %get-tuple-element.39), channel_id=1, source_target_pairs={{0,16},{16,0},{1,17},{17,1},{2,18},{18,2},{3,19},{19,3},{4,20},{20... | collective-permute-start | bytes 1179656 | tf_op jit(solution)/shard_map/ppermute | solution.py:268
  58.2 1.3 %collective-permute-done.4 = bf16[1536,128]{1,0:T(8,128)(2,1)S(1)} collective-permute-done((bf16[1536,128]{1,0:T(8,128)(2,1)S(1)}, bf16[1536,128]{1,0:T(8,128)(2,1)S(1)}, u32[]{:S(2)}, u32[]{:S(2)}) %collective-permute-start.4) | collective-permute-done | bytes 393248 | tf_op jit(solution)/shard_map/ppermute | solution.py:268
  59.5 0.1 add_convert_fusion
  59.6 10.2 %all_to_all.25 = bf16[4,384,128]{2,1,0:T(8,128)(2,1)S(1)} all-to-all(bf16[4,384,128]{2,1,0:T(8,128)(2,1)S(1)} %bitcast.13), channel_id=1, replica_groups=mesh['zl'=6,'x'=4,'c'=2,'zh'=2,'y'=8] {'x'}, dimensions={0} | all-to-all | bytes 786432 | tf_op jit(solution)/shard_map/all_to_all | solution.py:256
  69.8 0.1 reduce_sum.33
  69.9 10.1 %all_to_all.26 = bf16[8,48,128]{2,1,0:T(8,128)(2,1)S(1)} all-to-all(bf16[8,48,128]{2,1,0:T(8,128)(2,1)S(1)} %bitcast.14), channel_id=1, replica_groups=mesh['zl'=6,'x'=4,'c'=2,'zh'=2,'y'=8] {'y'}, dimensions={0} | all-to-all | bytes 196608 | tf_op jit(solution)/shard_map/all_to_all | solution.py:256
  80.0 15.7 %all_to_all.27 = bf16[12,48,128]{2,1,0:T(8,128)(2,1)S(1)} all-to-all(bf16[12,48,128]{2,1,0:T(8,128)(2,1)S(1)} %broadcast_in_dim.27), channel_id=1, replica_groups=mesh['zl'=6,'x'=4,'c'=2,'zh'=2,'y'=8] {'zl','zh'}, dimensions={0} | all-to-all | bytes 294912 | tf_op jit(solution)/shard_map/all_to_all | solution.py:263
  95.8 10.0 %all_to_all.28 = bf16[8,48,128]{2,1,0:T(8,128)(2,1)S(1)} all-to-all(bf16[8,48,128]{2,1,0:T(8,128)(2,1)S(1)} %broadcast_in_dim.28), channel_id=1, replica_groups=mesh['zl'=6,'x'=4,'c'=2,'zh'=2,'y'=8] {'y'}, dimensions={0} | all-to-all | bytes 196608 | tf_op jit(solution)/shard_map/all_to_all | solution.py:263
  105.7 0.1 broadcast_in_dim.30
  105.8 8.6 %all_to_all.29 = bf16[4,384,128]{2,1,0:T(8,128)(2,1)S(1)} all-to-all(bf16[4,384,128]{2,1,0:T(8,128)(2,1)S(1)} %broadcast_in_dim.30), channel_id=1, replica_groups=mesh['zl'=6,'x'=4,'c'=2,'zh'=2,'y'=8] {'x'}, dimensions={0} | all-to-all | bytes 786432 | tf_op jit(solution)/shard_map/all_to_all | solution.py:263
  114.4 8.6 %collective-permute-start.5 = (bf16[1536,128]{1,0:T(8,128)(2,1)S(1)}, bf16[1536,128]{1,0:T(8,128)(2,1)S(1)}, u32[]{:S(2)}, u32[]{:S(2)}) collective-permute-start(bf16[1536,128]{1,0:T(8,128)(2,1)S(1)} %bitcast.9), channel_id=1, source_target_pairs={{0,16},{16,0},{1,17},{17,1},{2,18},{18,2},{3,19},{19,3},{4,20},{20... | collective-permute-start | bytes 1179656 | tf_op jit(solution)/shard_map/ppermute | solution.py:276
  123.0 1.3 %collective-permute-done.5.other_ref = bf16[1536,128]{1,0:T(8,128)(2,1)S(1)} collective-permute-done((bf16[1536,128]{1,0:T(8,128)(2,1)S(1)}, bf16[1536,128]{1,0:T(8,128)(2,1)S(1)}, u32[]{:S(2)}, u32[]{:S(2)}) %collective-permute-start.5) | collective-permute-done | bytes 393248 | tf_op jit(solution)/shard_map/ppermute | solution.py:276
  124.3 1.1 shard_map.189
  (22 shorter events, 0.1 us)
Async XLA Ops:
  0.6 0.9 copy-start
  1.5 0.9 copy-start.1
  2.5 0.7 copy-start.2
  3.2 33.9 %copy-start.10 = (f32[4,15,15]{2,0,1:T(4,128)S(1)}, f32[4,15,15]{2,0,1:T(4,128)}, u32[]{:S(2)}) copy-start(f32[4,15,15]{2,0,1:T(4,128)} %param.21) | copy-start | bytes 10804
  3.2 37.3 %copy-start.6 = (bf16[128,384]{1,0:T(8,128)(2,1)S(1)}, bf16[128,384]{1,0:T(8,128)(2,1)}, u32[]{:S(2)}) copy-start(bf16[128,384]{1,0:T(8,128)(2,1)} %qkv_hbm.1) | copy-start | bytes 294916
  3.6 17.8 %collective-permute-start = (bf16[10,32,128]{2,1,0:T(8,128)(2,1)S(1)}, bf16[10,32,128]{2,1,0:T(8,128)(2,1)S(1)}, u32[]{:S(2)}, u32[]{:S(2)}) collective-permute-start(bf16[10,32,128]{2,1,0:T(8,128)(2,1)S(1)} %get-tuple-element.32), channel_id=1, source_target_pairs={{0,752},{16,32},{32,16},{48,64},{64,48},{80,96},{96,80},{112,128},... | collective-permute-start | bytes 245768 | tf_op jit(solution)/shard_map/ppermute | solution.py:44
  8.1 14.2 %collective-permute-start.1 = (bf16[10,32,128]{2,1,0:T(8,128)(2,1)S(1)}, bf16[10,32,128]{2,1,0:T(8,128)(2,1)S(1)}, u32[]{:S(2)}, u32[]{:S(2)}) collective-permute-start(bf16[10,32,128]{2,1,0:T(8,128)(2,1)S(1)} %get-tuple-element.33), channel_id=1, source_target_pairs={{0,16},{16,0},{32,48},{48,32},{64,80},{80,64},{96,112},{112,96},{1... | collective-permute-start | bytes 245768 | tf_op jit(solution)/shard_map/ppermute | solution.py:44
  22.2 18.2 %copy-start.3 = (bf16[9,128,128]{2,1,0:T(8,128)(2,1)S(1)}, bf16[9,128,128]{2,1,0:T(8,128)(2,1)}, u32[]{:S(2)}) copy-start(bf16[9,128,128]{2,1,0:T(8,128)(2,1)} %conv_hbm.1) | copy-start | bytes 884740
  22.2 18.2 %copy-start.5 = (bf16[512,128]{1,0:T(8,128)(2,1)S(1)}, bf16[512,128]{1,0:T(8,128)(2,1)}, u32[]{:S(2)}) copy-start(bf16[512,128]{1,0:T(8,128)(2,1)} %down_hbm.1) | copy-start | bytes 393220
  22.4 18.1 %copy-start.4 = (bf16[128,512]{1,0:T(8,128)(2,1)S(1)}, bf16[128,512]{1,0:T(8,128)(2,1)}, u32[]{:S(2)}) copy-start(bf16[128,512]{1,0:T(8,128)(2,1)} %up_hbm.1) | copy-start | bytes 393220
  22.4 14.9 %collective-permute-start.2 = (bf16[240,128]{1,0:T(8,128)(2,1)S(1)}, bf16[240,128]{1,0:T(8,128)(2,1)S(1)}, u32[]{:S(2)}, u32[]{:S(2)}) collective-permute-start(bf16[240,128]{1,0:T(8,128)(2,1)S(1)} %get-tuple-element.34), channel_id=1, source_target_pairs={{0,15},{1,2},{2,1},{3,4},{4,3},{5,6},{6,5},{7,8},{8,7},{9,10},{10,... | collective-permute-start | bytes 184328 | tf_op jit(solution)/shard_map/ppermute | solution.py:44
  35.2 5.3 %collective-permute-start.3 = (bf16[240,128]{1,0:T(8,128)(2,1)S(1)}, bf16[240,128]{1,0:T(8,128)(2,1)S(1)}, u32[]{:S(2)}, u32[]{:S(2)}) collective-permute-start(bf16[240,128]{1,0:T(8,128)(2,1)S(1)} %get-tuple-element.35), channel_id=1, source_target_pairs={{0,1},{1,0},{2,3},{3,2},{4,5},{5,4},{6,7},{7,6},{8,9},{9,8},{10,11... | collective-permute-start | bytes 184328 | tf_op jit(solution)/shard_map/ppermute | solution.py:44
  37.1 3.3 %copy-start.7 = (bf16[128,128]{1,0:T(8,128)(2,1)S(1)}, bf16[128,128]{1,0:T(8,128)(2,1)}, u32[]{:S(2)}) copy-start(bf16[128,128]{1,0:T(8,128)(2,1)} %proj_hbm.1) | copy-start | bytes 98308
  40.4 0.7 copy-start.8
  40.4 0.7 copy-start.9
  54.5 5.0 %collective-permute-start.4 = (bf16[1536,128]{1,0:T(8,128)(2,1)S(1)}, bf16[1536,128]{1,0:T(8,128)(2,1)S(1)}, u32[]{:S(2)}, u32[]{:S(2)}) collective-permute-start(bf16[1536,128]{1,0:T(8,128)(2,1)S(1)} %get-tuple-element.39), channel_id=1, source_target_pairs={{0,16},{16,0},{1,17},{17,1},{2,18},{18,2},{3,19},{19,3},{4,20},{20... | collective-permute-start | bytes 1179656 | tf_op jit(solution)/shard_map/ppermute | solution.py:268
  114.4 9.9 %collective-permute-start.5 = (bf16[1536,128]{1,0:T(8,128)(2,1)S(1)}, bf16[1536,128]{1,0:T(8,128)(2,1)S(1)}, u32[]{:S(2)}, u32[]{:S(2)}) collective-permute-start(bf16[1536,128]{1,0:T(8,128)(2,1)S(1)} %bitcast.9), channel_id=1, source_target_pairs={{0,16},{16,0},{1,17},{17,1},{2,18},{18,2},{3,19},{19,3},{4,20},{20... | collective-permute-start | bytes 1179656 | tf_op jit(solution)/shard_map/ppermute | solution.py:276

commit v5 on v4

--- a/solution.py
+++ b/solution.py
@@ -250,6 +250,13 @@
     return jnp.concatenate(rows, axis=0)
 
 
+def bias_kernel(table_ref, gain_one_ref, gain_two_ref, bias_ref, gains_ref):
+    bias_ref[...] = bias_rows(table_ref)
+    gains_ref[...] = jnp.zeros_like(gains_ref)
+    gains_ref[0:1, :] = gain_one_ref[...]
+    gains_ref[1:2, :] = gain_two_ref[...]
+
+
 def scattered_sum(partial, axes):
     count = lax.axis_size(axes)
     chunks = partial.reshape(count, partial.shape[0] // count, partial.shape[1])
@@ -267,8 +274,7 @@
     cores = [(0, 1), (1, 0)]
     other = lax.ppermute(sent, "c", cores)
     own = (kept.astype(jnp.float32) + other.astype(jnp.float32)).astype(jnp.bfloat16)
-    own = scattered_sum(own, ("x",)).astype(jnp.bfloat16)
-    own = scattered_sum(own, ("y",)).astype(jnp.bfloat16)
+    own = scattered_sum(own, ("x", "y")).astype(jnp.bfloat16)
     parts = spread(own, DEEP)
     own = (jnp.sum(parts.astype(jnp.float32), axis=0) * grad_scale).astype(jnp.bfloat16)
     own = spread(own, ("y",)).reshape(-1, 128)
@@ -401,14 +407,13 @@
     lon_near_ref,
     lat_far_ref,
     lat_near_ref,
-    table_ref,
-    qkv_hbm,
-    proj_hbm,
-    up_hbm,
-    down_hbm,
-    conv_hbm,
-    gain_one_hbm,
-    gain_two_hbm,
+    bias_ref,
+    gains_ref,
+    qkv_ref,
+    proj_ref,
+    up_ref,
+    down_ref,
+    conv_ref,
     down_out_ref,
     grad_tokens_ref,
     kept_ref,
@@ -429,27 +434,7 @@
     grad_att_s,
     grad_qkv_s,
     message_s,
-    qkv_ref,
-    proj_ref,
-    up_ref,
-    down_ref,
-    conv_ref,
-    gain_one_ref,
-    gain_two_ref,
-    sems,
 ):
-    copies = fetched(
-        (
-            (qkv_hbm, qkv_ref),
-            (gain_one_hbm, gain_one_ref),
-            (gain_two_hbm, gain_two_ref),
-            (proj_hbm, proj_ref),
-            (up_hbm, up_ref),
-            (down_hbm, down_ref),
-            (conv_hbm, conv_ref),
-        ),
-        sems,
-    )
     own_rows, own_cols = tokens_ref.shape[0], tokens_ref.shape[1]
     first_col = place_along(LAT) * own_cols
     labels = assembled(
@@ -485,10 +470,8 @@
         lax.broadcasted_iota(jnp.int32, (AREA, HEADS * AREA), 1) % AREA
         == lax.broadcasted_iota(jnp.int32, (AREA, HEADS * AREA), 0)
     )
-    biases = bias_rows(table_ref)
-    for copy in copies:
-        copy.wait()
-    gain_one, gain_two = gain_one_ref[...], gain_two_ref[...]
+    biases = bias_ref[...]
+    gain_one, gain_two = gains_ref[0:1, :], gains_ref[1:2, :]
     lane = lax.broadcasted_iota(jnp.int32, (AREA, 128), 1)
     head_lanes = [lane // HEAD_DIM == head for head in range(HEADS)]
     head_masks = [jnp.where(hit, 1.0, 0.0).astype(jnp.bfloat16) for hit in head_lanes]
@@ -497,7 +480,8 @@
     bias_sum = jnp.zeros((AREA, HEADS * AREA), jnp.float32)
     gain_one_sum = jnp.zeros((1, 128), jnp.float32)
     gain_two_sum = jnp.zeros((1, 128), jnp.float32)
-    for chunk in range(WIN_ROWS):
+    def chunk_steps(chunk):
+        nonlocal bias_sum, gain_one_sum, gain_two_sum
         top = chunk * WIN
         source = jnp.concatenate(
             [
@@ -514,38 +498,9 @@
             axis=0,
         )
         ln_one, normed_one, inverse_one = layer_norm(source, gain_one)
+        yield
         qkv_all = matmul(ln_one, qkv_ref[...]).astype(jnp.bfloat16)
-        saved, mixed_parts = [], []
-        for win in range(WIN_COLS):
-            part = qkv_all[win * AREA : (win + 1) * AREA]
-            query, key, value = part[:, :128], part[:, 128:256], part[:, 256:]
-            query_heads = by_heads(query, head_masks)
-            picked = jnp.where(lane == win * WIN + lane_row % WIN, label_rows, 0.0)
-            column = jnp.broadcast_to(
-                jnp.sum(picked, axis=1, keepdims=True), (AREA, HEADS * AREA)
-            )
-            across = jnp.sum(jnp.where(diagonal, column, 0.0), axis=0, keepdims=True)
-            allowed = column == across
-            scores = matmul_nt(key, query_heads) * score_scale + biases
-            scores = jnp.where(allowed, scores, -1e30)
-            raised = jnp.exp(scores - jnp.max(scores, axis=0, keepdims=True))
-            probabilities = raised * (1.0 / jnp.sum(raised, axis=0, keepdims=True))
-            weights = probabilities.astype(jnp.bfloat16)
-            mixed_parts.append(own_heads(matmul_tn(weights, value), head_lanes).astype(jnp.bfloat16))
-            saved.append((query_heads, key, value, probabilities, weights))
-        mixed = jnp.concatenate(mixed_parts, axis=0)
-        projected = matmul(mixed, proj_ref[...]).astype(jnp.bfloat16)
-        middle = source + projected.astype(jnp.float32)
-        ln_two, normed_two, inverse_two = layer_norm(middle, gain_two)
-        pre_act = matmul(ln_two, up_ref[...])
-        cumulative = 0.5 * (1.0 + lax.erf(pre_act * 0.7071067811865476))
-        hidden = (pre_act * cumulative).astype(jnp.bfloat16)
-        slope = cumulative + pre_act * (jnp.exp(-0.5 * pre_act * pre_act) * 0.3989422804014327)
-        block_out = (middle + matmul(hidden, down_ref[...])).astype(jnp.bfloat16).astype(jnp.float32)
-        for win in range(WIN_COLS):
-            piece = block_out[win * AREA : (win + 1) * AREA].reshape(WIN, WIN, 128)
-            block_out_s[top : top + WIN, win * WIN : (win + 1) * WIN, :] = piece
-
+        yield
         grad_grid = jnp.zeros((WIN * PAD_COLS, 128), jnp.float32)
         for tap in range(3):
             first = (top + 2 - tap) * PAD_COLS
@@ -559,31 +514,89 @@
             ],
             axis=0,
         )
+        saved, mixed_parts = [], []
+        raw = []
+        for win in range(WIN_COLS):
+            part = qkv_all[win * AREA : (win + 1) * AREA]
+            query, key, value = part[:, :128], part[:, 128:256], part[:, 256:]
+            query_heads = by_heads(query, head_masks)
+            picked = jnp.where(lane == win * WIN + lane_row % WIN, label_rows, 0.0)
+            column = jnp.broadcast_to(
+                jnp.sum(picked, axis=1, keepdims=True), (AREA, HEADS * AREA)
+            )
+            across = jnp.sum(jnp.where(diagonal, column, 0.0), axis=0, keepdims=True)
+            scores = matmul_nt(key, query_heads) * score_scale + biases
+            scores = jnp.where(column == across, scores, -1e30)
+            raw.append((query_heads, key, value, scores))
+        yield
+        for query_heads, key, value, scores in raw:
+            raised = jnp.exp(scores - jnp.max(scores, axis=0, keepdims=True))
+            probabilities = raised * (1.0 / jnp.sum(raised, axis=0, keepdims=True))
+            saved.append((query_heads, key, value, probabilities, probabilities.astype(jnp.bfloat16)))
+        yield
+        for query_heads, key, value, probabilities, weights in saved:
+            mixed_parts.append(own_heads(matmul_tn(weights, value), head_lanes).astype(jnp.bfloat16))
+        yield
+        mixed = jnp.concatenate(mixed_parts, axis=0)
+        projected = matmul(mixed, proj_ref[...]).astype(jnp.bfloat16)
+        yield
+        middle = source + projected.astype(jnp.float32)
+        ln_two, normed_two, inverse_two = layer_norm(middle, gain_two)
+        yield
+        pre_act = matmul(ln_two, up_ref[...])
+        yield
+        cumulative = 0.5 * (1.0 + lax.erf(pre_act * 0.7071067811865476))
+        hidden = (pre_act * cumulative).astype(jnp.bfloat16)
+        slope = cumulative + pre_act * (jnp.exp(-0.5 * pre_act * pre_act) * 0.3989422804014327)
+        yield
+        block_out = (middle + matmul(hidden, down_ref[...])).astype(jnp.bfloat16).astype(jnp.float32)
+        for win in range(WIN_COLS):
+            piece = block_out[win * AREA : (win + 1) * AREA].reshape(WIN, WIN, 128)
+            block_out_s[top : top + WIN, win * WIN : (win + 1) * WIN, :] = piece
+
+        yield
         grad_block_b = grad_block.astype(jnp.bfloat16)
         grad_hidden = matmul_nt(grad_block_b, down_ref[...])
+        yield
         grad_pre = (grad_hidden * slope).astype(jnp.bfloat16)
         grad_ln_two = matmul_nt(grad_pre, up_ref[...])
+        yield
         grad_middle = grad_block + layer_norm_back(grad_ln_two, normed_two, inverse_two, gain_two)
         grad_att = grad_middle.astype(jnp.bfloat16)
+        yield
         grad_mixed = matmul_nt(grad_att, proj_ref[...]).astype(jnp.bfloat16)
-        grad_parts = []
+        yield
+        grad_parts, steps_back = [], []
         for win in range(WIN_COLS):
             query_heads, key, value, probabilities, weights = saved[win]
             grad_heads = by_heads(grad_mixed[win * AREA : (win + 1) * AREA], head_masks)
             grad_probs = matmul_nt(value, grad_heads)
             grad_value = matmul(weights, grad_heads)
+            steps_back.append((grad_probs, grad_value))
+        yield
+        grads = []
+        for win in range(WIN_COLS):
+            probabilities = saved[win][3]
+            grad_probs = steps_back[win][0]
             centre = jnp.sum(probabilities * grad_probs, axis=0, keepdims=True)
             grad_scores = probabilities * (grad_probs - centre)
             if chunk and win:
                 bias_sum = bias_sum + grad_scores
-            grad_scores_b = grad_scores.astype(jnp.bfloat16)
-            grad_key = matmul(grad_scores_b, query_heads) * score_scale
-            grad_query = own_heads(matmul_tn(grad_scores_b, key), head_lanes) * score_scale
+            grads.append(grad_scores.astype(jnp.bfloat16))
+        yield
+        for win in range(WIN_COLS):
+            query_heads, key = saved[win][:2]
+            grad_key = matmul(grads[win], query_heads) * score_scale
+            grad_query = own_heads(matmul_tn(grads[win], key), head_lanes) * score_scale
             grad_parts.append(
-                jnp.concatenate([grad_query, grad_key, grad_value], axis=1).astype(jnp.bfloat16)
+                jnp.concatenate([grad_query, grad_key, steps_back[win][1]], axis=1).astype(
+                    jnp.bfloat16
+                )
             )
+        yield
         grad_qkv = jnp.concatenate(grad_parts, axis=0)
         grad_ln_one = matmul_nt(grad_qkv, qkv_ref[...])
+        yield
         grad_tokens = grad_middle + layer_norm_back(grad_ln_one, normed_one, inverse_one, gain_one)
         for win in range(WIN_COLS):
             piece = grad_tokens[win * AREA : (win + 1) * AREA].reshape(WIN, WIN, 128)
@@ -604,6 +617,11 @@
             mixed_s[kept, :] = mixed[AREA:]
             grad_att_s[kept, :] = grad_att[AREA:]
             grad_qkv_s[kept, :] = grad_qkv[AREA:]
+
+
+    running = [chunk_steps(chunk) for chunk in range(WIN_ROWS)]
+    while running:
+        running = [steps for steps in running if next(steps, running) is not running]
 
     col = first_col + lax.broadcasted_iota(jnp.int32, (own_cols, 128), 0)
     keeps = (col != 0, None, col != lat_total - 1)
@@ -674,6 +692,14 @@
     held = lambda *shape: pltpu.VMEM(shape, jnp.bfloat16)
     wide = lambda *shape: pltpu.VMEM(shape, jnp.float32)
     table = jnp.pad(position_bias, ((0, 0), (0, 1), (0, 1))).reshape(HEADS, 256)
+    biases, gains = pl.pallas_call(
+        bias_kernel,
+        out_shape=(f32(AREA, HEADS * AREA), f32(WIN, width)),
+        in_specs=[vmem] * 3,
+        out_specs=(vmem,) * 2,
+        compiler_params=params,
+        cost_estimate=pl.CostEstimate(flops=10_000_000, bytes_accessed=80_000, transcendentals=0),
+    )(table, gain_one[None], gain_two[None])
     slabs = TOKEN_RIM + GRAD_RIM + 1
     anywhere = pl.BlockSpec(memory_space=pltpu.HBM)
     far, near, tokens, grad_out, window_ids = pl.pallas_call(
@@ -716,7 +742,7 @@
             bf16(ROWS // 2, width),
             bf16(ROWS // 2, width),
         ),
-        in_specs=[vmem] * 8 + [anywhere] * 7,
+        in_specs=[vmem] * 14,
         out_specs=(vmem,) * 4,
         scratch_shapes=[
             wide(TOKEN_ROWS, 48, width),
@@ -735,14 +761,6 @@
             held(count, width),
             held(count, 3 * width),
             wide(2, MESSAGE, width),
-            held(*qkv_weight.shape),
-            held(*proj_weight.shape),
-            held(*up_weight.shape),
-            held(*down_weight.shape),
-            held(*conv_weight.shape),
-            wide(1, width),
-            wide(1, width),
-            pltpu.SemaphoreType.DMA((7,)),
         ],
         compiler_params=params,
         cost_estimate=pl.CostEstimate(
@@ -756,14 +774,13 @@
         lon_near,
         lat_far,
         lat_near,
-        table,
+        biases,
+        gains,
         qkv_weight,
         proj_weight,
         up_weight,
         down_weight,
         conv_weight,
-        gain_one[None],
-        gain_two[None],
     )
     own, other = total_over_devices(kept, sent, 1.0 / math.sqrt(tokens_all))
     results = pl.pallas_call(

time: 126 us -> 117 us (0.929)
  Pallas kernels: 15 us -> 8.68 us
  blocking collectives: 54.6 us -> 53.1 us
    pallas_call x1, Pallas kernels: 13.4 us -> 6.71 us  [per_device(): pl.pallas_call(functools.partial(block_kernel, lat_total), out_shape=(bf1...]
    all_to_all x2 -> x1, blocking collectives: 20.3 us -> 15.3 us  [scattered_sum(): received = lax.all_to_all(chunks, axes, 0, 0, tiled=True)]
    all_to_all x3, blocking collectives: 34.3 us -> 37.8 us  [spread(): return lax.all_to_all(copies, axes, 0, 0, tiled=True)]
where the time goes in v5:
time: 117 us
  blocking collectives  53.1 us (45%)
  starting transfers between devices  45 us (38%)
  Pallas kernels  8.68 us (7%)
  waiting for transfers between devices  6.38 us (5%)
  local copies, waits for them, and re-layouts  2.72 us (2%)
    all_to_all x3, blocking collectives, spread(): return lax.all_to_all(copies, axes, 0, 0, tiled=True)  37.8 us
    ppermute x4, starting transfers between devices, swapped(): return lax.ppermute(value, axes, pairs)  32.6 us
    all_to_all x1, blocking collectives, scattered_sum(): received = lax.all_to_all(chunks, axes, 0, 0, tiled=True)  15.3 us
    ppermute x1, starting transfers between devices, total_over_devices(): return (own, lax.ppermute(own, 'c', cores))  8.72 us
    pallas_call x1, Pallas kernels, per_device(): pl.pallas_call(functools.partial(block_kernel, lat_total), out_shape=(bf1...  6.71 us
    ppermute x4, waiting for transfers between devices, swapped(): return lax.ppermute(value, axes, pairs)  3.73 us
    ppermute x1, starting transfers between devices, total_over_devices(): other = lax.ppermute(sent, 'c', cores)  3.65 us
    unnamed x23, local copies, waits for them, and re-layouts  2.53 us
  transfers between devices with their start and end apart: 6, of which 4 were waited for; matrix products, arithmetic and copies ran while one was open for 0% of the time, Pallas kernels for 0%

profile of v5, /device:TPU:1, one launch (start us, length us, event | category | flops | bytes accessed | tf_op | source)
XLA Modules:
  0.0 116.9 jit_solution(8564815915541258677)
XLA Ops:
  0.6 0.0 copy-start
  0.7 0.9 copy-done
  1.6 0.9 copy-done.1
  2.5 0.7 copy-done.2
  3.2 0.4 shard_map.186
  3.6 0.0 copy-start.6
  3.6 4.6 %collective-permute-start = (bf16[10,32,128]{2,1,0:T(8,128)(2,1)S(1)}, bf16[10,32,128]{2,1,0:T(8,128)(2,1)S(1)}, u32[]{:S(2)}, u32[]{:S(2)}) collective-permute-start(bf16[10,32,128]{2,1,0:T(8,128)(2,1)S(1)} %get-tuple-element.34), channel_id=1, source_target_pairs={{0,752},{16,32},{32,16},{48,64},{64,48},{80,96},{96,80},{112,128},... | collective-permute-start | bytes 245768 | tf_op jit(solution)/shard_map/ppermute | solution.py:44
  8.2 13.3 %collective-permute-start.1 = (bf16[10,32,128]{2,1,0:T(8,128)(2,1)S(1)}, bf16[10,32,128]{2,1,0:T(8,128)(2,1)S(1)}, u32[]{:S(2)}, u32[]{:S(2)}) collective-permute-start(bf16[10,32,128]{2,1,0:T(8,128)(2,1)S(1)} %get-tuple-element.35), channel_id=1, source_target_pairs={{0,16},{16,0},{32,48},{48,32},{64,80},{80,64},{96,112},{112,96},{1... | collective-permute-start | bytes 245768 | tf_op jit(solution)/shard_map/ppermute | solution.py:44
  21.5 0.0 collective-permute-done.lon_far_ref
  21.5 0.9 collective-permute-done.1.lon_near_ref
  22.4 0.1 shard_map.187
  22.5 12.8 %collective-permute-start.2 = (bf16[240,128]{1,0:T(8,128)(2,1)S(1)}, bf16[240,128]{1,0:T(8,128)(2,1)S(1)}, u32[]{:S(2)}, u32[]{:S(2)}) collective-permute-start(bf16[240,128]{1,0:T(8,128)(2,1)S(1)} %get-tuple-element.36), channel_id=1, source_target_pairs={{0,15},{1,2},{2,1},{3,4},{4,3},{5,6},{6,5},{7,8},{8,7},{9,10},{10,... | collective-permute-start | bytes 184328 | tf_op jit(solution)/shard_map/ppermute | solution.py:44
  35.3 1.9 %collective-permute-start.3 = (bf16[240,128]{1,0:T(8,128)(2,1)S(1)}, bf16[240,128]{1,0:T(8,128)(2,1)S(1)}, u32[]{:S(2)}, u32[]{:S(2)}) collective-permute-start(bf16[240,128]{1,0:T(8,128)(2,1)S(1)} %get-tuple-element.37), channel_id=1, source_target_pairs={{0,1},{1,0},{2,3},{3,2},{4,5},{5,4},{6,7},{7,6},{8,9},{9,8},{10,11... | collective-permute-start | bytes 184328 | tf_op jit(solution)/shard_map/ppermute | solution.py:44
  37.2 0.0 copy-done.10
  37.3 0.1 reshape.35.table_ref
  37.4 0.3 shard_map.188
  37.7 0.0 collective-permute-done.2.lat_far_ref
  37.7 2.8 %collective-permute-done.3.lat_near_ref = bf16[240,128]{1,0:T(8,128)(2,1)S(1)} collective-permute-done((bf16[240,128]{1,0:T(8,128)(2,1)S(1)}, bf16[240,128]{1,0:T(8,128)(2,1)S(1)}, u32[]{:S(2)}, u32[]{:S(2)}) %collective-permute-start.3) | collective-permute-done | bytes 61472 | tf_op jit(solution)/shard_map/ppermute | solution.py:44
  40.6 0.0 copy-done.7
  40.6 6.7 %shard_map.189 = (bf16[16,32,128]{2,1,0:T(8,128)(2,1)}, bf16[16,32,128]{2,1,0:T(8,128)(2,1)}, bf16[1536,128]{1,0:T(8,128)(2,1)S(1)}, bf16[1536,128]{1,0:T(8,128)(2,1)S(1)}) custom-call(bf16[16,32,128]{2,1,0:T(8,128)(2,1)S(1)} %get-tuple-element.31.tokens_ref, bf16[16,32,128]{2,1,0:T(8,128)(2,1)S(1)} %get-tuple-element.32.grad_ref, ...), custom_call_target="tpu_custom_call" | custom-call | flops 3000000000 | bytes 8000000 | tf_op jit(solution)/shard_map/pallas_call | solution.py:737
  47.3 3.7 %collective-permute-start.4 = (bf16[1536,128]{1,0:T(8,128)(2,1)S(1)}, bf16[1536,128]{1,0:T(8,128)(2,1)S(1)}, u32[]{:S(2)}, u32[]{:S(2)}) collective-permute-start(bf16[1536,128]{1,0:T(8,128)(2,1)S(1)} %get-tuple-element.43), channel_id=1, source_target_pairs={{0,16},{16,0},{1,17},{17,1},{2,18},{18,2},{3,19},{19,3},{4,20},{20... | collective-permute-start | bytes 1179656 | tf_op jit(solution)/shard_map/ppermute | solution.py:275
  51.0 1.3 %collective-permute-done.4 = bf16[1536,128]{1,0:T(8,128)(2,1)S(1)} collective-permute-done((bf16[1536,128]{1,0:T(8,128)(2,1)S(1)}, bf16[1536,128]{1,0:T(8,128)(2,1)S(1)}, u32[]{:S(2)}, u32[]{:S(2)}) %collective-permute-start.4) | collective-permute-done | bytes 393248 | tf_op jit(solution)/shard_map/ppermute | solution.py:275
  52.3 0.1 add_convert_fusion
  52.4 15.3 %all_to_all.20 = bf16[32,48,128]{2,1,0:T(8,128)(2,1)S(1)} all-to-all(bf16[32,48,128]{2,1,0:T(8,128)(2,1)S(1)} %bitcast.12), channel_id=1, replica_groups=mesh['zl'=6,'x'=4,'c'=2,'zh'=2,'y'=8] {'x','y'}, dimensions={0} | all-to-all | bytes 786432 | tf_op jit(solution)/shard_map/all_to_all | solution.py:263
  67.7 0.1 reduce_sum.21
  67.8 15.9 %all_to_all.21 = bf16[12,48,128]{2,1,0:T(8,128)(2,1)S(1)} all-to-all(bf16[12,48,128]{2,1,0:T(8,128)(2,1)S(1)} %broadcast_in_dim.27), channel_id=1, replica_groups=mesh['zl'=6,'x'=4,'c'=2,'zh'=2,'y'=8] {'zl','zh'}, dimensions={0} | all-to-all | bytes 294912 | tf_op jit(solution)/shard_map/all_to_all | solution.py:270
  83.8 13.2 %all_to_all.22 = bf16[8,48,128]{2,1,0:T(8,128)(2,1)S(1)} all-to-all(bf16[8,48,128]{2,1,0:T(8,128)(2,1)S(1)} %broadcast_in_dim.28), channel_id=1, replica_groups=mesh['zl'=6,'x'=4,'c'=2,'zh'=2,'y'=8] {'y'}, dimensions={0} | all-to-all | bytes 196608 | tf_op jit(solution)/shard_map/all_to_all | solution.py:270
  97.0 0.1 broadcast_in_dim.30
  97.1 8.6 %all_to_all.23 = bf16[4,384,128]{2,1,0:T(8,128)(2,1)S(1)} all-to-all(bf16[4,384,128]{2,1,0:T(8,128)(2,1)S(1)} %broadcast_in_dim.30), channel_id=1, replica_groups=mesh['zl'=6,'x'=4,'c'=2,'zh'=2,'y'=8] {'x'}, dimensions={0} | all-to-all | bytes 786432 | tf_op jit(solution)/shard_map/all_to_all | solution.py:270
  105.7 8.7 %collective-permute-start.5 = (bf16[1536,128]{1,0:T(8,128)(2,1)S(1)}, bf16[1536,128]{1,0:T(8,128)(2,1)S(1)}, u32[]{:S(2)}, u32[]{:S(2)}) collective-permute-start(bf16[1536,128]{1,0:T(8,128)(2,1)S(1)} %bitcast.8), channel_id=1, source_target_pairs={{0,16},{16,0},{1,17},{17,1},{2,18},{18,2},{3,19},{19,3},{4,20},{20... | collective-permute-start | bytes 1179656 | tf_op jit(solution)/shard_map/ppermute | solution.py:282
  114.4 1.3 %collective-permute-done.5.other_ref = bf16[1536,128]{1,0:T(8,128)(2,1)S(1)} collective-permute-done((bf16[1536,128]{1,0:T(8,128)(2,1)S(1)}, bf16[1536,128]{1,0:T(8,128)(2,1)S(1)}, u32[]{:S(2)}, u32[]{:S(2)}) %collective-permute-start.5) | collective-permute-done | bytes 393248 | tf_op jit(solution)/shard_map/ppermute | solution.py:282
  115.7 1.1 shard_map.190
  (21 shorter events, 0.1 us)
Async XLA Ops:
  0.6 0.9 copy-start
  1.5 0.9 copy-start.1
  2.5 0.7 copy-start.2
  3.2 34.1 %copy-start.10 = (f32[4,15,15]{2,0,1:T(4,128)S(1)}, f32[4,15,15]{2,0,1:T(4,128)}, u32[]{:S(2)}) copy-start(f32[4,15,15]{2,0,1:T(4,128)} %param.21) | copy-start | bytes 10804
  3.2 37.4 %copy-start.7 = (bf16[128,128]{1,0:T(8,128)(2,1)S(1)}, bf16[128,128]{1,0:T(8,128)(2,1)}, u32[]{:S(2)}) copy-start(bf16[128,128]{1,0:T(8,128)(2,1)} %proj_ref.1) | copy-start | bytes 98308
  3.6 37.0 %copy-start.6 = (bf16[128,384]{1,0:T(8,128)(2,1)S(1)}, bf16[128,384]{1,0:T(8,128)(2,1)}, u32[]{:S(2)}) copy-start(bf16[128,384]{1,0:T(8,128)(2,1)} %qkv_ref.1) | copy-start | bytes 294916
  3.6 17.9 %collective-permute-start = (bf16[10,32,128]{2,1,0:T(8,128)(2,1)S(1)}, bf16[10,32,128]{2,1,0:T(8,128)(2,1)S(1)}, u32[]{:S(2)}, u32[]{:S(2)}) collective-permute-start(bf16[10,32,128]{2,1,0:T(8,128)(2,1)S(1)} %get-tuple-element.34), channel_id=1, source_target_pairs={{0,752},{16,32},{32,16},{48,64},{64,48},{80,96},{96,80},{112,128},... | collective-permute-start | bytes 245768 | tf_op jit(solution)/shard_map/ppermute | solution.py:44
  8.2 14.2 %collective-permute-start.1 = (bf16[10,32,128]{2,1,0:T(8,128)(2,1)S(1)}, bf16[10,32,128]{2,1,0:T(8,128)(2,1)S(1)}, u32[]{:S(2)}, u32[]{:S(2)}) collective-permute-start(bf16[10,32,128]{2,1,0:T(8,128)(2,1)S(1)} %get-tuple-element.35), channel_id=1, source_target_pairs={{0,16},{16,0},{32,48},{48,32},{64,80},{80,64},{96,112},{112,96},{1... | collective-permute-start | bytes 245768 | tf_op jit(solution)/shard_map/ppermute | solution.py:44
  22.4 15.0 %copy-start.8 = (f32[128]{0:T(128)S(1)}, f32[128]{0:T(128)}, u32[]{:S(2)}) copy-start(f32[128]{0:T(128)} %param.19) | copy-start | bytes 1540
  22.4 15.0 %copy-start.9 = (f32[128]{0:T(128)S(1)}, f32[128]{0:T(128)}, u32[]{:S(2)}) copy-start(f32[128]{0:T(128)} %param.20) | copy-start | bytes 1540
  22.4 18.2 %copy-start.3 = (bf16[9,128,128]{2,1,0:T(8,128)(2,1)S(1)}, bf16[9,128,128]{2,1,0:T(8,128)(2,1)}, u32[]{:S(2)}) copy-start(bf16[9,128,128]{2,1,0:T(8,128)(2,1)} %conv_ref.1) | copy-start | bytes 884740
  22.4 18.2 %copy-start.5 = (bf16[512,128]{1,0:T(8,128)(2,1)S(1)}, bf16[512,128]{1,0:T(8,128)(2,1)}, u32[]{:S(2)}) copy-start(bf16[512,128]{1,0:T(8,128)(2,1)} %down_ref.1) | copy-start | bytes 393220
  22.5 18.1 %copy-start.4 = (bf16[128,512]{1,0:T(8,128)(2,1)S(1)}, bf16[128,512]{1,0:T(8,128)(2,1)}, u32[]{:S(2)}) copy-start(bf16[128,512]{1,0:T(8,128)(2,1)} %up_ref.1) | copy-start | bytes 393220
  22.5 15.2 %collective-permute-start.2 = (bf16[240,128]{1,0:T(8,128)(2,1)S(1)}, bf16[240,128]{1,0:T(8,128)(2,1)S(1)}, u32[]{:S(2)}, u32[]{:S(2)}) collective-permute-start(bf16[240,128]{1,0:T(8,128)(2,1)S(1)} %get-tuple-element.36), channel_id=1, source_target_pairs={{0,15},{1,2},{2,1},{3,4},{4,3},{5,6},{6,5},{7,8},{8,7},{9,10},{10,... | collective-permute-start | bytes 184328 | tf_op jit(solution)/shard_map/ppermute | solution.py:44
  35.3 5.3 %collective-permute-start.3 = (bf16[240,128]{1,0:T(8,128)(2,1)S(1)}, bf16[240,128]{1,0:T(8,128)(2,1)S(1)}, u32[]{:S(2)}, u32[]{:S(2)}) collective-permute-start(bf16[240,128]{1,0:T(8,128)(2,1)S(1)} %get-tuple-element.37), channel_id=1, source_target_pairs={{0,1},{1,0},{2,3},{3,2},{4,5},{5,4},{6,7},{7,6},{8,9},{9,8},{10,11... | collective-permute-start | bytes 184328 | tf_op jit(solution)/shard_map/ppermute | solution.py:44
  47.3 5.0 %collective-permute-start.4 = (bf16[1536,128]{1,0:T(8,128)(2,1)S(1)}, bf16[1536,128]{1,0:T(8,128)(2,1)S(1)}, u32[]{:S(2)}, u32[]{:S(2)}) collective-permute-start(bf16[1536,128]{1,0:T(8,128)(2,1)S(1)} %get-tuple-element.43), channel_id=1, source_target_pairs={{0,16},{16,0},{1,17},{17,1},{2,18},{18,2},{3,19},{19,3},{4,20},{20... | collective-permute-start | bytes 1179656 | tf_op jit(solution)/shard_map/ppermute | solution.py:275
  105.7 10.1 %collective-permute-start.5 = (bf16[1536,128]{1,0:T(8,128)(2,1)S(1)}, bf16[1536,128]{1,0:T(8,128)(2,1)S(1)}, u32[]{:S(2)}, u32[]{:S(2)}) collective-permute-start(bf16[1536,128]{1,0:T(8,128)(2,1)S(1)} %bitcast.8), channel_id=1, source_target_pairs={{0,16},{16,0},{1,17},{17,1},{2,18},{18,2},{3,19},{19,3},{4,20},{20... | collective-permute-start | bytes 1179656 | tf_op jit(solution)/shard_map/ppermute | solution.py:282

commit v6 on v5

--- a/solution.py
+++ b/solution.py
@@ -18,7 +18,7 @@
 WIN_ROWS = 3
 WIN_COLS = 5
 PAD_COLS = 48
-ROWS = 3072
+ROWS = 2816
 TOKEN_RIM = 4
 GRAD_RIM = 5
 LABEL_RIM = 8
@@ -55,33 +55,16 @@
     return jnp.where(choice, jnp.int32(first), jnp.int32(second))
 
 
-def fetched(pairs, sems):
-    copies = [
-        pltpu.make_async_copy(source, target, sems.at[place])
-        for place, (source, target) in enumerate(pairs)
-    ]
-    for copy in copies:
-        copy.start()
-    return copies
-
-
-def lon_pack_kernel(
-    tokens_hbm, grad_hbm, ids_hbm, far_ref, near_ref, tokens_ref, grad_ref, ids_ref, ids_s, sems
-):
-    copies = fetched(
-        ((tokens_hbm, tokens_ref), (grad_hbm, grad_ref), (ids_hbm, ids_ref)), sems
-    )
+def lon_pack_kernel(fields_ref, ids_ref, far_ref, near_ref, ids_s):
     even = place_along(LON) % 2 == 0
-    rows = tokens_ref.shape[0]
+    rows, cols = ids_ref.shape
     ids_s[...] = jnp.zeros_like(ids_s)
-    for copy in copies:
-        copy.wait()
-    ids_s[0:LABEL_RIM, 0 : ids_ref.shape[1]] = ids_ref[rows - LABEL_RIM :, :].astype(jnp.float32)
+    ids_s[0:LABEL_RIM, 0:cols] = ids_ref[rows - LABEL_RIM :, :].astype(jnp.float32)
     ids = ids_s[...].astype(jnp.bfloat16)
     for ref, upper in ((near_ref, even), (far_ref, jnp.logical_not(even))):
-        ref[0:TOKEN_RIM] = tokens_ref[pl.ds(either(upper, rows - TOKEN_RIM, 0), TOKEN_RIM)]
-        ref[TOKEN_RIM : TOKEN_RIM + GRAD_RIM] = grad_ref[
-            pl.ds(either(upper, rows - GRAD_RIM, 0), GRAD_RIM)
+        ref[0:TOKEN_RIM] = fields_ref[0, pl.ds(either(upper, rows - TOKEN_RIM, 0), TOKEN_RIM)]
+        ref[TOKEN_RIM : TOKEN_RIM + GRAD_RIM] = fields_ref[
+            1, pl.ds(either(upper, rows - GRAD_RIM, 0), GRAD_RIM)
         ]
         ref[TOKEN_RIM + GRAD_RIM] = ids
 
@@ -99,8 +82,7 @@
 
 
 def lat_pack_kernel(
-    tokens_ref,
-    grad_ref,
+    fields_ref,
     ids_ref,
     lon_far_ref,
     lon_near_ref,
@@ -113,7 +95,7 @@
 ):
     lon_even = place_along(LON) % 2 == 0
     lat_even = place_along(LAT) % 2 == 0
-    cols = tokens_ref.shape[1]
+    cols = fields_ref.shape[2]
 
     def edges(scratch, row, values):
         values = values.astype(jnp.float32)
@@ -121,8 +103,8 @@
         scratch[0, pl.ds(row, count)] = values[:, 0:WIN]
         scratch[1, pl.ds(row, count)] = values[:, cols - WIN :]
 
-    edges(tokens_s, TOKEN_RIM, tokens_ref[...])
-    edges(grad_s, GRAD_RIM, grad_ref[...])
+    edges(tokens_s, TOKEN_RIM, fields_ref[0])
+    edges(grad_s, GRAD_RIM, fields_ref[1])
     split = TOKEN_RIM + GRAD_RIM
     for ref, below in ((lon_near_ref, lon_even), (lon_far_ref, jnp.logical_not(lon_even))):
         edges(tokens_s, either(below, TOKEN_ROWS - TOKEN_RIM, 0), ref[0:TOKEN_RIM])
@@ -155,8 +137,7 @@
 
 
 def assembled(
-    tokens_ref,
-    grad_ref,
+    fields_ref,
     ids_ref,
     lon_near_ref,
     lon_far_ref,
@@ -171,10 +152,10 @@
 ):
     lon_even = place_along(LON) % 2 == 0
     lat_even = place_along(LAT) % 2 == 0
-    rows, cols = tokens_ref.shape[0], tokens_ref.shape[1]
+    rows, cols = ids_ref.shape
     middle = slice(WIN, WIN + cols)
-    tokens_s[TOKEN_RIM : TOKEN_RIM + rows, middle, :] = tokens_ref[...].astype(jnp.float32)
-    grad_s[GRAD_RIM : GRAD_RIM + rows, middle, :] = grad_ref[...].astype(jnp.float32)
+    tokens_s[TOKEN_RIM : TOKEN_RIM + rows, middle, :] = fields_ref[0].astype(jnp.float32)
+    grad_s[GRAD_RIM : GRAD_RIM + rows, middle, :] = fields_ref[1].astype(jnp.float32)
     split = TOKEN_RIM + GRAD_RIM
     for ref, below in ((lon_near_ref, lon_even), (lon_far_ref, jnp.logical_not(lon_even))):
         row = either(below, TOKEN_ROWS - TOKEN_RIM, 0)
@@ -259,7 +240,7 @@
 
 def scattered_sum(partial, axes):
     count = lax.axis_size(axes)
-    chunks = partial.reshape(count, partial.shape[0] // count, partial.shape[1])
+    chunks = partial.reshape(count, -1, 4, partial.shape[-1])
     received = lax.all_to_all(chunks, axes, 0, 0, tiled=True)
     return jnp.sum(received.astype(jnp.float32), axis=0)
 
@@ -277,8 +258,7 @@
     own = scattered_sum(own, ("x", "y")).astype(jnp.bfloat16)
     parts = spread(own, DEEP)
     own = (jnp.sum(parts.astype(jnp.float32), axis=0) * grad_scale).astype(jnp.bfloat16)
-    own = spread(own, ("y",)).reshape(-1, 128)
-    own = spread(own, ("x",)).reshape(-1, 128)
+    own = spread(own, ("x", "y")).reshape(-1, 128)
     return own, lax.ppermute(own, "c", cores)
 
 
@@ -400,8 +380,7 @@
 
 def block_kernel(
     lat_total,
-    tokens_ref,
-    grad_ref,
+    fields_ref,
     ids_ref,
     lon_far_ref,
     lon_near_ref,
@@ -435,11 +414,10 @@
     grad_qkv_s,
     message_s,
 ):
-    own_rows, own_cols = tokens_ref.shape[0], tokens_ref.shape[1]
+    own_rows, own_cols = ids_ref.shape
     first_col = place_along(LAT) * own_cols
     labels = assembled(
-        tokens_ref,
-        grad_ref,
+        fields_ref,
         ids_ref,
         lon_near_ref,
         lon_far_ref,
@@ -634,7 +612,7 @@
     patches = jnp.concatenate(shifted, axis=1)
     count = own_rows * own_cols
     downscaled = jnp.zeros((count, 128), jnp.float32)
-    grad_own = grad_ref[...].reshape(count, 128)
+    grad_own = fields_ref[1].reshape(count, 128)
     for tap in range(3):
         rows = patches[tap * own_cols : tap * own_cols + count]
         downscaled = downscaled + matmul(rows, conv_ref[3 * tap : 3 * tap + 3].reshape(384, 128))
@@ -701,27 +679,21 @@
         cost_estimate=pl.CostEstimate(flops=10_000_000, bytes_accessed=80_000, transcendentals=0),
     )(table, gain_one[None], gain_two[None])
     slabs = TOKEN_RIM + GRAD_RIM + 1
-    anywhere = pl.BlockSpec(memory_space=pltpu.HBM)
-    far, near, tokens, grad_out, window_ids = pl.pallas_call(
+    fields = jnp.stack([tokens, grad_out])
+    far, near = pl.pallas_call(
         lon_pack_kernel,
-        out_shape=(
-            bf16(slabs, col_count, width),
-            bf16(slabs, col_count, width),
-            bf16(*tokens.shape),
-            bf16(*grad_out.shape),
-            jax.ShapeDtypeStruct(window_ids.shape, jnp.int32),
-        ),
-        in_specs=[anywhere] * 3,
-        out_specs=(vmem,) * 5,
-        scratch_shapes=[wide(col_count, width), pltpu.SemaphoreType.DMA((3,))],
+        out_shape=(bf16(slabs, col_count, width),) * 2,
+        in_specs=[vmem] * 2,
+        out_specs=(vmem,) * 2,
+        scratch_shapes=[wide(col_count, width)],
         compiler_params=params,
-    )(tokens, grad_out, window_ids)
+    )(fields, window_ids)
     lon_far = swapped(far, LON, False)
     lon_near = swapped(near, LON, True)
     far, near = pl.pallas_call(
         lat_pack_kernel,
         out_shape=(bf16(MESSAGE, width),) * 2,
-        in_specs=[vmem] * 5,
+        in_specs=[vmem] * 4,
         out_specs=(vmem,) * 2,
         scratch_shapes=[
             wide(2, TOKEN_ROWS, WIN, width),
@@ -730,7 +702,7 @@
             wide(2, MESSAGE, width),
         ],
         compiler_params=params,
-    )(tokens, grad_out, window_ids, lon_far, lon_near)
+    )(fields, window_ids, lon_far, lon_near)
     lat_far = swapped(far, LAT, False)
     lat_near = swapped(near, LAT, True)
     count = AREA * (WIN_ROWS - 1) * (WIN_COLS - 1)
@@ -742,7 +714,7 @@
             bf16(ROWS // 2, width),
             bf16(ROWS // 2, width),
         ),
-        in_specs=[vmem] * 14,
+        in_specs=[vmem] * 13,
         out_specs=(vmem,) * 4,
         scratch_shapes=[
             wide(TOKEN_ROWS, 48, width),
@@ -767,8 +739,7 @@
             flops=3_000_000_000, bytes_accessed=8_000_000, transcendentals=2_000_000
         ),
     )(
-        tokens,
-        grad_out,
+        fields,
         window_ids,
         lon_far,
         lon_near,

time: 117 us -> 109 us (0.932)
  blocking collectives: 53.1 us -> 47.5 us
  local copies, waits for them, and re-layouts: 2.72 us -> 0.93 us
  starting transfers between devices: 45 us -> 43.3 us
    all_to_all x3 -> x2, blocking collectives: 37.8 us -> 32.8 us  [spread(): return lax.all_to_all(copies, axes, 0, 0, tiled=True)]
    unnamed x23 -> x19, local copies, waits for them, and re-layouts: 2.53 us -> 0.7 us
    ppermute x1, starting transfers between devices: 8.72 us -> 7.22 us  [total_over_devices(): return (own, lax.ppermute(own, 'c', cores))]
where the time goes in v6:
time: 109 us; the launch traced here: 108 us
  blocking collectives  47.5 us (44%)
  starting transfers between devices  43.3 us (40%)
  Pallas kernels  8.31 us (8%)
  waiting for transfers between devices  5.62 us (5%)
  other arithmetic  1.34 us (1%)
    all_to_all x2, blocking collectives, spread(): return lax.all_to_all(copies, axes, 0, 0, tiled=True)  32.8 us
    ppermute x4, starting transfers between devices, swapped(): return lax.ppermute(value, axes, pairs)  32.6 us
    all_to_all x1, blocking collectives, scattered_sum(): received = lax.all_to_all(chunks, axes, 0, 0, tiled=True)  14.7 us
    ppermute x1, starting transfers between devices, total_over_devices(): return (own, lax.ppermute(own, 'c', cores))  7.22 us
    pallas_call x1, Pallas kernels, per_device(): pl.pallas_call(functools.partial(block_kernel, lat_total), out_shape=(bf1...  6.7 us
    ppermute x1, starting transfers between devices, total_over_devices(): other = lax.ppermute(sent, 'c', cores)  3.49 us
    ppermute x4, waiting for transfers between devices, swapped(): return lax.ppermute(value, axes, pairs)  3.06 us
  transfers between devices with their start and end apart: 6, of which 4 were waited for; matrix products, arithmetic and copies ran while one was open for 0% of the time, Pallas kernels for 0%

profile of v6, /device:TPU:1, one launch (start us, length us, event | category | flops | bytes accessed | tf_op | source)
XLA Modules:
  0.0 107.9 jit_solution(10967474282588573570)
XLA Ops:
  0.6 0.0 copy-start
  0.7 1.0 pad_maximum_fusion.fields_ref
  1.7 0.0 copy-start.8
  1.7 0.0 copy-start.4
  1.7 4.5 %collective-permute-start = (bf16[10,32,128]{2,1,0:T(8,128)(2,1)S(1)}, bf16[10,32,128]{2,1,0:T(8,128)(2,1)S(1)}, u32[]{:S(2)}, u32[]{:S(2)}) collective-permute-start(bf16[10,32,128]{2,1,0:T(8,128)(2,1)S(1)} %get-tuple-element.28), channel_id=1, source_target_pairs={{0,752},{16,32},{32,16},{48,64},{64,48},{80,96},{96,80},{112,128},... | collective-permute-start | bytes 245768 | tf_op jit(solution)/shard_map/ppermute | solution.py:44
  6.2 0.0 copy-start.1
  6.3 13.4 %collective-permute-start.1 = (bf16[10,32,128]{2,1,0:T(8,128)(2,1)S(1)}, bf16[10,32,128]{2,1,0:T(8,128)(2,1)S(1)}, u32[]{:S(2)}, u32[]{:S(2)}) collective-permute-start(bf16[10,32,128]{2,1,0:T(8,128)(2,1)S(1)} %get-tuple-element.29), channel_id=1, source_target_pairs={{0,16},{16,0},{32,48},{48,32},{64,80},{80,64},{96,112},{112,96},{1... | collective-permute-start | bytes 245768 | tf_op jit(solution)/shard_map/ppermute | solution.py:44
  19.7 0.0 collective-permute-done.lon_far_ref
  19.7 0.9 collective-permute-done.1.lon_near_ref
  20.6 0.1 shard_map.187
  20.7 12.8 %collective-permute-start.2 = (bf16[240,128]{1,0:T(8,128)(2,1)S(1)}, bf16[240,128]{1,0:T(8,128)(2,1)S(1)}, u32[]{:S(2)}, u32[]{:S(2)}) collective-permute-start(bf16[240,128]{1,0:T(8,128)(2,1)S(1)} %get-tuple-element.30), channel_id=1, source_target_pairs={{0,15},{1,2},{2,1},{3,4},{4,3},{5,6},{6,5},{7,8},{8,7},{9,10},{10,... | collective-permute-start | bytes 184328 | tf_op jit(solution)/shard_map/ppermute | solution.py:44
  33.5 1.9 %collective-permute-start.3 = (bf16[240,128]{1,0:T(8,128)(2,1)S(1)}, bf16[240,128]{1,0:T(8,128)(2,1)S(1)}, u32[]{:S(2)}, u32[]{:S(2)}) collective-permute-start(bf16[240,128]{1,0:T(8,128)(2,1)S(1)} %get-tuple-element.31), channel_id=1, source_target_pairs={{0,1},{1,0},{2,3},{3,2},{4,5},{5,4},{6,7},{7,6},{8,9},{9,8},{10,11... | collective-permute-start | bytes 184328 | tf_op jit(solution)/shard_map/ppermute | solution.py:44
  35.4 0.0 copy-start.5
  35.5 0.1 reshape.34.table_ref
  35.6 0.6 copy-done.6
  36.2 0.0 copy-done.7
  36.2 0.3 shard_map.188
  36.6 0.0 collective-permute-done.2.lat_far_ref
  36.6 2.2 %collective-permute-done.3.lat_near_ref = bf16[240,128]{1,0:T(8,128)(2,1)S(1)} collective-permute-done((bf16[240,128]{1,0:T(8,128)(2,1)S(1)}, bf16[240,128]{1,0:T(8,128)(2,1)S(1)}, u32[]{:S(2)}, u32[]{:S(2)}) %collective-permute-start.3) | collective-permute-done | bytes 61472 | tf_op jit(solution)/shard_map/ppermute | solution.py:44
  38.8 6.7 %shard_map.189 = (bf16[16,32,128]{2,1,0:T(8,128)(2,1)}, bf16[16,32,128]{2,1,0:T(8,128)(2,1)}, bf16[1408,128]{1,0:T(8,128)(2,1)S(1)}, bf16[1408,128]{1,0:T(8,128)(2,1)S(1)}) custom-call(bf16[2,16,32,128]{3,2,1,0:T(8,128)(2,1)S(1)} %pad_maximum_fusion.fields_ref, s32[16,32]{1,0:T(8,128)S(1)} %copy-done, ...), custom_call_target="tpu_custom_call" | custom-call | flops 3000000000 | bytes 8000000 | tf_op jit(solution)/shard_map/pallas_call | solution.py:709
  45.5 3.5 %collective-permute-start.4 = (bf16[1408,128]{1,0:T(8,128)(2,1)S(1)}, bf16[1408,128]{1,0:T(8,128)(2,1)S(1)}, u32[]{:S(2)}, u32[]{:S(2)}) collective-permute-start(bf16[1408,128]{1,0:T(8,128)(2,1)S(1)} %get-tuple-element.37), channel_id=1, source_target_pairs={{0,16},{16,0},{1,17},{17,1},{2,18},{18,2},{3,19},{19,3},{4,20},{20... | collective-permute-start | bytes 1081352 | tf_op jit(solution)/shard_map/ppermute | solution.py:256
  49.0 1.3 %collective-permute-done.4 = bf16[1408,128]{1,0:T(8,128)(2,1)S(1)} collective-permute-done((bf16[1408,128]{1,0:T(8,128)(2,1)S(1)}, bf16[1408,128]{1,0:T(8,128)(2,1)S(1)}, u32[]{:S(2)}, u32[]{:S(2)}) %collective-permute-start.4) | collective-permute-done | bytes 360480 | tf_op jit(solution)/shard_map/ppermute | solution.py:256
  50.2 0.1 add_convert_fusion
  50.3 14.7 %all_to_all.15 = bf16[32,11,4,128]{3,2,1,0:T(4,128)(2,1)S(1)} all-to-all(bf16[32,11,4,128]{3,2,1,0:T(4,128)(2,1)S(1)} %bitcast.13), channel_id=1, replica_groups=mesh['zl'=6,'x'=4,'c'=2,'zh'=2,'y'=8] {'x','y'}, dimensions={0} | all-to-all | bytes 720896 | tf_op jit(solution)/shard_map/all_to_all | solution.py:244
  65.1 0.2 reduce_sum.21
  65.3 15.6 %all_to_all.16 = bf16[12,11,4,128]{3,2,1,0:T(4,128)(2,1)S(1)} all-to-all(bf16[12,11,4,128]{3,2,1,0:T(4,128)(2,1)S(1)} %broadcast_in_dim.20), channel_id=1, replica_groups=mesh['zl'=6,'x'=4,'c'=2,'zh'=2,'y'=8] {'zl','zh'}, dimensions={0} | all-to-all | bytes 270336 | tf_op jit(solution)/shard_map/all_to_all | solution.py:251
  80.9 0.1 convert_reduce_fusion
  80.9 0.1 broadcast_in_dim.21
  81.1 17.2 %all_to_all.17 = bf16[32,11,4,128]{3,2,1,0:T(4,128)(2,1)S(1)} all-to-all(bf16[32,11,4,128]{3,2,1,0:T(4,128)(2,1)S(1)} %broadcast_in_dim.21), channel_id=1, replica_groups=mesh['zl'=6,'x'=4,'c'=2,'zh'=2,'y'=8] {'x','y'}, dimensions={0} | all-to-all | bytes 720896 | tf_op jit(solution)/shard_map/all_to_all | solution.py:251
  98.3 7.2 %collective-permute-start.5 = (bf16[1408,128]{1,0:T(8,128)(2,1)S(1)}, bf16[1408,128]{1,0:T(8,128)(2,1)S(1)}, u32[]{:S(2)}, u32[]{:S(2)}) collective-permute-start(bf16[1408,128]{1,0:T(8,128)(2,1)S(1)} %bitcast.9), channel_id=1, source_target_pairs={{0,16},{16,0},{1,17},{17,1},{2,18},{18,2},{3,19},{19,3},{4,20},{20... | collective-permute-start | bytes 1081352 | tf_op jit(solution)/shard_map/ppermute | solution.py:262
  105.5 1.3 %collective-permute-done.5.other_ref = bf16[1408,128]{1,0:T(8,128)(2,1)S(1)} collective-permute-done((bf16[1408,128]{1,0:T(8,128)(2,1)S(1)}, bf16[1408,128]{1,0:T(8,128)(2,1)S(1)}, u32[]{:S(2)}, u32[]{:S(2)}) %collective-permute-start.5) | collective-permute-done | bytes 360480 | tf_op jit(solution)/shard_map/ppermute | solution.py:262
  106.8 1.1 %shard_map.190 = (f32[128,384]{1,0:T(8,128)}, f32[128,128]{1,0:T(8,128)}, f32[128,512]{1,0:T(8,128)}, f32[512,128]{1,0:T(8,128)}, f32[9,128,128]{2,1,0:T(8,128)}...) custom-call(bf16[1408,128]{1,0:T(8,128)(2,1)S(1)} %bitcast.10, ...), custom_call_target="tpu_custom_call" | custom-call | tf_op jit(solution)/shard_map/pallas_call | solution.py:757
  (16 shorter events, 0.1 us)
Async XLA Ops:
  0.6 1.0 copy-start
  1.7 33.7 %copy-start.8 = (f32[4,15,15]{2,0,1:T(4,128)S(1)}, f32[4,15,15]{2,0,1:T(4,128)}, u32[]{:S(2)}) copy-start(f32[4,15,15]{2,0,1:T(4,128)} %param.21) | copy-start | bytes 10804
  1.7 37.1 %copy-start.4 = (bf16[128,384]{1,0:T(8,128)(2,1)S(1)}, bf16[128,384]{1,0:T(8,128)(2,1)}, u32[]{:S(2)}) copy-start(bf16[128,384]{1,0:T(8,128)(2,1)} %qkv_ref.1) | copy-start | bytes 294916
  1.7 17.9 %collective-permute-start = (bf16[10,32,128]{2,1,0:T(8,128)(2,1)S(1)}, bf16[10,32,128]{2,1,0:T(8,128)(2,1)S(1)}, u32[]{:S(2)}, u32[]{:S(2)}) collective-permute-start(bf16[10,32,128]{2,1,0:T(8,128)(2,1)S(1)} %get-tuple-element.28), channel_id=1, source_target_pairs={{0,752},{16,32},{32,16},{48,64},{64,48},{80,96},{96,80},{112,128},... | collective-permute-start | bytes 245768 | tf_op jit(solution)/shard_map/ppermute | solution.py:44
  6.2 32.5 %copy-start.1 = (bf16[9,128,128]{2,1,0:T(8,128)(2,1)S(1)}, bf16[9,128,128]{2,1,0:T(8,128)(2,1)}, u32[]{:S(2)}) copy-start(bf16[9,128,128]{2,1,0:T(8,128)(2,1)} %conv_ref.1) | copy-start | bytes 884740
  6.3 14.3 %collective-permute-start.1 = (bf16[10,32,128]{2,1,0:T(8,128)(2,1)S(1)}, bf16[10,32,128]{2,1,0:T(8,128)(2,1)S(1)}, u32[]{:S(2)}, u32[]{:S(2)}) collective-permute-start(bf16[10,32,128]{2,1,0:T(8,128)(2,1)S(1)} %get-tuple-element.29), channel_id=1, source_target_pairs={{0,16},{16,0},{32,48},{48,32},{64,80},{80,64},{96,112},{112,96},{1... | collective-permute-start | bytes 245768 | tf_op jit(solution)/shard_map/ppermute | solution.py:44
  20.6 18.2 %copy-start.3 = (bf16[512,128]{1,0:T(8,128)(2,1)S(1)}, bf16[512,128]{1,0:T(8,128)(2,1)}, u32[]{:S(2)}) copy-start(bf16[512,128]{1,0:T(8,128)(2,1)} %down_ref.1) | copy-start | bytes 393220
  20.7 18.1 %copy-start.2 = (bf16[128,512]{1,0:T(8,128)(2,1)S(1)}, bf16[128,512]{1,0:T(8,128)(2,1)}, u32[]{:S(2)}) copy-start(bf16[128,512]{1,0:T(8,128)(2,1)} %up_ref.1) | copy-start | bytes 393220
  20.7 15.9 %collective-permute-start.2 = (bf16[240,128]{1,0:T(8,128)(2,1)S(1)}, bf16[240,128]{1,0:T(8,128)(2,1)S(1)}, u32[]{:S(2)}, u32[]{:S(2)}) collective-permute-start(bf16[240,128]{1,0:T(8,128)(2,1)S(1)} %get-tuple-element.30), channel_id=1, source_target_pairs={{0,15},{1,2},{2,1},{3,4},{4,3},{5,6},{6,5},{7,8},{8,7},{9,10},{10,... | collective-permute-start | bytes 184328 | tf_op jit(solution)/shard_map/ppermute | solution.py:44
  33.5 5.3 %collective-permute-start.3 = (bf16[240,128]{1,0:T(8,128)(2,1)S(1)}, bf16[240,128]{1,0:T(8,128)(2,1)S(1)}, u32[]{:S(2)}, u32[]{:S(2)}) collective-permute-start(bf16[240,128]{1,0:T(8,128)(2,1)S(1)} %get-tuple-element.31), channel_id=1, source_target_pairs={{0,1},{1,0},{2,3},{3,2},{4,5},{5,4},{6,7},{7,6},{8,9},{9,8},{10,11... | collective-permute-start | bytes 184328 | tf_op jit(solution)/shard_map/ppermute | solution.py:44
  35.4 3.3 %copy-start.5 = (bf16[128,128]{1,0:T(8,128)(2,1)S(1)}, bf16[128,128]{1,0:T(8,128)(2,1)}, u32[]{:S(2)}) copy-start(bf16[128,128]{1,0:T(8,128)(2,1)} %proj_ref.1) | copy-start | bytes 98308
  35.5 0.7 copy-start.6
  35.5 0.7 copy-start.7
  45.5 4.8 %collective-permute-start.4 = (bf16[1408,128]{1,0:T(8,128)(2,1)S(1)}, bf16[1408,128]{1,0:T(8,128)(2,1)S(1)}, u32[]{:S(2)}, u32[]{:S(2)}) collective-permute-start(bf16[1408,128]{1,0:T(8,128)(2,1)S(1)} %get-tuple-element.37), channel_id=1, source_target_pairs={{0,16},{16,0},{1,17},{17,1},{2,18},{18,2},{3,19},{19,3},{4,20},{20... | collective-permute-start | bytes 1081352 | tf_op jit(solution)/shard_map/ppermute | solution.py:256
  98.3 8.5 %collective-permute-start.5 = (bf16[1408,128]{1,0:T(8,128)(2,1)S(1)}, bf16[1408,128]{1,0:T(8,128)(2,1)S(1)}, u32[]{:S(2)}, u32[]{:S(2)}) collective-permute-start(bf16[1408,128]{1,0:T(8,128)(2,1)S(1)} %bitcast.9), channel_id=1, source_target_pairs={{0,16},{16,0},{1,17},{17,1},{2,18},{18,2},{3,19},{19,3},{4,20},{20... | collective-permute-start | bytes 1081352 | tf_op jit(solution)/shard_map/ppermute | solution.py:262

commit v7 on v6

--- a/solution.py
+++ b/solution.py
@@ -378,6 +378,31 @@
     return rows
 
 
+def shifted_columns(grid_ref, first_col, lat_total, own_rows, own_cols):
+    col = first_col + lax.broadcasted_iota(jnp.int32, (own_cols, 128), 0)
+    keeps = (col != 0, None, col != lat_total - 1)
+    shifted = []
+    for tap in range(3):
+        piece = grid_ref[3 : own_rows + 5, 3 + tap : 3 + tap + own_cols, :]
+        if keeps[tap] is not None:
+            piece = piece * jnp.where(keeps[tap], 1.0, 0.0)[None]
+        shifted.append(piece.reshape((own_rows + 2) * own_cols, 128).astype(jnp.bfloat16))
+    return jnp.concatenate(shifted, axis=1)
+
+
+def finish_kernel(lat_total, block_out_ref, grad_grid_ref, conv_ref, down_out_ref, grad_tokens_ref):
+    own_rows, own_cols = down_out_ref.shape[0], down_out_ref.shape[1]
+    first_col = place_along(LAT) * own_cols
+    patches = shifted_columns(block_out_ref, first_col, lat_total, own_rows, own_cols)
+    count = own_rows * own_cols
+    downscaled = jnp.zeros((count, 128), jnp.float32)
+    for tap in range(3):
+        rows = patches[tap * own_cols : tap * own_cols + count]
+        downscaled = downscaled + matmul(rows, conv_ref[3 * tap : 3 * tap + 3].reshape(384, 128))
+    down_out_ref[...] = downscaled.astype(jnp.bfloat16).reshape(own_rows, own_cols, 128)
+    grad_tokens_ref[...] = grad_grid_ref[4 : own_rows + 4, 4 : own_cols + 4, :].astype(jnp.bfloat16)
+
+
 def block_kernel(
     lat_total,
     fields_ref,
@@ -393,8 +418,8 @@
     up_ref,
     down_ref,
     conv_ref,
-    down_out_ref,
-    grad_tokens_ref,
+    block_out_s,
+    grad_tokens_s,
     kept_ref,
     sent_ref,
     tokens_s,
@@ -402,8 +427,6 @@
     ids_s,
     gcat_s,
     rows_s,
-    block_out_s,
-    grad_tokens_s,
     ln_one_s,
     ln_two_s,
     hidden_s,
@@ -597,30 +620,20 @@
             grad_qkv_s[kept, :] = grad_qkv[AREA:]
 
 
-    running = [chunk_steps(chunk) for chunk in range(WIN_ROWS)]
+    running = []
+    for chunk in range(WIN_ROWS):
+        running.append(chunk_steps(chunk))
+        for _ in range(2):
+            running = [steps for steps in running if next(steps, running) is not running]
     while running:
         running = [steps for steps in running if next(steps, running) is not running]
 
-    col = first_col + lax.broadcasted_iota(jnp.int32, (own_cols, 128), 0)
-    keeps = (col != 0, None, col != lat_total - 1)
-    shifted = []
-    for tap in range(3):
-        piece = block_out_s[3 : own_rows + 5, 3 + tap : 3 + tap + own_cols, :]
-        if keeps[tap] is not None:
-            piece = piece * jnp.where(keeps[tap], 1.0, 0.0)[None]
-        shifted.append(piece.reshape((own_rows + 2) * own_cols, 128).astype(jnp.bfloat16))
-    patches = jnp.concatenate(shifted, axis=1)
+    patches = shifted_columns(block_out_s, first_col, lat_total, own_rows, own_cols)
     count = own_rows * own_cols
-    downscaled = jnp.zeros((count, 128), jnp.float32)
     grad_own = fields_ref[1].reshape(count, 128)
     for tap in range(3):
         rows = patches[tap * own_cols : tap * own_cols + count]
-        downscaled = downscaled + matmul(rows, conv_ref[3 * tap : 3 * tap + 3].reshape(384, 128))
         rows_s[tap * 384 : (tap + 1) * 384, :] = matmul_tn(rows, grad_own).astype(jnp.bfloat16)
-    down_out_ref[...] = downscaled.astype(jnp.bfloat16).reshape(own_rows, own_cols, 128)
-    grad_tokens_ref[...] = (
-        grad_tokens_s[4 : own_rows + 4, 4 : own_cols + 4, :].astype(jnp.bfloat16)
-    )
     place = 1152
     for left, right, flipped in (
         (ln_one_s, grad_qkv_s, False),
@@ -706,11 +719,11 @@
     lat_far = swapped(far, LAT, False)
     lat_near = swapped(near, LAT, True)
     count = AREA * (WIN_ROWS - 1) * (WIN_COLS - 1)
-    downscaled, grad_tokens, kept, sent = pl.pallas_call(
+    block_out, grad_grid, kept, sent = pl.pallas_call(
         functools.partial(block_kernel, lat_total),
         out_shape=(
-            bf16(*tokens.shape),
-            bf16(*tokens.shape),
+            f32(TOKEN_ROWS, 40, width),
+            f32(TOKEN_ROWS, 40, width),
             bf16(ROWS // 2, width),
             bf16(ROWS // 2, width),
         ),
@@ -722,8 +735,6 @@
             wide(32, width),
             held(GRAD_ROWS * PAD_COLS, 3 * width),
             held(ROWS, width),
-            wide(TOKEN_ROWS, 40, width),
-            wide(TOKEN_ROWS, 40, width),
             held(count, width),
             held(count, width),
             held(count, 4 * width),
@@ -753,6 +764,16 @@
         down_weight,
         conv_weight,
     )
+    downscaled, grad_tokens = pl.pallas_call(
+        functools.partial(finish_kernel, lat_total),
+        out_shape=(bf16(*tokens.shape),) * 2,
+        in_specs=[vmem] * 3,
+        out_specs=(vmem,) * 2,
+        compiler_params=params,
+        cost_estimate=pl.CostEstimate(
+            flops=160_000_000, bytes_accessed=1_600_000, transcendentals=0
+        ),
+    )(block_out, grad_grid, conv_weight)
     own, other = total_over_devices(kept, sent, 1.0 / math.sqrt(tokens_all))
     results = pl.pallas_call(
         unpack_kernel,

time: 109 us -> 108 us (level)
  waiting for transfers between devices: 5.62 us -> 4.49 us
    ppermute x1, waiting for transfers between devices: 1.28 us -> 0.16 us  [total_over_devices(): return (own, lax.ppermute(own, 'c', cores))]
    pallas_call x1 -> x2, Pallas kernels: 6.7 us -> 7.05 us  [the longest x1 5.92 us: per_device(): pl.pallas_call(functools.partial(block_kernel, lat_total), out_shape=(f32...]
  transfers between devices with their start and end apart: 6 -> 6, of which waited for: 4 -> 4; matrix products, arithmetic and copies ran while one was open for 0% -> 0% of each run, Pallas kernels for 0% -> 1%
where the time goes in v7:
time: 108 us; the launch traced here: 107 us
  blocking collectives  47.5 us (44%)
  starting transfers between devices  43.3 us (40%)
  Pallas kernels  8.66 us (8%)
  waiting for transfers between devices  4.49 us (4%)
  other arithmetic  1.34 us (1%)
    all_to_all x2, blocking collectives, spread(): return lax.all_to_all(copies, axes, 0, 0, tiled=True)  32.8 us
    ppermute x4, starting transfers between devices, swapped(): return lax.ppermute(value, axes, pairs)  32.6 us
    all_to_all x1, blocking collectives, scattered_sum(): received = lax.all_to_all(chunks, axes, 0, 0, tiled=True)  14.7 us
    ppermute x1, starting transfers between devices, total_over_devices(): return (own, lax.ppermute(own, 'c', cores))  7.22 us
    pallas_call x1, Pallas kernels, per_device(): pl.pallas_call(functools.partial(block_kernel, lat_total), out_shape=(f32...  5.92 us
    ppermute x1, starting transfers between devices, total_over_devices(): other = lax.ppermute(sent, 'c', cores)  3.48 us
    ppermute x4, waiting for transfers between devices, swapped(): return lax.ppermute(value, axes, pairs)  3.06 us
  transfers between devices with their start and end apart: 6, of which 4 were waited for; matrix products, arithmetic and copies ran while one was open for 0% of the time, Pallas kernels for 1%

profile of v7, /device:TPU:1, one launch (start us, length us, event | category | flops | bytes accessed | tf_op | source)
XLA Modules:
  0.0 107.1 jit_solution(17358330303497541801)
XLA Ops:
  0.7 1.0 pad_maximum_fusion.fields_ref
  1.7 0.0 copy-start.8
  1.7 0.0 copy-start.4
  1.7 4.5 %collective-permute-start = (bf16[10,32,128]{2,1,0:T(8,128)(2,1)S(1)}, bf16[10,32,128]{2,1,0:T(8,128)(2,1)S(1)}, u32[]{:S(2)}, u32[]{:S(2)}) collective-permute-start(bf16[10,32,128]{2,1,0:T(8,128)(2,1)S(1)} %get-tuple-element.30), channel_id=1, source_target_pairs={{0,752},{16,32},{32,16},{48,64},{64,48},{80,96},{96,80},{112,128},... | collective-permute-start | bytes 245768 | tf_op jit(solution)/shard_map/ppermute | solution.py:44
  6.2 0.0 copy-start
  6.3 13.4 %collective-permute-start.1 = (bf16[10,32,128]{2,1,0:T(8,128)(2,1)S(1)}, bf16[10,32,128]{2,1,0:T(8,128)(2,1)S(1)}, u32[]{:S(2)}, u32[]{:S(2)}) collective-permute-start(bf16[10,32,128]{2,1,0:T(8,128)(2,1)S(1)} %get-tuple-element.31), channel_id=1, source_target_pairs={{0,16},{16,0},{32,48},{48,32},{64,80},{80,64},{96,112},{112,96},{1... | collective-permute-start | bytes 245768 | tf_op jit(solution)/shard_map/ppermute | solution.py:44
  19.7 0.0 collective-permute-done.lon_far_ref
  19.7 0.9 collective-permute-done.1.lon_near_ref
  20.6 0.1 shard_map.187
  20.7 12.8 %collective-permute-start.2 = (bf16[240,128]{1,0:T(8,128)(2,1)S(1)}, bf16[240,128]{1,0:T(8,128)(2,1)S(1)}, u32[]{:S(2)}, u32[]{:S(2)}) collective-permute-start(bf16[240,128]{1,0:T(8,128)(2,1)S(1)} %get-tuple-element.32), channel_id=1, source_target_pairs={{0,15},{1,2},{2,1},{3,4},{4,3},{5,6},{6,5},{7,8},{8,7},{9,10},{10,... | collective-permute-start | bytes 184328 | tf_op jit(solution)/shard_map/ppermute | solution.py:44
  33.5 1.9 %collective-permute-start.3 = (bf16[240,128]{1,0:T(8,128)(2,1)S(1)}, bf16[240,128]{1,0:T(8,128)(2,1)S(1)}, u32[]{:S(2)}, u32[]{:S(2)}) collective-permute-start(bf16[240,128]{1,0:T(8,128)(2,1)S(1)} %get-tuple-element.33), channel_id=1, source_target_pairs={{0,1},{1,0},{2,3},{3,2},{4,5},{5,4},{6,7},{7,6},{8,9},{9,8},{10,11... | collective-permute-start | bytes 184328 | tf_op jit(solution)/shard_map/ppermute | solution.py:44
  35.4 0.0 copy-start.5
  35.5 0.1 reshape.34.table_ref
  35.6 0.6 copy-done.6
  36.2 0.0 copy-done.7
  36.2 0.3 shard_map.188
  36.6 0.0 collective-permute-done.2.lat_far_ref
  36.6 2.2 %collective-permute-done.3.lat_near_ref = bf16[240,128]{1,0:T(8,128)(2,1)S(1)} collective-permute-done((bf16[240,128]{1,0:T(8,128)(2,1)S(1)}, bf16[240,128]{1,0:T(8,128)(2,1)S(1)}, u32[]{:S(2)}, u32[]{:S(2)}) %collective-permute-start.3) | collective-permute-done | bytes 61472 | tf_op jit(solution)/shard_map/ppermute | solution.py:44
  38.8 5.9 %shard_map.189 = (f32[24,40,128]{2,1,0:T(8,128)S(1)}, f32[24,40,128]{2,1,0:T(8,128)S(1)}, bf16[1408,128]{1,0:T(8,128)(2,1)S(1)}, bf16[1408,128]{1,0:T(8,128)(2,1)S(1)}) custom-call(bf16[2,16,32,128]{3,2,1,0:T(8,128)(2,1)S(1)} %pad_maximum_fusion.fields_ref, s32[16,32]{1,0:T(8,128)S(1)} %copy-done.1, ...), custom_call_target="tpu_custom_call" | custom-call | flops 3000000000 | bytes 8000000 | tf_op jit(solution)/shard_map/pallas_call | solution.py:722
  44.7 3.5 %collective-permute-start.4 = (bf16[1408,128]{1,0:T(8,128)(2,1)S(1)}, bf16[1408,128]{1,0:T(8,128)(2,1)S(1)}, u32[]{:S(2)}, u32[]{:S(2)}) collective-permute-start(bf16[1408,128]{1,0:T(8,128)(2,1)S(1)} %get-tuple-element.41), channel_id=1, source_target_pairs={{0,16},{16,0},{1,17},{17,1},{2,18},{18,2},{3,19},{19,3},{4,20},{20... | collective-permute-start | bytes 1081352 | tf_op jit(solution)/shard_map/ppermute | solution.py:256
  48.2 1.3 %collective-permute-done.4 = bf16[1408,128]{1,0:T(8,128)(2,1)S(1)} collective-permute-done((bf16[1408,128]{1,0:T(8,128)(2,1)S(1)}, bf16[1408,128]{1,0:T(8,128)(2,1)S(1)}, u32[]{:S(2)}, u32[]{:S(2)}) %collective-permute-start.4) | collective-permute-done | bytes 360480 | tf_op jit(solution)/shard_map/ppermute | solution.py:256
  49.5 0.1 add_convert_fusion
  49.6 14.7 %all_to_all.15 = bf16[32,11,4,128]{3,2,1,0:T(4,128)(2,1)S(1)} all-to-all(bf16[32,11,4,128]{3,2,1,0:T(4,128)(2,1)S(1)} %bitcast.13), channel_id=1, replica_groups=mesh['zl'=6,'x'=4,'c'=2,'zh'=2,'y'=8] {'x','y'}, dimensions={0} | all-to-all | bytes 720896 | tf_op jit(solution)/shard_map/all_to_all | solution.py:244
  64.3 0.2 reduce_sum.21
  64.5 15.6 %all_to_all.16 = bf16[12,11,4,128]{3,2,1,0:T(4,128)(2,1)S(1)} all-to-all(bf16[12,11,4,128]{3,2,1,0:T(4,128)(2,1)S(1)} %broadcast_in_dim.20), channel_id=1, replica_groups=mesh['zl'=6,'x'=4,'c'=2,'zh'=2,'y'=8] {'zl','zh'}, dimensions={0} | all-to-all | bytes 270336 | tf_op jit(solution)/shard_map/all_to_all | solution.py:251
  80.1 0.1 convert_reduce_fusion
  80.2 0.1 broadcast_in_dim.21
  80.3 17.2 %all_to_all.17 = bf16[32,11,4,128]{3,2,1,0:T(4,128)(2,1)S(1)} all-to-all(bf16[32,11,4,128]{3,2,1,0:T(4,128)(2,1)S(1)} %broadcast_in_dim.21), channel_id=1, replica_groups=mesh['zl'=6,'x'=4,'c'=2,'zh'=2,'y'=8] {'x','y'}, dimensions={0} | all-to-all | bytes 720896 | tf_op jit(solution)/shard_map/all_to_all | solution.py:251
  97.5 7.2 %collective-permute-start.5 = (bf16[1408,128]{1,0:T(8,128)(2,1)S(1)}, bf16[1408,128]{1,0:T(8,128)(2,1)S(1)}, u32[]{:S(2)}, u32[]{:S(2)}) collective-permute-start(bf16[1408,128]{1,0:T(8,128)(2,1)S(1)} %bitcast.9), channel_id=1, source_target_pairs={{0,16},{16,0},{1,17},{17,1},{2,18},{18,2},{3,19},{19,3},{4,20},{20... | collective-permute-start | bytes 1081352 | tf_op jit(solution)/shard_map/ppermute | solution.py:262
  104.7 1.1 %shard_map.190 = (bf16[16,32,128]{2,1,0:T(8,128)(2,1)}, bf16[16,32,128]{2,1,0:T(8,128)(2,1)}) custom-call(f32[24,40,128]{2,1,0:T(8,128)S(1)} %get-tuple-element.36.block_out_ref, f32[24,40,128]{2,1,0:T(8,128)S(1)} %get-tuple-element.37.grad_grid_ref, bf16[9,128,128]{2,1,0:T(8,128)(2,1)S(1)} %copy-done), custom_call_target="tpu_custom_call" | custom-call | flops 160000000 | bytes 1600000 | tf_op jit(solution)/shard_map/pallas_call | solution.py:767
  105.8 0.2 collective-permute-done.5.other_ref
  106.0 1.1 %shard_map.191 = (f32[128,384]{1,0:T(8,128)}, f32[128,128]{1,0:T(8,128)}, f32[128,512]{1,0:T(8,128)}, f32[512,128]{1,0:T(8,128)}, f32[9,128,128]{2,1,0:T(8,128)}...) custom-call(bf16[1408,128]{1,0:T(8,128)(2,1)S(1)} %bitcast.10, ...), custom_call_target="tpu_custom_call" | custom-call | tf_op jit(solution)/shard_map/pallas_call | solution.py:778
  (17 shorter events, 0.1 us)
Async XLA Ops:
  0.6 1.0 copy-start.1
  1.7 33.7 %copy-start.8 = (f32[4,15,15]{2,0,1:T(4,128)S(1)}, f32[4,15,15]{2,0,1:T(4,128)}, u32[]{:S(2)}) copy-start(f32[4,15,15]{2,0,1:T(4,128)} %param.21) | copy-start | bytes 10804
  1.7 37.1 %copy-start.4 = (bf16[128,384]{1,0:T(8,128)(2,1)S(1)}, bf16[128,384]{1,0:T(8,128)(2,1)}, u32[]{:S(2)}) copy-start(bf16[128,384]{1,0:T(8,128)(2,1)} %qkv_ref.1) | copy-start | bytes 294916
  1.7 17.9 %collective-permute-start = (bf16[10,32,128]{2,1,0:T(8,128)(2,1)S(1)}, bf16[10,32,128]{2,1,0:T(8,128)(2,1)S(1)}, u32[]{:S(2)}, u32[]{:S(2)}) collective-permute-start(bf16[10,32,128]{2,1,0:T(8,128)(2,1)S(1)} %get-tuple-element.30), channel_id=1, source_target_pairs={{0,752},{16,32},{32,16},{48,64},{64,48},{80,96},{96,80},{112,128},... | collective-permute-start | bytes 245768 | tf_op jit(solution)/shard_map/ppermute | solution.py:44
  6.2 32.5 %copy-start = (bf16[9,128,128]{2,1,0:T(8,128)(2,1)S(1)}, bf16[9,128,128]{2,1,0:T(8,128)(2,1)}, u32[]{:S(2)}) copy-start(bf16[9,128,128]{2,1,0:T(8,128)(2,1)} %conv_ref.3) | copy-start | bytes 884740
  6.3 14.3 %collective-permute-start.1 = (bf16[10,32,128]{2,1,0:T(8,128)(2,1)S(1)}, bf16[10,32,128]{2,1,0:T(8,128)(2,1)S(1)}, u32[]{:S(2)}, u32[]{:S(2)}) collective-permute-start(bf16[10,32,128]{2,1,0:T(8,128)(2,1)S(1)} %get-tuple-element.31), channel_id=1, source_target_pairs={{0,16},{16,0},{32,48},{48,32},{64,80},{80,64},{96,112},{112,96},{1... | collective-permute-start | bytes 245768 | tf_op jit(solution)/shard_map/ppermute | solution.py:44
  20.6 18.2 %copy-start.3 = (bf16[512,128]{1,0:T(8,128)(2,1)S(1)}, bf16[512,128]{1,0:T(8,128)(2,1)}, u32[]{:S(2)}) copy-start(bf16[512,128]{1,0:T(8,128)(2,1)} %down_ref.1) | copy-start | bytes 393220
  20.7 18.1 %copy-start.2 = (bf16[128,512]{1,0:T(8,128)(2,1)S(1)}, bf16[128,512]{1,0:T(8,128)(2,1)}, u32[]{:S(2)}) copy-start(bf16[128,512]{1,0:T(8,128)(2,1)} %up_ref.1) | copy-start | bytes 393220
  20.7 15.9 %collective-permute-start.2 = (bf16[240,128]{1,0:T(8,128)(2,1)S(1)}, bf16[240,128]{1,0:T(8,128)(2,1)S(1)}, u32[]{:S(2)}, u32[]{:S(2)}) collective-permute-start(bf16[240,128]{1,0:T(8,128)(2,1)S(1)} %get-tuple-element.32), channel_id=1, source_target_pairs={{0,15},{1,2},{2,1},{3,4},{4,3},{5,6},{6,5},{7,8},{8,7},{9,10},{10,... | collective-permute-start | bytes 184328 | tf_op jit(solution)/shard_map/ppermute | solution.py:44
  33.5 5.3 %collective-permute-start.3 = (bf16[240,128]{1,0:T(8,128)(2,1)S(1)}, bf16[240,128]{1,0:T(8,128)(2,1)S(1)}, u32[]{:S(2)}, u32[]{:S(2)}) collective-permute-start(bf16[240,128]{1,0:T(8,128)(2,1)S(1)} %get-tuple-element.33), channel_id=1, source_target_pairs={{0,1},{1,0},{2,3},{3,2},{4,5},{5,4},{6,7},{7,6},{8,9},{9,8},{10,11... | collective-permute-start | bytes 184328 | tf_op jit(solution)/shard_map/ppermute | solution.py:44
  35.4 3.3 %copy-start.5 = (bf16[128,128]{1,0:T(8,128)(2,1)S(1)}, bf16[128,128]{1,0:T(8,128)(2,1)}, u32[]{:S(2)}) copy-start(bf16[128,128]{1,0:T(8,128)(2,1)} %proj_ref.1) | copy-start | bytes 98308
  35.5 0.7 copy-start.6
  35.5 0.7 copy-start.7
  44.7 4.8 %collective-permute-start.4 = (bf16[1408,128]{1,0:T(8,128)(2,1)S(1)}, bf16[1408,128]{1,0:T(8,128)(2,1)S(1)}, u32[]{:S(2)}, u32[]{:S(2)}) collective-permute-start(bf16[1408,128]{1,0:T(8,128)(2,1)S(1)} %get-tuple-element.41), channel_id=1, source_target_pairs={{0,16},{16,0},{1,17},{17,1},{2,18},{18,2},{3,19},{19,3},{4,20},{20... | collective-permute-start | bytes 1081352 | tf_op jit(solution)/shard_map/ppermute | solution.py:256
  97.5 8.5 %collective-permute-start.5 = (bf16[1408,128]{1,0:T(8,128)(2,1)S(1)}, bf16[1408,128]{1,0:T(8,128)(2,1)S(1)}, u32[]{:S(2)}, u32[]{:S(2)}) collective-permute-start(bf16[1408,128]{1,0:T(8,128)(2,1)S(1)} %bitcast.9), channel_id=1, source_target_pairs={{0,16},{16,0},{1,17},{17,1},{2,18},{18,2},{3,19},{19,3},{4,20},{20... | collective-permute-start | bytes 1081352 | tf_op jit(solution)/shard_map/ppermute | solution.py:262
